TPU v7x, 32 devices: a whole 2x2x4 slice. The times are simulated.
32 devices in a mesh: section: 2 (over core), dp: 4 (over y, x), tensor: 4 (over z).
Axes of the slice: x: 2, y: 2, z: 4, core: 2. Of those that a mesh axis runs over, the one named last changes fastest.
Arguments:
- tokens: bfloat16 [16, 1024, 512], P('dp', 'tensor'), may hold values from -6 to 6
- lengths: int32 [16, 8], P('dp'), may hold values from 1 to 896, 1024 in all within a row
- cotangent: bfloat16 [16, 1024, 512], P('dp', 'tensor'), may hold values from -6 to 6
- ln_one_gain: float32 [2, 512], P('section'), may hold values from 0.5 to 1.5
- ln_one_bias: float32 [2, 512], P('section'), may hold values from -1.75 to 1.75
- qkv_weight: bfloat16 [2, 512, 3, 512], P('section', None, None, 'tensor'), may hold values from -0.25 to 0.25
- out_weight: bfloat16 [2, 512, 512], P('section', 'tensor'), may hold values from -1.5 to 1.5
- out_bias: float32 [2, 512], P('section'), may hold values from -3 to 3
- ln_two_gain: float32 [2, 512], P('section'), may hold values from 0.5 to 1.5
- ln_two_bias: float32 [2, 512], P('section'), may hold values from -1.75 to 1.75
- up_weight: bfloat16 [2, 512, 2048], P('section', None, 'tensor'), may hold values from -0.25 to 0.25
- up_bias: float32 [2, 2048], P('section', 'tensor'), may hold values from -3 to 3
- down_weight: bfloat16 [2, 2048, 512], P('section', 'tensor'), may hold values from -0.125 to 0.125
- down_bias: float32 [2, 512], P('section'), may hold values from -3 to 3
Outputs:
- block_outputs: bfloat16 [2, 16, 1024, 512], P('section', 'dp', 'tensor')
- input_grads: float32 [2, 16, 1024, 512], P('section', 'dp', 'tensor')
- grad_ln_one_gain: float32 [2, 512], P('section', ('dp', 'tensor'))
- grad_ln_one_bias: float32 [2, 512], P('section', ('dp', 'tensor'))
- grad_qkv_weight: float32 [2, 512, 3, 512], P('section', 'dp', None, 'tensor')
- grad_out_weight: float32 [2, 512, 512], P('section', 'tensor', 'dp')
- grad_out_bias: float32 [2, 512], P('section', ('dp', 'tensor'))
- grad_ln_two_gain: float32 [2, 512], P('section', ('dp', 'tensor'))
- grad_ln_two_bias: float32 [2, 512], P('section', ('dp', 'tensor'))
- grad_up_weight: float32 [2, 512, 2048], P('section', 'dp', 'tensor')
- grad_up_bias: float32 [2, 4, 512], P('section', 'tensor', 'dp')
- grad_down_weight: float32 [2, 2048, 512], P('section', 'tensor', 'dp')
- grad_down_bias: float32 [2, 512], P('section', ('dp', 'tensor'))
Inputs may be any that keep to these rules, and one draw needn't show every extreme that they name: Each row holds 8 lengths that fill 1024 rows exactly; the largest of each row is 896.
All inputs are finite; a program needn't handle non-finite values.
Results may differ from a plain program's by a relative error of at most 0.025.
Values may be sent and summed in bfloat16 or wider, within the bound.
A program may use at most 192 MiB of HBM per device.

v0:
```python
from functools import partial
import math

import jax
import jax.numpy as jnp
from jax import lax
from jax.sharding import PartitionSpec as P

HEAD = 64
FF = 2048


def passed_along(block, axis, distance):
    devices = range(lax.axis_size(axis))
    route = [(i - distance, i) for i in devices if i - distance in devices]
    return lax.ppermute(block, axis, route)


def normalize(values, gain_vec, bias_vec):
    centre = values - jnp.mean(values, axis=-1, keepdims=True)
    spread = jnp.mean(centre * centre, axis=-1, keepdims=True)
    return centre * lax.rsqrt(spread + 1e-05) * gain_vec + bias_vec


def document_ids(seq_lens, row_count):
    bounds = jnp.cumsum(seq_lens)
    places = jnp.arange(row_count, dtype=jnp.int32)
    return jnp.sum((places[:, None] >= bounds[None, :]).astype(jnp.int32), axis=1)


def first_key_block(doc_number, seq_lens, block):
    starts = jnp.cumsum(seq_lens) - seq_lens
    numbers = jnp.arange(seq_lens.shape[0], dtype=jnp.int32)
    return jnp.sum(jnp.where(numbers == doc_number, starts, 0)) // block


def grouped_sum(left, right, groups):
    row_count, inner = left.shape
    terms = jnp.einsum(
        "rgc,gcd->grd",
        left.reshape(row_count, groups, inner // groups),
        right.reshape(groups, inner // groups, right.shape[-1]),
        preferred_element_type=jnp.float32,
    )
    return jnp.sum(lax.optimization_barrier(terms.astype(jnp.bfloat16)).astype(jnp.float32), axis=0)


def branch_total(left, right):
    return grouped_sum(left, right, lax.axis_size("tensor"))


def key_scores(query_rows, key_part, query_docs, key_docs, query_first, key_first, signed):
    scale = 1.0 / math.sqrt(query_rows.shape[-1])
    scores = (
        jnp.einsum("qhe,khe->hqk", query_rows, key_part, preferred_element_type=jnp.float32) * scale
    )
    query_places = query_first + jnp.arange(query_rows.shape[0], dtype=jnp.int32)
    key_places = key_first + jnp.arange(key_part.shape[0], dtype=jnp.int32)
    allowed = (query_docs[:, None] == key_docs[None, :]) & (
        query_places[:, None] >= key_places[None, :]
    )
    modulus = jnp.sqrt(scores * scores + 1.0)
    logits = jnp.where(signed, modulus, scores)
    factor = jnp.where(signed, scores / modulus, 1.0)
    return (modulus, logits, factor, allowed[None])


def attend(queries, key_rows, values, doc_rows, seq_lens, signed, offset):
    query_count, heads_here, head_size = queries.shape
    key_count = key_rows.shape[0]
    query_block = min(512, query_count)
    key_block = min(512, key_count)
    query_first = offset + 0
    query_docs = lax.dynamic_slice_in_dim(doc_rows, query_first, query_block, 0)
    lowest = first_key_block(query_docs[0], seq_lens, key_block)
    upper = (query_first + query_block - 1) // key_block + 1

    def block_scores(key_index):
        key_first = key_index * key_block
        return key_scores(
            queries,
            lax.dynamic_slice_in_dim(key_rows, key_first, key_block, 0),
            query_docs,
            lax.dynamic_slice_in_dim(doc_rows, key_first, key_block, 0),
            query_first,
            key_first,
            signed,
        )

    def measure(key_index, carry):
        running_max, running_sum = carry
        modulus, logits, factor, allowed = block_scores(key_index)
        masked = jnp.where(allowed, logits, -1e30)
        new_max = jnp.maximum(running_max, jnp.max(masked, axis=-1))
        added = jnp.sum(jnp.where(allowed, jnp.exp(masked - new_max[:, :, None]), 0.0), axis=-1)
        return (new_max, running_sum * jnp.exp(running_max - new_max) + added)

    start_max = jnp.full((heads_here, query_block), -1e30, jnp.float32)
    start_sum = jnp.zeros((heads_here, query_block), jnp.float32)
    row_max, row_sum = lax.fori_loop(lowest, upper, measure, (start_max, start_sum))
    log_total = row_max + jnp.log(row_sum)

    def accumulate(key_index, partial_out):
        modulus, logits, factor, allowed = block_scores(key_index)
        probs = jnp.where(allowed, jnp.exp(logits - log_total[:, :, None]), 0.0)
        weights = (factor * probs).astype(jnp.bfloat16)
        value_rows = lax.dynamic_slice_in_dim(values, key_index * key_block, key_block, 0)
        return partial_out + jnp.einsum(
            "hqk,khe->qhe", weights, value_rows, preferred_element_type=jnp.float32
        )

    outputs_list = lax.fori_loop(
        lowest, upper, accumulate, jnp.zeros((query_block, heads_here, head_size), jnp.float32)
    )
    return (outputs_list, log_total)


def attend_back(
    queries,
    key_rows,
    values,
    doc_rows,
    seq_lens,
    signed,
    attended,
    log_totals,
    grad_attended,
    offset,
):
    query_count, heads_here, head_size = queries.shape
    key_count = key_rows.shape[0]
    query_block = min(512, query_count)
    key_block = min(512, key_count)
    scale = 1.0 / math.sqrt(head_size)
    centre_terms = jnp.sum(grad_attended.astype(jnp.float32) * attended, axis=-1).T
    grad_keys = jnp.zeros(key_rows.shape, jnp.float32)
    grad_values = jnp.zeros(key_rows.shape, jnp.float32)
    query_first = offset + 0
    query_docs = lax.dynamic_slice_in_dim(doc_rows, query_first, query_block, 0)
    lowest = first_key_block(query_docs[0], seq_lens, key_block)
    upper = (query_first + query_block - 1) // key_block + 1

    def backward_step(key_index, carry):
        grad_query, keys_total, values_total = carry
        key_first = key_index * key_block
        key_part = lax.dynamic_slice_in_dim(key_rows, key_first, key_block, 0)
        value_rows = lax.dynamic_slice_in_dim(values, key_first, key_block, 0)
        modulus, logits, factor, allowed = key_scores(
            queries,
            key_part,
            query_docs,
            lax.dynamic_slice_in_dim(doc_rows, key_first, key_block, 0),
            query_first,
            key_first,
            signed,
        )
        probs = jnp.where(allowed, jnp.exp(logits - log_totals[:, :, None]), 0.0)
        weights = (factor * probs).astype(jnp.bfloat16)
        grad_weights = jnp.einsum(
            "qhe,khe->hqk", grad_attended, value_rows, preferred_element_type=jnp.float32
        )
        grad_scores = factor * probs * (factor * grad_weights - centre_terms[:, :, None])
        grad_scores = grad_scores + jnp.where(
            signed, probs * grad_weights / (modulus * modulus * modulus), 0.0
        )
        grad_low = grad_scores.astype(jnp.bfloat16)
        grad_query = (
            grad_query
            + jnp.einsum("hqk,khe->qhe", grad_low, key_part, preferred_element_type=jnp.float32)
            * scale
        )
        key_term = (
            jnp.einsum("hqk,qhe->khe", grad_low, queries, preferred_element_type=jnp.float32)
            * scale
        )
        value_term = jnp.einsum(
            "hqk,qhe->khe", weights, grad_attended, preferred_element_type=jnp.float32
        )
        keys_total = lax.dynamic_update_slice_in_dim(
            keys_total,
            lax.dynamic_slice_in_dim(keys_total, key_first, key_block, 0) + key_term,
            key_first,
            0,
        )
        values_total = lax.dynamic_update_slice_in_dim(
            values_total,
            lax.dynamic_slice_in_dim(values_total, key_first, key_block, 0) + value_term,
            key_first,
            0,
        )
        return (grad_query, keys_total, values_total)

    start_query = jnp.zeros((query_block, heads_here, head_size), jnp.float32)
    grad_query, grad_keys, grad_values = lax.fori_loop(
        lowest, upper, backward_step, (start_query, grad_keys, grad_values)
    )
    return (grad_query, grad_keys, grad_values)


def forward_layer(inputs, seq_lens, params, signed, finish):
    (
        gain_one,
        bias_one,
        qkv_weight,
        out_weight,
        out_bias,
        gain_two,
        bias_two,
        up_weight,
        up_bias,
        down_weight,
        down_bias,
    ) = params
    normed_one = normalize(inputs, gain_one, bias_one).astype(jnp.bfloat16)
    offset = lax.axis_index("tensor") * normed_one.shape[0]
    row_count = normed_one.shape[0]
    width = qkv_weight.shape[-1]
    projected = jnp.dot(
        normed_one,
        qkv_weight.reshape(qkv_weight.shape[0], 3 * width),
        preferred_element_type=jnp.float32,
    ).astype(jnp.bfloat16)
    head_shape = (row_count, width // HEAD, HEAD)
    queries = projected[:, :width].reshape(head_shape)
    key_rows = projected[:, width : 2 * width].reshape(head_shape)
    values = projected[:, 2 * width :].reshape(head_shape)
    key_all, value_all = (
        lax.all_gather(key_rows, "tensor", axis=0, tiled=True),
        lax.all_gather(values, "tensor", axis=0, tiled=True),
    )
    doc_rows = document_ids(seq_lens, key_all.shape[0])
    attended, log_totals = attend(queries, key_all, value_all, doc_rows, seq_lens, signed, offset)
    attended_low = attended.reshape(row_count, width).astype(jnp.bfloat16)
    hidden_one = inputs + branch_total(attended_low, out_weight) + out_bias
    normed_two = normalize(hidden_one, gain_two, bias_two).astype(jnp.bfloat16)
    up_values = jnp.dot(normed_two, up_weight, preferred_element_type=jnp.float32) + up_bias
    activated = jax.nn.gelu(up_values, approximate=False).astype(jnp.bfloat16)
    if finish:
        outputs = hidden_one + branch_total(activated, down_weight) + down_bias
    else:
        outputs = hidden_one
    saved = (
        normed_one,
        queries,
        key_all,
        value_all,
        doc_rows,
        attended,
        attended_low,
        log_totals,
        hidden_one,
        normed_two,
        up_values,
        activated,
        offset,
    )
    return (outputs, saved)


def backward_layer(inputs, seq_lens, params, signed, grad_outputs):
    (
        gain_one,
        bias_one,
        qkv_weight,
        out_weight,
        out_bias,
        gain_two,
        bias_two,
        up_weight,
        up_bias,
        down_weight,
        down_bias,
    ) = params
    unused_out, saved = forward_layer(inputs, seq_lens, params, signed, False)
    (
        rows_one,
        queries,
        key_all,
        value_all,
        doc_rows,
        attended,
        attended_low,
        log_totals,
        hidden_one,
        rows_two,
        up_values,
        activated,
        offset,
    ) = saved
    row_count, width = attended_low.shape
    grad_low = grad_outputs.astype(jnp.bfloat16)
    grad_down = jnp.einsum("rf,rd->fd", activated, grad_low, preferred_element_type=jnp.float32)
    grad_act = jnp.einsum("rd,fd->rf", grad_low, down_weight, preferred_element_type=jnp.float32)
    gelu_value, gelu_back = jax.vjp(partial(jax.nn.gelu, approximate=False), up_values)
    grad_up_values = gelu_back(grad_act)[0].astype(jnp.bfloat16)
    grad_up_bias = jnp.sum(grad_up_values.astype(jnp.float32), axis=0)
    grad_up = jnp.einsum("rd,rf->df", rows_two, grad_up_values, preferred_element_type=jnp.float32)
    normed_two_terms = jnp.einsum(
        "rf,df->rd", grad_up_values, up_weight, preferred_element_type=jnp.float32
    )
    norm_value, norm_back = jax.vjp(normalize, hidden_one, gain_two, bias_two)
    grad_hidden, grad_gain_two, grad_bias_two = norm_back(normed_two_terms)
    grad_hidden = grad_hidden + grad_outputs
    hidden_low = grad_hidden.astype(jnp.bfloat16)
    grad_out = jnp.einsum("rc,rd->cd", attended_low, hidden_low, preferred_element_type=jnp.float32)
    grad_attended = (
        jnp.einsum("rd,cd->rc", hidden_low, out_weight, preferred_element_type=jnp.float32)
        .astype(jnp.bfloat16)
        .reshape(queries.shape)
    )
    grad_queries, grad_keys, grad_values = attend_back(
        queries,
        key_all,
        value_all,
        doc_rows,
        seq_lens,
        signed,
        attended,
        log_totals,
        grad_attended,
        offset,
    )
    grad_keys, grad_values = (
        lax.psum_scatter(
            grad_keys.astype(jnp.bfloat16), "tensor", scatter_dimension=0, tiled=True
        ).astype(jnp.float32),
        lax.psum_scatter(
            grad_values.astype(jnp.bfloat16), "tensor", scatter_dimension=0, tiled=True
        ).astype(jnp.float32),
    )
    grad_projected = jnp.concatenate(
        [
            grad_queries.reshape(row_count, width),
            grad_keys.reshape(row_count, width),
            grad_values.reshape(row_count, width),
        ],
        axis=1,
    ).astype(jnp.bfloat16)
    grad_qkv = jnp.einsum(
        "rd,rc->dc", rows_one, grad_projected, preferred_element_type=jnp.float32
    ).reshape(qkv_weight.shape)
    normed_one_terms = jnp.einsum(
        "rc,dc->rd",
        grad_projected,
        qkv_weight.reshape(qkv_weight.shape[0], 3 * width),
        preferred_element_type=jnp.float32,
    )
    norm_value_one, norm_back_one = jax.vjp(normalize, inputs, gain_one, bias_one)
    grad_inputs, grad_gain_one, grad_bias_one = norm_back_one(normed_one_terms)
    grad_inputs = grad_inputs + grad_hidden
    matrices = (
        grad_qkv[None],
        grad_out[None],
        grad_up[None],
        grad_up_bias.reshape(1, -1, FF // lax.axis_size("tensor")),
        grad_down[None],
    )
    vectors = (
        grad_gain_one[None],
        grad_bias_one[None],
        jnp.sum(grad_hidden, axis=0)[None],
        grad_gain_two[None],
        grad_bias_two[None],
        jnp.sum(grad_outputs, axis=0)[None],
    )
    return (grad_inputs, matrices, vectors)


def on_device(
    tokens,
    lengths,
    cotangent,
    ln_one_gain,
    ln_one_bias,
    qkv_weight,
    out_weight,
    out_bias,
    ln_two_gain,
    ln_two_bias,
    up_weight,
    up_bias,
    down_weight,
    down_bias,
):
    signed = lax.axis_index("section") == 0
    params = tuple(
        (
            array_item[0]
            for array_item in (
                ln_one_gain,
                ln_one_bias,
                qkv_weight,
                out_weight,
                out_bias,
                ln_two_gain,
                ln_two_bias,
                up_weight,
                up_bias,
                down_weight,
                down_bias,
            )
        )
    )
    whole = (
        lax.all_gather(qkv_weight, "tensor", axis=3, tiled=True),
        lax.all_gather(out_weight, "tensor", axis=1, tiled=True),
        lax.all_gather(up_weight, "tensor", axis=2, tiled=True),
        lax.all_gather(down_weight, "tensor", axis=1, tiled=True),
    )
    bias_whole = lax.all_gather(up_bias, "tensor", axis=1, tiled=True)
    params = (
        params[0],
        params[1],
        whole[0][0],
        whole[1][0],
        params[4],
        params[5],
        params[6],
        whole[2][0],
        bias_whole[0],
        whole[3][0],
        params[10],
    )
    batches = tokens.shape[0]
    arrived = jnp.zeros(tokens.shape[1:], jnp.bfloat16)
    produced_all = jnp.zeros(tokens.shape, jnp.bfloat16)
    received_all = jnp.zeros(tokens.shape, jnp.bfloat16)
    for tick in range(batches + 1):
        own_index = min(tick, batches - 1)
        prior_index = max(tick - 1, 0)
        inputs_now = jnp.where(signed, tokens[own_index], arrived).astype(jnp.float32)
        lens_now = jnp.where(signed, lengths[own_index], lengths[prior_index])
        produced = forward_layer(inputs_now, lens_now, params, signed, True)[0].astype(jnp.bfloat16)
        if tick < batches:
            produced_all = produced_all.at[tick].set(
                jnp.where(signed, produced, produced_all[tick])
            )
        if tick > 0:
            produced_all = produced_all.at[tick - 1].set(
                jnp.where(signed, produced_all[tick - 1], produced)
            )
            received_all = received_all.at[tick - 1].set(arrived)
        if tick < batches:
            arrived = passed_along(produced, "section", 1)
    block_inputs = jnp.where(signed, tokens, received_all)
    returned = jnp.zeros(tokens.shape[1:], jnp.float32)
    grad_inputs_all = jnp.zeros(tokens.shape, jnp.float32)
    matrix_total = None
    vector_total = None
    for tick in range(batches + 1):
        later_index = batches - 1 - tick if tick < batches else 0
        earlier_index = batches - tick if tick > 0 else 0
        index_now = jnp.where(signed, earlier_index, later_index)
        live_now = jnp.where(signed, tick > 0, tick < batches)
        grad_now = jnp.where(signed, returned, cotangent[later_index].astype(jnp.float32))
        grad_now = jnp.where(live_now, grad_now, 0.0)
        inputs_now = block_inputs[index_now].astype(jnp.float32)
        grad_back, matrices, vectors = backward_layer(
            inputs_now, lengths[index_now], params, signed, grad_now
        )
        if tick == 0:
            matrix_total = tuple(matrices)
            vector_total = tuple(vectors)
        else:
            matrix_total = tuple(
                (
                    jnp.add(total_item, new_item)
                    for total_item, new_item in zip(matrix_total, matrices)
                )
            )
            vector_total = tuple(
                (
                    jnp.add(total_item, new_item)
                    for total_item, new_item in zip(vector_total, vectors)
                )
            )
        if tick > 0:
            grad_inputs_all = grad_inputs_all.at[earlier_index].set(
                jnp.where(signed, grad_back, grad_inputs_all[earlier_index])
            )
        if tick < batches:
            grad_inputs_all = grad_inputs_all.at[later_index].set(
                jnp.where(signed, grad_inputs_all[later_index], grad_back)
            )
            returned = passed_along(grad_back.astype(jnp.bfloat16), "section", -1).astype(
                grad_back.dtype
            )
    matrix_final = (
        lax.psum_scatter(
            matrix_total[0].astype(jnp.bfloat16), "dp", scatter_dimension=1, tiled=True
        ).astype(jnp.float32),
        lax.psum_scatter(
            matrix_total[1].astype(jnp.bfloat16), "dp", scatter_dimension=2, tiled=True
        ).astype(jnp.float32),
        lax.psum_scatter(
            matrix_total[2].astype(jnp.bfloat16), "dp", scatter_dimension=1, tiled=True
        ).astype(jnp.float32),
        lax.psum_scatter(
            matrix_total[3].astype(jnp.bfloat16), "dp", scatter_dimension=2, tiled=True
        ).astype(jnp.float32),
        lax.psum_scatter(
            matrix_total[4].astype(jnp.bfloat16), "dp", scatter_dimension=2, tiled=True
        ).astype(jnp.float32),
    )
    vector_final = (
        lax.psum_scatter(vector_total[0], ("dp", "tensor"), scatter_dimension=1, tiled=True),
        lax.psum_scatter(vector_total[1], ("dp", "tensor"), scatter_dimension=1, tiled=True),
        lax.psum_scatter(vector_total[2], ("dp", "tensor"), scatter_dimension=1, tiled=True),
        lax.psum_scatter(vector_total[3], ("dp", "tensor"), scatter_dimension=1, tiled=True),
        lax.psum_scatter(vector_total[4], ("dp", "tensor"), scatter_dimension=1, tiled=True),
        lax.psum_scatter(vector_total[5], ("dp", "tensor"), scatter_dimension=1, tiled=True),
    )
    matrix_final = (
        lax.psum_scatter(
            matrix_final[0].astype(jnp.bfloat16), "tensor", scatter_dimension=3, tiled=True
        ).astype(jnp.float32),
        lax.psum_scatter(
            matrix_final[1].astype(jnp.bfloat16), "tensor", scatter_dimension=1, tiled=True
        ).astype(jnp.float32),
        lax.psum_scatter(
            matrix_final[2].astype(jnp.bfloat16), "tensor", scatter_dimension=2, tiled=True
        ).astype(jnp.float32),
        lax.psum_scatter(
            matrix_final[3].astype(jnp.bfloat16), "tensor", scatter_dimension=1, tiled=True
        ).astype(jnp.float32),
        lax.psum_scatter(
            matrix_final[4].astype(jnp.bfloat16), "tensor", scatter_dimension=1, tiled=True
        ).astype(jnp.float32),
    )
    grad_qkv, grad_out, grad_up, grad_up_bias, grad_down = matrix_final
    grad_gain_one, grad_bias_one, grad_out_bias, grad_gain_two, grad_bias_two, grad_down_bias = (
        vector_final
    )
    return (
        produced_all[None],
        grad_inputs_all[None],
        grad_gain_one,
        grad_bias_one,
        grad_qkv,
        grad_out,
        grad_out_bias,
        grad_gain_two,
        grad_bias_two,
        grad_up,
        grad_up_bias,
        grad_down,
        grad_down_bias,
    )


def solution(mesh):
    return jax.shard_map(
        on_device,
        mesh=mesh,
        in_specs=(
            P("dp", "tensor", None),
            P("dp", None),
            P("dp", "tensor", None),
            P("section", None),
            P("section", None),
            P("section", None, None, "tensor"),
            P("section", "tensor", None),
            P("section", None),
            P("section", None),
            P("section", None),
            P("section", None, "tensor"),
            P("section", "tensor"),
            P("section", "tensor", None),
            P("section", None),
        ),
        out_specs=(
            P("section", "dp", "tensor", None),
            P("section", "dp", "tensor", None),
            P("section", ("dp", "tensor")),
            P("section", ("dp", "tensor")),
            P("section", "dp", None, "tensor"),
            P("section", "tensor", "dp"),
            P("section", ("dp", "tensor")),
            P("section", ("dp", "tensor")),
            P("section", ("dp", "tensor")),
            P("section", "dp", "tensor"),
            P("section", "tensor", "dp"),
            P("section", "tensor", "dp"),
            P("section", ("dp", "tensor")),
        ),
        check_vma=False,
    )
```

profile of v0, /device:TPU:0, one launch (start us, length us, event | category | flops | bytes accessed | tf_op | source)
XLA Modules:
  0.0 2130.6 jit_solution(13919966785200758895)
XLA Ops:
  11.5 38.5 %all-gather.24.cloned.1.call-done = bf16[1,512,3,512]{1,3,2,0:T(8,128)(2,1)} async-done(((bf16[1,512,3,128]{1,3,2,0:T(8,128)(2,1)}), bf16[1,512,3,512]{1,3,2,0:T(8,128)(2,1)}) %all-gather.24.cloned.1.call-update) | async-done | bytes 1572880 | tf_op jit(solution)/shard_map/all_gather | solution.py:405
  65.8 12.0 all_gather.80
  77.8 15.4 all_gather.78
  99.7 14.8 all-gather.26.cloned.1.call-done
  123.3 36.9 %all-gather.30.cloned.1.call-done = bf16[1,512,2048]{2,1,0:T(8,128)(2,1)} async-done(((bf16[1,512,512]{2,1,0:T(8,128)(2,1)}), bf16[1,512,2048]{2,1,0:T(8,128)(2,1)}) %all-gather.30.cloned.1.call-update) | async-done | bytes 2097168 | tf_op jit(solution)/shard_map/all_gather | solution.py:407
  160.2 7.7 fusion.463
  167.9 38.4 %all-gather.32.cloned.1.call-done = bf16[1,2048,512]{2,1,0:T(8,128)(2,1)} async-done(((bf16[1,512,512]{2,1,0:T(8,128)(2,1)}), bf16[1,2048,512]{2,1,0:T(8,128)(2,1)}) %all-gather.32.cloned.1.call-update) | async-done | bytes 2097168 | tf_op jit(solution)/shard_map/all_gather | solution.py:408
  221.8 23.4 %all-gather.36.cloned.1.call-done = bf16[1024,8,64]{0,2,1:T(8,128)(2,1)} async-done(((bf16[256,8,64]{0,2,1:T(8,128)(2,1)}), bf16[1024,8,64]{0,2,1:T(8,128)(2,1)}) %all-gather.36.cloned.1.call-update) | async-done | bytes 1048592 | tf_op jit(solution)/shard_map/all_gather | solution.py:228
  245.2 6.6 while.312
  252.5 23.4 %all-gather.34.cloned.1.call-done = bf16[1024,8,64]{0,2,1:T(8,128)(2,1)} async-done(((bf16[256,8,64]{0,2,1:T(8,128)(2,1)}), bf16[1024,8,64]{0,2,1:T(8,128)(2,1)}) %all-gather.34.cloned.1.call-update) | async-done | bytes 1048592 | tf_op jit(solution)/shard_map/all_gather | solution.py:229
  275.9 8.8 while.313
  315.0 22.2 %all-gather.40.cloned.1.call-done = bf16[1024,8,64]{0,2,1:T(8,128)(2,1)} async-done(((bf16[256,8,64]{0,2,1:T(8,128)(2,1)}), bf16[1024,8,64]{0,2,1:T(8,128)(2,1)}) %all-gather.40.cloned.1.call-update) | async-done | bytes 1048592 | tf_op jit(solution)/shard_map/all_gather | solution.py:228
  337.3 7.1 while.314
  345.0 22.9 %all-gather.38.cloned.1.call-done = bf16[1024,8,64]{0,2,1:T(8,128)(2,1)} async-done(((bf16[256,8,64]{0,2,1:T(8,128)(2,1)}), bf16[1024,8,64]{0,2,1:T(8,128)(2,1)}) %all-gather.38.cloned.1.call-update) | async-done | bytes 1048592 | tf_op jit(solution)/shard_map/all_gather | solution.py:229
  367.9 8.5 while.315
  398.8 30.4 %all-gather.44.cloned.1.call-done = bf16[1024,8,64]{0,2,1:T(8,128)(2,1)} async-done(((bf16[256,8,64]{0,2,1:T(8,128)(2,1)}), bf16[1024,8,64]{0,2,1:T(8,128)(2,1)}) %all-gather.44.cloned.1.call-update) | async-done | bytes 1048592 | tf_op jit(solution)/shard_map/all_gather | solution.py:228
  429.2 6.6 while.316
  436.5 23.4 %all-gather.42.cloned.1.call-done = bf16[1024,8,64]{0,2,1:T(8,128)(2,1)} async-done(((bf16[256,8,64]{0,2,1:T(8,128)(2,1)}), bf16[1024,8,64]{0,2,1:T(8,128)(2,1)}) %all-gather.42.cloned.1.call-update) | async-done | bytes 1048592 | tf_op jit(solution)/shard_map/all_gather | solution.py:229
  459.9 8.7 while.317
  487.3 33.7 %all-gather.50.cloned.1.call-done = bf16[1024,8,64]{0,2,1:T(8,128)(2,1)} async-done(((bf16[256,8,64]{0,2,1:T(8,128)(2,1)}), bf16[1024,8,64]{0,2,1:T(8,128)(2,1)}) %all-gather.50.cloned.1.call-update) | async-done | bytes 1048592 | tf_op jit(solution)/shard_map/all_gather | solution.py:228
  527.4 24.3 %all-gather.52.cloned.1.call-done = bf16[1024,8,64]{0,2,1:T(8,128)(2,1)} async-done(((bf16[256,8,64]{0,2,1:T(8,128)(2,1)}), bf16[1024,8,64]{0,2,1:T(8,128)(2,1)}) %all-gather.52.cloned.1.call-update) | async-done | bytes 1048592 | tf_op jit(solution)/shard_map/all_gather | solution.py:229
  573.2 14.6 while.322
  593.5 42.4 %reduce-scatter.49.cloned.1.call-done = bf16[256,8,64]{0,2,1:T(8,128)(2,1)} async-done(((bf16[1024,8,64]{0,2,1:T(8,128)(2,1)}), bf16[256,8,64]{0,2,1:T(8,128)(2,1)}) %reduce-scatter.49.cloned.1.call-update) | async-done | bytes 262160 | tf_op jit(solution)/shard_map/reduce_scatter | solution.py:327
  636.0 28.1 %reduce-scatter.47.cloned.1.call-done = bf16[256,8,64]{0,2,1:T(8,128)(2,1)} async-done(((bf16[1024,8,64]{0,2,1:T(8,128)(2,1)}), bf16[256,8,64]{0,2,1:T(8,128)(2,1)}) %reduce-scatter.47.cloned.1.call-update) | async-done | bytes 262160 | tf_op jit(solution)/shard_map/reduce_scatter | solution.py:324
  673.2 25.4 %all-gather.54.cloned.1.call-done = bf16[1024,8,64]{0,2,1:T(8,128)(2,1)} async-done(((bf16[256,8,64]{0,2,1:T(8,128)(2,1)}), bf16[1024,8,64]{0,2,1:T(8,128)(2,1)}) %all-gather.54.cloned.1.call-update) | async-done | bytes 1048592 | tf_op jit(solution)/shard_map/all_gather | solution.py:228
  698.6 6.8 while.323
  705.5 23.7 %all-gather.56.cloned.1.call-done = bf16[1024,8,64]{0,2,1:T(8,128)(2,1)} async-done(((bf16[256,8,64]{0,2,1:T(8,128)(2,1)}), bf16[1024,8,64]{0,2,1:T(8,128)(2,1)}) %all-gather.56.cloned.1.call-update) | async-done | bytes 1048592 | tf_op jit(solution)/shard_map/all_gather | solution.py:229
  753.4 14.6 while.325
  779.3 37.7 %reduce-scatter.53.cloned.1.call-done = bf16[256,8,64]{0,2,1:T(8,128)(2,1)} async-done(((bf16[1024,8,64]{0,2,1:T(8,128)(2,1)}), bf16[256,8,64]{0,2,1:T(8,128)(2,1)}) %reduce-scatter.53.cloned.1.call-update) | async-done | bytes 262160 | tf_op jit(solution)/shard_map/reduce_scatter | solution.py:327
  816.9 28.2 %reduce-scatter.51.cloned.1.call-done = bf16[256,8,64]{0,2,1:T(8,128)(2,1)} async-done(((bf16[1024,8,64]{0,2,1:T(8,128)(2,1)}), bf16[256,8,64]{0,2,1:T(8,128)(2,1)}) %reduce-scatter.51.cloned.1.call-update) | async-done | bytes 262160 | tf_op jit(solution)/shard_map/reduce_scatter | solution.py:324
  867.6 7.9 all-gather.48.cloned.1.call-done
  882.8 22.8 %all-gather.46.cloned.1.call-done = bf16[1024,8,64]{0,2,1:T(8,128)(2,1)} async-done(((bf16[256,8,64]{0,2,1:T(8,128)(2,1)}), bf16[1024,8,64]{0,2,1:T(8,128)(2,1)}) %all-gather.46.cloned.1.call-update) | async-done | bytes 1048592 | tf_op jit(solution)/shard_map/all_gather | solution.py:229
  915.0 22.1 %all-gather.66.cloned.1.call-done = bf16[1024,8,64]{0,2,1:T(8,128)(2,1)} async-done(((bf16[256,8,64]{0,2,1:T(8,128)(2,1)}), bf16[1024,8,64]{0,2,1:T(8,128)(2,1)}) %all-gather.66.cloned.1.call-update) | async-done | bytes 1048592 | tf_op jit(solution)/shard_map/all_gather | solution.py:228
  943.5 23.1 %all-gather.68.cloned.1.call-done = bf16[1024,8,64]{0,2,1:T(8,128)(2,1)} async-done(((bf16[256,8,64]{0,2,1:T(8,128)(2,1)}), bf16[1024,8,64]{0,2,1:T(8,128)(2,1)}) %all-gather.68.cloned.1.call-update) | async-done | bytes 1048592 | tf_op jit(solution)/shard_map/all_gather | solution.py:229
  972.4 24.1 %all-gather.58.cloned.1.call-done = bf16[1024,8,64]{0,2,1:T(8,128)(2,1)} async-done(((bf16[256,8,64]{0,2,1:T(8,128)(2,1)}), bf16[1024,8,64]{0,2,1:T(8,128)(2,1)}) %all-gather.58.cloned.1.call-update) | async-done | bytes 1048592 | tf_op jit(solution)/shard_map/all_gather | solution.py:228
  996.6 6.6 while.326
  1003.2 23.4 %all-gather.62.cloned.1.call-done = bf16[1024,8,64]{0,2,1:T(8,128)(2,1)} async-done(((bf16[256,8,64]{0,2,1:T(8,128)(2,1)}), bf16[1024,8,64]{0,2,1:T(8,128)(2,1)}) %all-gather.62.cloned.1.call-update) | async-done | bytes 1048592 | tf_op jit(solution)/shard_map/all_gather | solution.py:228
  1033.0 23.5 %all-gather.60.cloned.1.call-done = bf16[1024,8,64]{0,2,1:T(8,128)(2,1)} async-done(((bf16[256,8,64]{0,2,1:T(8,128)(2,1)}), bf16[1024,8,64]{0,2,1:T(8,128)(2,1)}) %all-gather.60.cloned.1.call-update) | async-done | bytes 1048592 | tf_op jit(solution)/shard_map/all_gather | solution.py:229
  1065.6 20.9 all-gather.64.cloned.1.call-done
  1113.8 14.7 while.328
  1134.6 42.8 %reduce-scatter.57.cloned.1.call-done = bf16[256,8,64]{0,2,1:T(8,128)(2,1)} async-done(((bf16[1024,8,64]{0,2,1:T(8,128)(2,1)}), bf16[256,8,64]{0,2,1:T(8,128)(2,1)}) %reduce-scatter.57.cloned.1.call-update) | async-done | bytes 262160 | tf_op jit(solution)/shard_map/reduce_scatter | solution.py:327
  1177.4 28.2 %reduce-scatter.55.cloned.1.call-done = bf16[256,8,64]{0,2,1:T(8,128)(2,1)} async-done(((bf16[1024,8,64]{0,2,1:T(8,128)(2,1)}), bf16[256,8,64]{0,2,1:T(8,128)(2,1)}) %reduce-scatter.55.cloned.1.call-update) | async-done | bytes 262160 | tf_op jit(solution)/shard_map/reduce_scatter | solution.py:324
  1226.4 14.6 while.331
  1247.1 37.8 %reduce-scatter.61.cloned.1.call-done = bf16[256,8,64]{0,2,1:T(8,128)(2,1)} async-done(((bf16[1024,8,64]{0,2,1:T(8,128)(2,1)}), bf16[256,8,64]{0,2,1:T(8,128)(2,1)}) %reduce-scatter.61.cloned.1.call-update) | async-done | bytes 262160 | tf_op jit(solution)/shard_map/reduce_scatter | solution.py:327
  1284.9 28.2 %reduce-scatter.59.cloned.1.call-done = bf16[256,8,64]{0,2,1:T(8,128)(2,1)} async-done(((bf16[1024,8,64]{0,2,1:T(8,128)(2,1)}), bf16[256,8,64]{0,2,1:T(8,128)(2,1)}) %reduce-scatter.59.cloned.1.call-update) | async-done | bytes 262160 | tf_op jit(solution)/shard_map/reduce_scatter | solution.py:324
  1321.5 6.6 convert_reduce_fusion
  1335.9 13.6 while.334
  1396.5 11.0 copy.433
  1425.4 7.0 fusion.582
  1462.6 22.6 %reduce-scatter.71.cloned.1.call-done = bf16[1,128,2048]{2,1,0:T(8,128)(2,1)} async-done(((bf16[1,512,2048]{2,1,0:T(8,128)(2,1)}), bf16[1,128,2048]{2,1,0:T(8,128)(2,1)}) %reduce-scatter.71.cloned.1.call-update) | async-done | bytes 524304 | tf_op jit(solution)/shard_map/reduce_scatter | solution.py:495
  1489.3 34.0 %reduce-scatter.93.cloned.1.call-done = bf16[128,2048]{1,0:T(8,128)(2,1)} async-done(((bf16[512,2048]{1,0:T(8,128)(2,1)}), bf16[128,2048]{1,0:T(8,128)(2,1)}) %reduce-scatter.93.cloned.1.call-update) | async-done | bytes 524304
  1533.4 24.0 %reduce-scatter.67.cloned.1.call-done = bf16[1,128,3,512]{3,1,2,0:T(8,128)(2,1)} async-done(((bf16[1,512,3,512]{3,1,2,0:T(8,128)(2,1)}), bf16[1,128,3,512]{3,1,2,0:T(8,128)(2,1)}) %reduce-scatter.67.cloned.1.call-update) | async-done | bytes 393232 | tf_op jit(solution)/shard_map/reduce_scatter | solution.py:489
  1562.2 73.7 %reduce-scatter.85.cloned.1.call-done = f32[32,1]{1,0:T(8,128)} async-done(((f32[512,1]{1,0:T(8,128)}), f32[32,1]{1,0:T(8,128)}) %reduce-scatter.85.cloned.1.call-update) | async-done | bytes 144
  1637.2 73.5 %reduce-scatter.87.cloned.1.call-done = f32[32,1]{1,0:T(8,128)} async-done(((f32[512,1]{1,0:T(8,128)}), f32[32,1]{1,0:T(8,128)}) %reduce-scatter.87.cloned.1.call-update) | async-done | bytes 144
  1711.9 73.7 %reduce-scatter.89.cloned.1.call-done = f32[32,1]{1,0:T(8,128)} async-done(((f32[512,1]{1,0:T(8,128)}), f32[32,1]{1,0:T(8,128)}) %reduce-scatter.89.cloned.1.call-update) | async-done | bytes 144
  1786.9 73.6 %reduce-scatter.95.cloned.1.call-done = f32[32,1]{1,0:T(8,128)} async-done(((f32[512,1]{1,0:T(8,128)}), f32[32,1]{1,0:T(8,128)}) %reduce-scatter.95.cloned.1.call-update) | async-done | bytes 144
  1861.8 22.1 %reduce-scatter.91.cloned.1.call-done = bf16[128,4]{1,0:T(8,128)(2,1)} async-done(((bf16[512,4]{1,0:T(8,128)(2,1)}), bf16[128,4]{1,0:T(8,128)(2,1)}) %reduce-scatter.91.cloned.1.call-update) | async-done | bytes 1040
  1884.8 11.7 all-reduce.3
  1897.6 8.1 reduce-scatter.69.cloned.1.call-done
  1909.4 73.6 %reduce-scatter.77.cloned.1.call-done = f32[32,1]{1,0:T(8,128)} async-done(((f32[512,1]{1,0:T(8,128)}), f32[32,1]{1,0:T(8,128)}) %reduce-scatter.77.cloned.1.call-update) | async-done | bytes 144
  1984.3 74.1 %reduce-scatter.79.cloned.1.call-done = f32[32,1]{1,0:T(8,128)} async-done(((f32[512,1]{1,0:T(8,128)}), f32[32,1]{1,0:T(8,128)}) %reduce-scatter.79.cloned.1.call-update) | async-done | bytes 144
  2059.7 19.1 reduce-scatter.73.cloned.1.call-done
  2080.4 20.6 reduce-scatter.75.cloned.1.call-done
  2102.6 19.5 reduce-scatter.81.cloned.1.call-done
  (1543 shorter events, 648.7 us)
Async XLA Ops:
  7.2 42.8 %all-gather.24.cloned.1.call-start = ((), (), s32[]{:S(2)}) async-start(), calls=%async_computation.25 | async-start | bytes 1966080 | tf_op jit(solution)/shard_map/all_gather | solution.py:405
  9.2 84.1 %all-gather.28.cloned.1.call-start = ((), (), s32[]{:S(2)}) async-start(), calls=%async_computation.27 | async-start | bytes 1310720 | tf_op jit(solution)/shard_map/all_gather | solution.py:228
  53.1 61.4 %all-gather.26.cloned.1.call-start = ((), (), s32[]{:S(2)}) async-start(), calls=%async_computation.26 | async-start | bytes 1310720 | tf_op jit(solution)/shard_map/all_gather | solution.py:229
  54.0 106.2 %all-gather.30.cloned.1.call-start = ((), (), s32[]{:S(2)}) async-start(), calls=%async_computation.28 | async-start | bytes 2621440 | tf_op jit(solution)/shard_map/all_gather | solution.py:407
  54.6 151.7 %all-gather.32.cloned.1.call-start = ((), (), s32[]{:S(2)}) async-start(), calls=%async_computation.29 | async-start | bytes 2621440 | tf_op jit(solution)/shard_map/all_gather | solution.py:408
  55.2 190.0 %all-gather.36.cloned.1.call-start = ((), (), s32[]{:S(2)}) async-start(), calls=%async_computation.31 | async-start | bytes 1310720 | tf_op jit(solution)/shard_map/all_gather | solution.py:228
  77.8 82.4 %copy-start.245 = (f32[1,2048]{1,0:T(1,128)}, f32[1,2048]{1,0:T(1,128)S(1)}, u32[]{:S(2)}) copy-start(f32[1,2048]{1,0:T(1,128)S(1)} %all_gather.80) | copy-start | bytes 24580
  93.1 475.5 %copy-start = (bf16[1,512,512]{2,1,0:T(8,128)(2,1)}, bf16[1,512,512]{2,1,0:T(8,128)(2,1)S(1)}, u32[]{:S(2)}) copy-start(bf16[1,512,512]{2,1,0:T(8,128)(2,1)S(1)} %all_gather.78) | copy-start | bytes 1572868
  209.3 3.0 collective-permute-start
  216.1 59.8 %all-gather.34.cloned.1.call-start = ((), (), s32[]{:S(2)}) async-start(), calls=%async_computation.30 | async-start | bytes 1310720 | tf_op jit(solution)/shard_map/all_gather | solution.py:229
  221.8 115.4 %all-gather.40.cloned.1.call-start = ((), (), s32[]{:S(2)}) async-start(), calls=%async_computation.33 | async-start | bytes 1310720 | tf_op jit(solution)/shard_map/all_gather | solution.py:228
  293.5 2.6 collective-permute-start.1
  299.9 68.0 %all-gather.38.cloned.1.call-start = ((), (), s32[]{:S(2)}) async-start(), calls=%async_computation.32 | async-start | bytes 1310720 | tf_op jit(solution)/shard_map/all_gather | solution.py:229
  314.9 114.3 %all-gather.44.cloned.1.call-start = ((), (), s32[]{:S(2)}) async-start(), calls=%async_computation.35 | async-start | bytes 1310720 | tf_op jit(solution)/shard_map/all_gather | solution.py:228
  385.3 2.6 collective-permute-start.2
  392.0 67.9 %all-gather.42.cloned.1.call-start = ((), (), s32[]{:S(2)}) async-start(), calls=%async_computation.34 | async-start | bytes 1310720 | tf_op jit(solution)/shard_map/all_gather | solution.py:229
  398.8 122.2 %all-gather.50.cloned.1.call-start = ((), (), s32[]{:S(2)}) async-start(), calls=%async_computation.38 | async-start | bytes 1310720 | tf_op jit(solution)/shard_map/all_gather | solution.py:228
  477.6 2.6 collective-permute-start.3
  480.3 383.6 %copy-start.5 = (bf16[4,256,512]{2,1,0:T(8,128)(2,1)}, bf16[4,256,512]{2,1,0:T(8,128)(2,1)S(1)}, u32[]{:S(2)}) copy-start(bf16[4,256,512]{2,1,0:T(8,128)(2,1)S(1)} %broadcast_select_fusion) | copy-start | bytes 3145732
  483.7 68.0 %all-gather.52.cloned.1.call-start = ((), (), s32[]{:S(2)}) async-start(), calls=%async_computation.39 | async-start | bytes 1310720 | tf_op jit(solution)/shard_map/all_gather | solution.py:229
  487.3 148.7 %reduce-scatter.49.cloned.1.call-start = ((), (), s32[]{:S(2)}) async-start(), calls=%async_computation.41 | async-start | bytes 1310720 | tf_op jit(solution)/shard_map/reduce_scatter | solution.py:327
  590.6 73.4 %reduce-scatter.47.cloned.1.call-start = ((), (), s32[]{:S(2)}) async-start(), calls=%async_computation.40 | async-start | bytes 1310720 | tf_op jit(solution)/shard_map/reduce_scatter | solution.py:324
  593.4 105.2 %all-gather.54.cloned.1.call-start = ((), (), s32[]{:S(2)}) async-start(), calls=%async_computation.42 | async-start | bytes 1310720 | tf_op jit(solution)/shard_map/all_gather | solution.py:228
  669.6 59.5 %all-gather.56.cloned.1.call-start = ((), (), s32[]{:S(2)}) async-start(), calls=%async_computation.43 | async-start | bytes 1310720 | tf_op jit(solution)/shard_map/all_gather | solution.py:229
  673.2 143.7 %reduce-scatter.53.cloned.1.call-start = ((), (), s32[]{:S(2)}) async-start(), calls=%async_computation.45 | async-start | bytes 1310720 | tf_op jit(solution)/shard_map/reduce_scatter | solution.py:327
  737.7 6.7 collective-permute-start.4
  770.8 74.3 %reduce-scatter.51.cloned.1.call-start = ((), (), s32[]{:S(2)}) async-start(), calls=%async_computation.44 | async-start | bytes 1310720 | tf_op jit(solution)/shard_map/reduce_scatter | solution.py:324
  773.7 101.8 %all-gather.48.cloned.1.call-start = ((), (), s32[]{:S(2)}) async-start(), calls=%async_computation.37 | async-start | bytes 1310720 | tf_op jit(solution)/shard_map/all_gather | solution.py:228
  778.2 127.4 %all-gather.46.cloned.1.call-start = ((), (), s32[]{:S(2)}) async-start(), calls=%async_computation.36 | async-start | bytes 1310720 | tf_op jit(solution)/shard_map/all_gather | solution.py:229
  779.1 84.8 %copy-start.279 = (f32[256]{0:T(256)}, f32[256]{0:T(256)S(1)}, u32[]{:S(2)}) copy-start(f32[256]{0:T(256)S(1)} %get-tuple-element.2879) | copy-start | bytes 3076
  779.1 157.9 %all-gather.66.cloned.1.call-start = ((), (), s32[]{:S(2)}) async-start(), calls=%async_computation.54 | async-start | bytes 1310720 | tf_op jit(solution)/shard_map/all_gather | solution.py:228
  851.7 114.9 %all-gather.68.cloned.1.call-start = ((), (), s32[]{:S(2)}) async-start(), calls=%async_computation.55 | async-start | bytes 1310720 | tf_op jit(solution)/shard_map/all_gather | solution.py:229
  852.6 143.9 %all-gather.58.cloned.1.call-start = ((), (), s32[]{:S(2)}) async-start(), calls=%async_computation.46 | async-start | bytes 1310720 | tf_op jit(solution)/shard_map/all_gather | solution.py:228
  856.1 170.5 %all-gather.62.cloned.1.call-start = ((), (), s32[]{:S(2)}) async-start(), calls=%async_computation.50 | async-start | bytes 1310720 | tf_op jit(solution)/shard_map/all_gather | solution.py:228
  867.5 189.0 %all-gather.60.cloned.1.call-start = ((), (), s32[]{:S(2)}) async-start(), calls=%async_computation.47 | async-start | bytes 1310720 | tf_op jit(solution)/shard_map/all_gather | solution.py:229
  882.8 203.7 %all-gather.64.cloned.1.call-start = ((), (), s32[]{:S(2)}) async-start(), calls=%async_computation.51 | async-start | bytes 1310720 | tf_op jit(solution)/shard_map/all_gather | solution.py:229
  914.9 262.4 %reduce-scatter.57.cloned.1.call-start = ((), (), s32[]{:S(2)}) async-start(), calls=%async_computation.49 | async-start | bytes 1310720 | tf_op jit(solution)/shard_map/reduce_scatter | solution.py:327
  972.4 90.2 %copy-start.82 = (f32[256,8,64]{0,2,1:T(8,128)}, f32[256,8,64]{0,2,1:T(8,128)S(1)}, u32[]{:S(2)}) copy-start(f32[256,8,64]{0,2,1:T(8,128)S(1)} %get-tuple-element.1814) | copy-start | bytes 1572868
  1098.1 6.7 collective-permute-start.5
  1109.4 99.9 %copy-start.68 = (f32[256,512]{1,0:T(8,128)}, f32[256,512]{1,0:T(8,128)S(1)}, u32[]{:S(2)}) copy-start(f32[256,512]{1,0:T(8,128)S(1)} %get-tuple-element.2734) | copy-start | bytes 1572868
  1131.3 74.3 %reduce-scatter.55.cloned.1.call-start = ((), (), s32[]{:S(2)}) async-start(), calls=%async_computation.48 | async-start | bytes 1310720 | tf_op jit(solution)/shard_map/reduce_scatter | solution.py:324
  1134.2 150.6 %reduce-scatter.61.cloned.1.call-start = ((), (), s32[]{:S(2)}) async-start(), calls=%async_computation.53 | async-start | bytes 1310720 | tf_op jit(solution)/shard_map/reduce_scatter | solution.py:327
  1134.3 86.4 %copy-start.274 = (f32[256]{0:T(256)}, f32[256]{0:T(256)S(1)}, u32[]{:S(2)}) copy-start(f32[256]{0:T(256)S(1)} %broadcast_multiply_fusion.2) | copy-start | bytes 3076
  1134.5 86.2 %copy-start.309 = (f32[256]{0:T(256)}, f32[256]{0:T(256)S(1)}, u32[]{:S(2)}) copy-start(f32[256]{0:T(256)S(1)} %fusion.966) | copy-start | bytes 3076
  1210.3 6.9 collective-permute-start.6
  1243.7 69.4 %reduce-scatter.59.cloned.1.call-start = ((), (), s32[]{:S(2)}) async-start(), calls=%async_computation.52 | async-start | bytes 1310720 | tf_op jit(solution)/shard_map/reduce_scatter | solution.py:324
  1246.7 177.5 %reduce-scatter.65.cloned.1.call-start = ((), (), s32[]{:S(2)}) async-start(), calls=%async_computation.57 | async-start | bytes 1310720 | tf_op jit(solution)/shard_map/reduce_scatter | solution.py:327
  1317.9 3.7 collective-permute-start.7
  1352.3 71.9 %reduce-scatter.63.cloned.1.call-start = ((), (), s32[]{:S(2)}) async-start(), calls=%async_computation.56 | async-start | bytes 1310720 | tf_op jit(solution)/shard_map/reduce_scatter | solution.py:324
  1353.6 97.6 %reduce-scatter.83.cloned.1.call-start = ((), (), s32[]{:S(2)}) async-start(), calls=%async_computation.66 | async-start | bytes 655360
  1370.4 114.8 %reduce-scatter.71.cloned.1.call-start = ((), (), s32[]{:S(2)}) async-start(), calls=%async_computation.60 | async-start | bytes 2621440 | tf_op jit(solution)/shard_map/reduce_scatter | solution.py:495
  1379.9 143.4 %reduce-scatter.93.cloned.1.call-start = ((), (), s32[]{:S(2)}) async-start(), calls=%async_computation.71 | async-start | bytes 2621440
  1412.3 145.0 %reduce-scatter.67.cloned.1.call-start = ((), (), s32[]{:S(2)}) async-start(), calls=%async_computation.58 | async-start | bytes 1966080 | tf_op jit(solution)/shard_map/reduce_scatter | solution.py:489
  1432.5 203.4 %reduce-scatter.85.cloned.1.call-start = ((), (), s32[]{:S(2)}) async-start(), calls=%async_computation.67 | async-start | bytes 278528
  1445.5 265.1 %reduce-scatter.87.cloned.1.call-start = ((), (), s32[]{:S(2)}) async-start(), calls=%async_computation.68 | async-start | bytes 278528
  1446.5 339.1 %reduce-scatter.89.cloned.1.call-start = ((), (), s32[]{:S(2)}) async-start(), calls=%async_computation.69 | async-start | bytes 278528
  1447.5 413.0 %reduce-scatter.95.cloned.1.call-start = ((), (), s32[]{:S(2)}) async-start(), calls=%async_computation.72 | async-start | bytes 278528
  1448.5 435.4 %reduce-scatter.91.cloned.1.call-start = ((), (), s32[]{:S(2)}) async-start(), calls=%async_computation.70 | async-start | bytes 163840
  1451.2 454.6 %reduce-scatter.69.cloned.1.call-start = ((), (), s32[]{:S(2)}) async-start(), calls=%async_computation.59 | async-start | bytes 163840 | tf_op jit(solution)/shard_map/reduce_scatter | solution.py:517
  1454.8 528.2 %reduce-scatter.77.cloned.1.call-start = ((), (), s32[]{:S(2)}) async-start(), calls=%async_computation.63 | async-start | bytes 278528
  1459.3 599.1 %reduce-scatter.79.cloned.1.call-start = ((), (), s32[]{:S(2)}) async-start(), calls=%async_computation.64 | async-start | bytes 278528
  1460.3 618.5 %reduce-scatter.73.cloned.1.call-start = ((), (), s32[]{:S(2)}) async-start(), calls=%async_computation.61 | async-start | bytes 655360 | tf_op jit(solution)/shard_map/reduce_scatter | solution.py:520
  1485.3 615.7 %reduce-scatter.75.cloned.1.call-start = ((), (), s32[]{:S(2)}) async-start(), calls=%async_computation.62 | async-start | bytes 655360 | tf_op jit(solution)/shard_map/reduce_scatter | solution.py:526
  1529.4 592.6 %reduce-scatter.81.cloned.1.call-start = ((), (), s32[]{:S(2)}) async-start(), calls=%async_computation.65 | async-start | bytes 491520
  (389 other events, 2834.7 us)
Sparse Core Ops, SparseCore 0:
  10.2 39.7 all-gather.23
  53.2 32.0 all-gather.27
  87.5 26.9 all-gather.25
  115.9 44.2 all-gather.29
  161.6 44.6 all-gather.31
  216.2 28.9 all-gather.35
  247.3 28.4 all-gather.33
  300.0 37.1 all-gather.39
  339.4 28.4 all-gather.37
  392.1 37.0 all-gather.43
  431.4 28.4 all-gather.41
  483.8 37.1 all-gather.49
  523.1 28.4 all-gather.51
  590.7 45.1 reduce-scatter.48
  638.2 25.7 reduce-scatter.46
  669.8 28.8 all-gather.53
  700.6 28.4 all-gather.55
  770.9 45.9 reduce-scatter.52
  819.3 25.7 reduce-scatter.50
  846.5 28.8 all-gather.47
  877.0 28.4 all-gather.45
  907.7 29.3 all-gather.65
  939.2 27.3 all-gather.67
  968.0 28.4 all-gather.57
  998.1 28.4 all-gather.61
  1028.0 28.4 all-gather.59
  1058.0 28.4 all-gather.63
  1131.4 45.9 reduce-scatter.56
  1179.8 25.7 reduce-scatter.54
  1243.9 40.9 reduce-scatter.60
  1287.3 25.7 reduce-scatter.58
  1352.4 39.3 reduce-scatter.64
  1394.1 25.7 reduce-scatter.62
  1422.7 23.4 reduce-scatter.82
  1450.0 35.1 reduce-scatter.70
  1488.1 35.1 reduce-scatter.92
  1526.4 30.9 reduce-scatter.66
  1559.7 76.1 reduce-scatter.84
  1637.9 72.6 reduce-scatter.86
  1712.9 72.6 reduce-scatter.88
  1787.9 72.5 reduce-scatter.94
  1863.5 20.3 reduce-scatter.90
  1886.5 19.1 reduce-scatter.68
  1908.7 74.2 reduce-scatter.76
  1985.7 72.6 reduce-scatter.78
  2060.6 18.1 reduce-scatter.72
  2081.0 19.9 reduce-scatter.74
  2103.2 18.8 reduce-scatter.80
where the time goes:
time: 2140 us; the launch traced here: 2130 us
  waiting for transfers between devices  1440 us (67%)
  matrix products  307 us (14%)
  local copies, waits for them, and re-layouts  155 us (7%)
  other arithmetic  123 us (6%)
  between operations  43.4 us (2%)
  blocking collectives  39.1 us (2%)
    unnamed x58, waiting for transfers between devices  519 us
    all_gather x10, waiting for transfers between devices, forward_layer(): lax.all_gather(values, 'tensor', axis=0, tiled=True)  223 us
    all_gather x10, waiting for transfers between devices, forward_layer(): lax.all_gather(key_rows, 'tensor', axis=0, tiled=True)  213 us
    reduce_scatter x5, waiting for transfers between devices, backward_layer(): lax.psum_scatter(grad_values.astype(jnp.bfloat16), 'tensor', scatter_dime...  161 us
    reduce_scatter x5, waiting for transfers between devices, backward_layer(): lax.psum_scatter(grad_keys.astype(jnp.bfloat16), 'tensor', scatter_dimens...  113 us
    unnamed x772, local copies, waits for them, and re-layouts  79.8 us
    dot_general x10, matrix products, accumulate(): jnp.einsum('hqk,khe->qhe', weights, value_rows, preferred_element_type=jn...  54 us
    dot_general x10, matrix products, forward_layer(): jnp.dot(normed_two, up_weight, preferred_element_type=jnp.float32) + up_bias  52.4 us
  transfers between devices with their start and end apart: 56, of which 49 were waited for; matrix products, arithmetic and copies ran while one was open for 15% of the time, Pallas kernels for 0%

commit v1 on v0

--- a/solution.py
+++ b/solution.py
@@ -4,6 +4,8 @@
 import jax
 import jax.numpy as jnp
 from jax import lax
+from jax.experimental import pallas as pl
+from jax.experimental.pallas import tpu as pltpu
 from jax.sharding import PartitionSpec as P
 
 HEAD = 64
@@ -548,9 +550,801 @@
     )
 
 
+MESH = pl.DeviceIdType.MESH
+PARTS = 4
+BLOCK = 256
+OWN = 512
+WIDTH = 512
+PAIRS = 4
+TASKS = 5
+NEGATIVE = -1e30
+LEFT = (((1,), (0,)), ((), ()))
+BOTH_LAST = (((1,), (1,)), ((), ()))
+BOTH_FIRST = (((0,), (0,)), ((), ()))
+
+
+def whole_batch_fits(mesh):
+    shape = dict(mesh.shape)
+    return shape["tensor"] == PARTS and shape["dp"] == PARTS and shape["section"] == 2
+
+
+def dot(left, right, dims=LEFT):
+    return lax.dot_general(left, right, dims, preferred_element_type=jnp.float32)
+
+
+def place():
+    return lax.axis_index("section"), lax.axis_index("dp"), lax.axis_index("tensor")
+
+
+def blocks_of(core):
+    return (core, 3 - core)
+
+
+def tile_rows(start, count):
+    return pl.ds(pl.multiple_of(start, count), count)
+
+
+def standard(values):
+    centre = values - jnp.mean(values, axis=-1, keepdims=True)
+    spread = jnp.mean(centre * centre, axis=-1, keepdims=True)
+    inverse = lax.rsqrt(spread + 1e-05)
+    return centre * inverse, inverse
+
+
+def standard_back(grads, gain, units, inverse):
+    scaled = grads * gain
+    inner = jnp.mean(scaled * units, axis=-1, keepdims=True)
+    return inverse * (scaled - jnp.mean(scaled, axis=-1, keepdims=True) - units * inner)
+
+
+def column_sum(values):
+    return jnp.sum(values, axis=0, keepdims=True)
+
+
+def keep_head(values, parity):
+    lane = lax.broadcasted_iota(jnp.int32, values.shape, 1)
+    return jnp.where((lane < HEAD) == (parity == 0), values, 0.0)
+
+
+def project(x_ref, vec_ref, weight_ref, normed_t_ref, query_ref, kv_ref, normed_ref):
+    gain, bias = vec_ref[0, 0:1, :], vec_ref[0, 1:2, :]
+
+    def norm_rows(index, carry):
+        rows = tile_rows(index * 128, 128)
+        units, _ = standard(x_ref[rows, :].astype(jnp.float32))
+        normed_ref[rows, :] = (units * gain + bias).astype(jnp.bfloat16)
+        return carry
+
+    lax.fori_loop(0, OWN // 128, norm_rows, 0)
+    normed_t_ref[...] = normed_ref[...].T
+
+    def pair_step(pair, carry):
+        out = dot(normed_ref[...], weight_ref[pair])
+        queries = out[:, :128] * 0.125
+        for parity in range(2):
+            query_ref[pair, parity] = keep_head(queries, parity).astype(jnp.bfloat16)
+        kv_ref[0, pair] = out[:, 128:256].astype(jnp.bfloat16)
+        kv_ref[1, pair] = out[:, 256:].astype(jnp.bfloat16)
+        return carry
+
+    lax.fori_loop(0, PAIRS, pair_step, 0)
+
+
+def task_plan(core):
+    first = core == 0
+    slots = (0, jnp.where(first, 1, 0), 1, 1, 1)
+    keys = (0, jnp.where(first, 0, 1), jnp.where(first, 1, 0), jnp.where(first, 2, 1), jnp.where(first, 3, 2))
+    return slots, keys
+
+
+def attend_rows(signed, query_ref, kv_ref, bias_ref, attended_ref, attended_t_ref, log_ref, logit_ref, factor_ref, stat_ref):
+    core = lax.axis_index("section")
+    slots, keys = task_plan(core)
+    middle_late = core == 0
+    lane = lax.broadcasted_iota(jnp.int32, (BLOCK, 128), 1)
+
+    def pair_step(pair, carry):
+        outs = [[None, None], [None, None]]
+        for parity in range(2):
+            tops = []
+            for task in range(TASKS):
+                rows = tile_rows(slots[task] * BLOCK, BLOCK)
+                key_rows = tile_rows(keys[task] * BLOCK, BLOCK)
+                scores = dot(query_ref[pair, parity, rows, :], kv_ref[0, pair, key_rows, :], BOTH_LAST)
+                if signed:
+                    raised = scores * scores + 1.0
+                    inverse = lax.rsqrt(raised)
+                    factor_ref[task] = scores * inverse
+                    scores = raised * inverse
+                logits = scores + bias_ref[task]
+                logit_ref[task] = logits
+                tops.append(jnp.maximum(logits[:, :128], logits[:, 128:]))
+            low = jnp.full((BLOCK, 128), NEGATIVE, jnp.float32)
+            top_early = jnp.maximum(tops[0], jnp.where(middle_late, low, tops[1]))
+            top_late = jnp.maximum(jnp.maximum(tops[2], tops[3]), jnp.maximum(tops[4], jnp.where(middle_late, tops[1], low)))
+            max_early = jnp.max(top_early, axis=-1, keepdims=True)
+            max_late = jnp.max(top_late, axis=-1, keepdims=True)
+            max_middle = jnp.where(middle_late, max_late, max_early)
+            shifts = (max_early, max_middle, max_late, max_late, max_late)
+            sums, terms = [], []
+            for task in range(TASKS):
+                key_rows = tile_rows(keys[task] * BLOCK, BLOCK)
+                powers = jnp.exp(logit_ref[task] - shifts[task])
+                sums.append(powers[:, :128] + powers[:, 128:])
+                if signed:
+                    powers = powers * factor_ref[task]
+                terms.append(dot(powers.astype(jnp.bfloat16), kv_ref[1, pair, key_rows, :]))
+            early = jnp.where(middle_late, 0.0, 1.0)
+            late = 1.0 - early
+            totals = (sums[0] + sums[1] * early, sums[2] + sums[3] + sums[4] + sums[1] * late)
+            values = (terms[0] + terms[1] * early, terms[2] + terms[3] + terms[4] + terms[1] * late)
+            for slot, top in enumerate((max_early, max_late)):
+                total = jnp.sum(totals[slot], axis=-1, keepdims=True)
+                outs[slot][parity] = values[slot] / total
+                head = pair * 2 + parity
+                stat_ref[slot] = jnp.where(lane == head, top + jnp.log(total), stat_ref[slot])
+        for slot in range(2):
+            merged = jnp.where(lane < HEAD, outs[slot][0], outs[slot][1])
+            attended_ref[pair, slot * BLOCK : (slot + 1) * BLOCK, :] = merged
+            attended_t_ref[pair, :, slot * BLOCK : (slot + 1) * BLOCK] = merged.T.astype(jnp.bfloat16)
+        return carry
+
+    stat_ref[...] = jnp.zeros_like(stat_ref)
+    lax.fori_loop(0, PAIRS, pair_step, 0)
+    for slot in range(2):
+        log_ref[slot] = stat_ref[slot].T[:8, :]
+
+
+def gelu_both(values):
+    lower = 0.5 * (1.0 + lax.erf(values * math.sqrt(0.5)))
+    density = jnp.exp(-0.5 * values * values) * (1.0 / math.sqrt(2.0 * math.pi))
+    return values * lower, lower + values * density
+
+
+def feed(x_ref, attended_ref, vec_ref, out_ref, up_ref, down_ref, hidden_ref, normed_t_ref, act_ref, slope_ref, y_ref, normed_ref, wide_ref, sum_ref):
+    out_bias = vec_ref[0, 2:3, :]
+    gain, bias = vec_ref[0, 3:4, :], vec_ref[0, 4:5, :]
+    down_bias = vec_ref[0, 5:6, :]
+    sum_ref[...] = jnp.zeros_like(sum_ref)
+
+    def out_step(pair, carry):
+        sum_ref[...] += dot(attended_ref[pair].astype(jnp.bfloat16), out_ref[pair])
+        return carry
+
+    lax.fori_loop(0, PAIRS, out_step, 0)
+
+    def norm_rows(index, carry):
+        rows = tile_rows(index * 128, 128)
+        hidden = x_ref[rows, :].astype(jnp.float32) + sum_ref[rows, :] + out_bias
+        hidden_ref[rows, :] = hidden
+        units, _ = standard(hidden)
+        normed_ref[rows, :] = (units * gain + bias).astype(jnp.bfloat16)
+        sum_ref[rows, :] = hidden + down_bias
+        return carry
+
+    lax.fori_loop(0, OWN // 128, norm_rows, 0)
+    normed_t_ref[...] = normed_ref[...].T
+
+    def chunk_step(chunk, carry):
+        wide_ref[...] = dot(normed_ref[...], up_ref[chunk])
+        up_bias = vec_ref[chunk, 6:7, :]
+
+        def gelu_rows(index, inner):
+            rows = tile_rows(index * 32, 32)
+            act, slope = gelu_both(wide_ref[rows, :] + up_bias)
+            act_ref[chunk, rows, :] = act.astype(jnp.bfloat16)
+            slope_ref[chunk, rows, :] = slope.astype(jnp.bfloat16)
+            return inner
+
+        lax.fori_loop(0, OWN // 32, gelu_rows, 0)
+        sum_ref[...] += dot(act_ref[chunk], down_ref[chunk])
+        return carry
+
+    lax.fori_loop(0, PARTS, chunk_step, 0)
+    y_ref[...] = sum_ref[...].astype(jnp.bfloat16)
+
+
+def feed_back(dy_ref, act_ref, slope_ref, down_ref, up_ref, hidden_ref, normed_t_ref, vec_ref, out_ref, attended_ref, attended_t_ref, grad_hidden_ref, grad_att_ref, centre_ref, grads_ref, vec_grad_ref, low_ref, low_t_ref, chunk_ref, sum_ref):
+    gain = vec_ref[0, 3:4, :]
+    low_ref[...] = dy_ref[...].astype(jnp.bfloat16)
+    low_t_ref[...] = low_ref[...].T
+    vec_grad_ref[...] = jnp.zeros_like(vec_grad_ref)
+    sum_ref[...] = jnp.zeros_like(sum_ref)
+
+    def chunk_step(chunk, carry):
+        grad_act = dot(low_ref[...], down_ref[chunk], BOTH_LAST)
+        grad_up = (grad_act * slope_ref[chunk].astype(jnp.float32)).astype(jnp.bfloat16)
+        chunk_ref[...] = grad_up
+        vec_grad_ref[pl.ds(6 + chunk, 1), :] = column_sum(grad_up.astype(jnp.float32))
+        down_term = dot(low_t_ref[...], act_ref[chunk]).astype(jnp.bfloat16)
+        up_term = dot(normed_t_ref[...], chunk_ref[...]).astype(jnp.bfloat16)
+        for part in range(PARTS):
+            grads_ref[part, chunk, :, 0:512] = down_term[part * 128 : (part + 1) * 128, :]
+            grads_ref[part, chunk, :, 512:1024] = up_term[part * 128 : (part + 1) * 128, :]
+        sum_ref[...] += dot(chunk_ref[...], up_ref[chunk], BOTH_LAST)
+        return carry
+
+    lax.fori_loop(0, PARTS, chunk_step, 0)
+
+    def norm_rows(index, carry):
+        rows = tile_rows(index * 128, 128)
+        grads, dy = sum_ref[rows, :], dy_ref[rows, :]
+        units, inverse = standard(hidden_ref[rows, :])
+        grad_hidden = dy + standard_back(grads, gain, units, inverse)
+        grad_hidden_ref[rows, :] = grad_hidden
+        low_ref[rows, :] = grad_hidden.astype(jnp.bfloat16)
+        vec_grad_ref[2:3, :] += column_sum(grad_hidden)
+        vec_grad_ref[3:4, :] += column_sum(grads * units)
+        vec_grad_ref[4:5, :] += column_sum(grads)
+        vec_grad_ref[5:6, :] += column_sum(dy)
+        return carry
+
+    lax.fori_loop(0, OWN // 128, norm_rows, 0)
+    row = lax.broadcasted_iota(jnp.int32, (8, 128), 0)
+    lane = lax.broadcasted_iota(jnp.int32, (8, 128), 1)
+    picks = jnp.where((row < 2) & ((lane < HEAD) == (row == 0)), 1.0, 0.0)
+
+    def pair_step(pair, carry):
+        out_term = dot(attended_t_ref[pair], low_ref[...]).astype(jnp.bfloat16)
+        for part in range(PARTS):
+            grads_ref[part, pair, :, 1024:1152] = out_term[:, part * 128 : (part + 1) * 128]
+        grad_att = dot(low_ref[...], out_ref[pair], BOTH_LAST).astype(jnp.bfloat16)
+        wide = grad_att.astype(jnp.float32)
+        for parity in range(2):
+            grad_att_ref[pair, parity] = keep_head(wide, parity).astype(jnp.bfloat16)
+        centres = lax.dot_general(picks, wide * attended_ref[pair], BOTH_LAST, precision=lax.Precision.HIGHEST, preferred_element_type=jnp.float32)
+        centre_ref[pair] = centres
+        return carry
+
+    lax.fori_loop(0, PAIRS, pair_step, 0)
+
+
+def attend_rows_back(signed, query_ref, kv_ref, grad_att_ref, bias_ref, log_ref, centre_ref, grad_query_ref, grad_kv_ref, grad_kv_low_ref):
+    core = lax.axis_index("section")
+    slots, keys = task_plan(core)
+    early = jnp.where(core == 0, 0.0, 1.0)
+    lane = lax.broadcasted_iota(jnp.int32, (BLOCK, 128), 1)
+    grad_kv_ref[...] = jnp.zeros_like(grad_kv_ref)
+
+    def pair_step(pair, carry):
+        parts = [[None] * TASKS, [None] * TASKS]
+        for task in range(TASKS):
+            rows = tile_rows(slots[task] * BLOCK, BLOCK)
+            key_rows = tile_rows(keys[task] * BLOCK, BLOCK)
+            key_part, value_part = kv_ref[0, pair, key_rows, :], kv_ref[1, pair, key_rows, :]
+            key_term, value_term = None, None
+            for parity in range(2):
+                queries = query_ref[pair, parity, rows, :]
+                grad_att = grad_att_ref[pair, parity, rows, :]
+                scores = dot(key_part, queries, BOTH_LAST)
+                grad_weights = dot(value_part, grad_att, BOTH_LAST)
+                log_row = log_ref[slots[task], pl.ds(pair * 2 + parity, 1), :]
+                centre = centre_ref[pair, parity : parity + 1, rows]
+                if signed:
+                    raised = scores * scores + 1.0
+                    inverse = lax.rsqrt(raised)
+                    factor = scores * inverse
+                    probs = jnp.exp(raised * inverse + bias_ref[task] - log_row)
+                    weights = factor * probs
+                    grad_scores = weights * (factor * grad_weights - centre)
+                    grad_scores = grad_scores + probs * grad_weights * (inverse * inverse * inverse)
+                else:
+                    weights = jnp.exp(scores + bias_ref[task] - log_row)
+                    grad_scores = weights * (grad_weights - centre)
+                grad_low = grad_scores.astype(jnp.bfloat16)
+                new_key = dot(grad_low, queries)
+                new_value = dot(weights.astype(jnp.bfloat16), grad_att)
+                key_term = new_key if parity == 0 else key_term + new_key
+                value_term = new_value if parity == 0 else value_term + new_value
+                parts[parity][task] = dot(grad_low, key_part, BOTH_FIRST)
+            grad_kv_ref[0, pair, key_rows, :] += key_term
+            grad_kv_ref[1, pair, key_rows, :] += value_term
+        merged = []
+        for task in range(TASKS):
+            merged.append(jnp.where(lane < HEAD, parts[0][task], parts[1][task]))
+        grad_query_ref[pair, :BLOCK, :] = ((merged[0] + merged[1] * early) * 0.125).astype(jnp.bfloat16)
+        grad_query_ref[pair, BLOCK:, :] = ((merged[1] * (1.0 - early) + merged[2] + merged[3] + merged[4]) * 0.125).astype(jnp.bfloat16)
+        grad_kv_low_ref[0, pair] = grad_kv_ref[0, pair].astype(jnp.bfloat16)
+        grad_kv_low_ref[1, pair] = grad_kv_ref[1, pair].astype(jnp.bfloat16)
+        return carry
+
+    lax.fori_loop(0, PAIRS, pair_step, 0)
+
+
+def project_back(grad_query_ref, grad_kv_ref, other_ref, x_ref, grad_hidden_ref, normed_t_ref, weight_ref, vec_ref, grad_x_ref, grads_ref, vec_grad_ref, sum_ref):
+    core = lax.axis_index("section")
+    gain = vec_ref[0, 0:1, :]
+    sum_ref[...] = jnp.zeros_like(sum_ref)
+    vec_grad_ref[...] = jnp.zeros_like(vec_grad_ref)
+
+    def pair_step(pair, carry):
+        parts = [grad_query_ref[pair]]
+        for kind in range(2):
+            halves = []
+            for slot, block in enumerate(blocks_of(core)):
+                own = grad_kv_ref[kind, pair, tile_rows(block * BLOCK, BLOCK), :]
+                halves.append(own + other_ref[kind, pair, slot * BLOCK : (slot + 1) * BLOCK, :].astype(jnp.float32))
+            parts.append(jnp.concatenate(halves, axis=0).astype(jnp.bfloat16))
+        grads = jnp.concatenate(parts, axis=1)
+        term = dot(normed_t_ref[...], grads).astype(jnp.bfloat16)
+        for part in range(PARTS):
+            grads_ref[part, pair] = term[part * 128 : (part + 1) * 128, :]
+        sum_ref[...] += dot(grads, weight_ref[pair], BOTH_LAST)
+        return carry
+
+    lax.fori_loop(0, PAIRS, pair_step, 0)
+
+    def norm_rows(index, carry):
+        rows = tile_rows(index * 128, 128)
+        grads = sum_ref[rows, :]
+        units, inverse = standard(x_ref[rows, :].astype(jnp.float32))
+        grad_x_ref[rows, :] = grad_hidden_ref[rows, :] + standard_back(grads, gain, units, inverse)
+        vec_grad_ref[0:1, :] += column_sum(grads * units)
+        vec_grad_ref[1:2, :] += column_sum(grads)
+        return carry
+
+    lax.fori_loop(0, OWN // 128, norm_rows, 0)
+
+
+def greet(partners):
+    barrier = pltpu.get_barrier_semaphore()
+    for partner in partners:
+        pl.semaphore_signal(barrier, inc=1, device_id=partner, device_id_type=MESH)
+    pl.semaphore_wait(barrier, len(partners))
+
+
+def along_tensor(step):
+    core, rep, part = place()
+    return (core, rep, lax.rem(part + step, PARTS))
+
+
+def along_dp(step):
+    core, rep, part = place()
+    return (core, lax.bitwise_xor(rep, step), part)
+
+
+def sibling():
+    core, rep, part = place()
+    return (1 - core, rep, part)
+
+
+def all_partners():
+    return [along_tensor(step) for step in (1, 2, 3)] + [along_dp(step) for step in (1, 2, 3)] + [sibling()]
+
+
+def remote(source, target, send, receive, device):
+    return pltpu.make_async_remote_copy(src_ref=source, dst_ref=target, send_sem=send, recv_sem=receive, device_id=device, device_id_type=MESH)
+
+
+def gather_kernel(tokens, cotangent, qkv, out, up, down, vec, x_ref, dy_ref, qkv_all, out_all, up_all, down_all, vec_all, tok_send, tok_recv, z_send, z_recv, xy_send, xy_recv, sib_send, sib_recv, local):
+    core, rep, part = place()
+    greet(all_partners())
+    owner = jnp.where((part == 0) | (part == 3), 0, 1)
+    slot = jnp.where(part < 2, 0, 1)
+    shards = (qkv, out, up, down, vec)
+    wholes = (qkv_all, out_all, up_all, down_all, vec_all)
+
+    def row_copies(array, source, target, batch):
+        there = remote(source.at[batch], target.at[slot], tok_send.at[array, batch], tok_recv.at[array, slot], (core, rep, batch))
+        here = pltpu.make_async_copy(source.at[batch], target.at[slot], tok_send.at[array, batch])
+        return there, here
+
+    def each_row_copy(act):
+        for array, (source, target) in enumerate(((tokens, x_ref), (cotangent, dy_ref))):
+            for batch in range(PARTS):
+                there, here = row_copies(array, source, target, batch)
+
+                @pl.when((core == owner) & (part != batch))
+                def _():
+                    if act == "start":
+                        there.start()
+                    else:
+                        there.wait_send()
+
+                @pl.when((core == owner) & (part == batch))
+                def _():
+                    if act == "start":
+                        here.start()
+                    else:
+                        here.wait()
+
+    each_row_copy("start")
+
+    def quarter(index, which):
+        count = shards[index].shape[0] // PARTS
+        return pl.ds(pl.multiple_of(which * count, count), count)
+
+    z_copies = []
+    for index in range(5):
+        own = pltpu.make_async_copy(shards[index], wholes[index].at[core, part], local.at[index])
+        own.start()
+        row = []
+        for step in (1, 2, 3):
+            if index < 4:
+                rows = quarter(index, rep)
+                copy = remote(shards[index].at[rows], wholes[index].at[core, part, rows], z_send.at[index, step - 1], z_recv.at[index, step - 1], along_tensor(step))
+            else:
+                copy = remote(shards[index], wholes[index].at[core, part], z_send.at[index, step - 1], z_recv.at[index, step - 1], along_tensor(step))
+            copy.start()
+            row.append(copy)
+        z_copies.append(row)
+    xy_copies = []
+    for index in range(5):
+        pltpu.make_async_copy(shards[index], wholes[index].at[core, part], local.at[index]).wait()
+        for copy in z_copies[index]:
+            copy.wait_recv()
+        row = []
+        if index < 4:
+            rows = quarter(index, rep)
+            for step in (1, 2, 3):
+                for far in (1, 2, 3):
+                    other = lax.rem(part + far, PARTS)
+                    view = wholes[index].at[core, other, rows]
+                    copy = remote(view, view, xy_send.at[index, step - 1, far - 1], xy_recv.at[index, step - 1, far - 1], along_dp(step))
+                    copy.start()
+                    row.append(copy)
+        xy_copies.append(row)
+    sib_copies = []
+    for index in range(5):
+        for copy in xy_copies[index]:
+            copy.wait_recv()
+        view = wholes[index].at[core]
+        copy = remote(view, view, sib_send.at[index], sib_recv.at[index], sibling())
+        copy.start()
+        sib_copies.append(copy)
+    for array, (source, target) in enumerate(((tokens, x_ref), (cotangent, dy_ref))):
+        for place_of, block in enumerate(blocks_of(core)):
+
+            @pl.when(block != part)
+            def _():
+                remote(source.at[0], target.at[place_of], tok_send.at[array, 0], tok_recv.at[array, place_of], sibling()).wait_recv()
+
+    each_row_copy("wait")
+    for row in z_copies:
+        for copy in row:
+            copy.wait_send()
+    for row in xy_copies:
+        for copy in row:
+            copy.wait_send()
+    for copy in sib_copies:
+        copy.wait_send()
+        copy.wait_recv()
+
+
+def exchange_kernel(own_ref, all_ref, send, receive, local):
+    core = lax.axis_index("section")
+    greet([sibling()])
+    copies = []
+    for slot, block in enumerate(blocks_of(core)):
+        source = own_ref.at[:, :, slot * BLOCK : (slot + 1) * BLOCK, :]
+        target = all_ref.at[:, :, tile_rows(block * BLOCK, BLOCK), :]
+        copies.append(remote(source, target, send.at[slot], receive.at[slot], sibling()))
+        copies.append(pltpu.make_async_copy(source, target, local.at[slot]))
+    for copy in copies:
+        copy.start()
+    for copy in copies:
+        copy.wait()
+
+
+def return_kernel(all_ref, got_ref, send, receive):
+    core = lax.axis_index("section")
+    greet([sibling()])
+    copies = []
+    for slot, block in enumerate(blocks_of(1 - core)):
+        source = all_ref.at[:, :, tile_rows(block * BLOCK, BLOCK), :]
+        target = got_ref.at[:, :, slot * BLOCK : (slot + 1) * BLOCK, :]
+        copies.append(remote(source, target, send.at[slot], receive.at[slot], sibling()))
+    for copy in copies:
+        copy.start()
+    for copy in copies:
+        copy.wait()
+
+
+GRAD_COLUMNS = ((0, 1152), (1152, 1536))
+
+
+def reduce_kernel(early_one, early_two, late_one, late_two, vec_ref, out_ref, vec_out_ref, got_core, chip, got_dp, part_sum, got_part, final, vec_core, vec_chip, vec_dp, vec_rep, vec_part, core_send, core_recv, dp_send, dp_recv, part_send, part_recv, vec_send, vec_recv, last_send, last_recv):
+    core, rep, part = place()
+    greet(all_partners())
+    grads = ((early_one, late_one), (early_two, late_two))
+    mine, theirs = tile_rows(core * 64, 64), tile_rows((1 - core) * 64, 64)
+    vec_copy = remote(vec_ref.at[1 - core], vec_core, vec_send.at[0], vec_recv.at[0], sibling())
+    vec_copy.start()
+    copies = {}
+    for layer in (1, 0):
+        for kind, (first, last) in enumerate(GRAD_COLUMNS):
+            copy = remote(grads[layer][kind].at[:, :, theirs, :], got_core.at[layer, :, :, :, first:last], core_send.at[layer, kind], core_recv.at[layer, kind], sibling())
+            copy.start()
+            copies["core", layer, kind] = copy
+    for layer in (1, 0):
+        for kind, (first, last) in enumerate(GRAD_COLUMNS):
+            copies["core", layer, kind].wait_recv()
+
+            def add_core(index, carry):
+                major, minor = index // PARTS, lax.rem(index, PARTS)
+                own = grads[layer][kind][major, minor, mine, :].astype(jnp.float32)
+                total = own + got_core[layer, major, minor, :, first:last].astype(jnp.float32)
+                chip[layer, major, minor, :, first:last] = total.astype(jnp.bfloat16)
+                return carry
+
+            lax.fori_loop(0, PARTS * PARTS, add_core, 0)
+        for step in (1, 2, 3):
+            copy = remote(chip.at[layer, lax.bitwise_xor(rep, step)], got_dp.at[layer, step - 1], dp_send.at[layer, step - 1], dp_recv.at[layer, step - 1], along_dp(step))
+            copy.start()
+            copies["dp", layer, step] = copy
+    vec_copy.wait()
+    vec_chip[...] = vec_ref[core] + vec_core[...]
+    vec_copies = [remote(vec_chip, vec_dp.at[step - 1], vec_send.at[step], vec_recv.at[step], along_dp(step)) for step in (1, 2, 3)]
+    for copy in vec_copies:
+        copy.start()
+    for layer in (1, 0):
+        for step in (1, 2, 3):
+            copies["dp", layer, step].wait_recv()
+        for minor in range(PARTS):
+            total = chip[layer, rep, minor].astype(jnp.float32)
+            for step in (1, 2, 3):
+                total = total + got_dp[layer, step - 1, minor].astype(jnp.float32)
+            part_sum[layer, minor] = total.astype(jnp.bfloat16)
+        for step in (1, 2, 3):
+            copy = remote(part_sum.at[layer, lax.rem(part + step, PARTS)], got_part.at[layer, step - 1], part_send.at[layer, step - 1], part_recv.at[layer, step - 1], along_tensor(step))
+            copy.start()
+            copies["part", layer, step] = copy
+    for copy in vec_copies:
+        copy.wait()
+    vec_rep[...] = vec_chip[...] + vec_dp[0] + vec_dp[1] + vec_dp[2]
+    vec_copies = [remote(vec_rep, vec_part.at[step - 1], vec_send.at[3 + step], vec_recv.at[3 + step], along_tensor(step)) for step in (1, 2, 3)]
+    for copy in vec_copies:
+        copy.start()
+    for layer in (1, 0):
+        for step in (1, 2, 3):
+            copies["part", layer, step].wait_recv()
+        total = part_sum[layer, part].astype(jnp.float32)
+        for step in (1, 2, 3):
+            total = total + got_part[layer, step - 1].astype(jnp.float32)
+        final[layer] = total
+    last_copy = remote(final.at[1 - core], out_ref.at[mine], last_send, last_recv, sibling())
+    last_copy.start()
+    out_ref[mine, :] = final[core]
+    for copy in vec_copies:
+        copy.wait()
+    vec_out_ref[...] = vec_rep[...] + vec_part[0] + vec_part[1] + vec_part[2]
+    for copy in copies.values():
+        copy.wait_send()
+    last_copy.wait()
+
+
+def deliver_kernel(first_y, second_y, second_grad, first_grad, y_ref, grad_ref, send, receive):
+    core, rep, part = place()
+    greet([along_tensor(step) for step in (1, 2, 3)] + [(1 - core, rep, lax.rem(part + step, PARTS)) for step in range(4)])
+    sources = ((first_y, second_y), (first_grad, second_grad))
+    targets = (y_ref, grad_ref)
+
+    def each(act):
+        for kind in range(2):
+            for layer in range(2):
+                for slot, block in enumerate(blocks_of(core)):
+                    source = sources[kind][layer].at[slot * BLOCK : (slot + 1) * BLOCK]
+                    target = targets[kind].at[part]
+                    semaphore = send.at[kind, layer, slot]
+                    stays = (core == layer) & (block == part)
+
+                    @pl.when(stays)
+                    def _():
+                        copy = pltpu.make_async_copy(source, target, semaphore)
+                        copy.start() if act == "start" else copy.wait()
+
+                    @pl.when(jnp.logical_not(stays))
+                    def _():
+                        copy = remote(source, target, semaphore, receive.at[kind, part], (layer, rep, block))
+                        copy.start() if act == "start" else copy.wait_send()
+
+    each("start")
+    owner = jnp.where((part == 0) | (part == 3), 0, 1)
+    for kind in range(2):
+        for batch in range(PARTS):
+
+            @pl.when((core != owner) | (part != batch))
+            def _():
+                remote(sources[kind][0].at[:BLOCK], targets[kind].at[batch], send.at[kind, 0, 0], receive.at[kind, batch], sibling()).wait_recv()
+
+    each("wait")
+
+
+def call(body, name, ins, outs, scratch=(), collective=None, space=pltpu.VMEM):
+    dma = pltpu.SemaphoreType.DMA
+    shapes = [dma(item) if isinstance(item, tuple) else item for item in scratch]
+    params = dict(vmem_limit_bytes=56 * 2**20)
+    if collective is not None:
+        params.update(collective_id=collective, has_side_effects=True)
+    return pl.pallas_call(
+        body,
+        out_shape=[jax.ShapeDtypeStruct(shape, kind) for shape, kind in outs],
+        in_specs=[pl.BlockSpec(memory_space=space)] * len(ins),
+        out_specs=[pl.BlockSpec(memory_space=space)] * len(outs),
+        scratch_shapes=shapes,
+        compiler_params=pltpu.CompilerParams(**params),
+        name=name,
+    )(*ins)
+
+
+def mask_terms(lens, core):
+    bounds = jnp.cumsum(lens)
+    first = core == 0
+    slots = jnp.where(first, jnp.array([0, 1, 1, 1, 1]), jnp.array([0, 0, 1, 1, 1]))
+    keys = jnp.where(first, jnp.array([0, 0, 1, 2, 3]), jnp.array([0, 1, 0, 1, 2]))
+    blocks = jnp.where(slots == 0, core, 3 - core)
+    places = jnp.arange(BLOCK, dtype=jnp.int32)
+    query = blocks[:, None] * BLOCK + places[None, :]
+    key = keys[:, None] * BLOCK + places[None, :]
+    starts = jnp.max(jnp.where(bounds[None, None, :] <= query[:, :, None], bounds[None, None, :], 0), axis=-1)
+    straight = (key[:, None, :] >= starts[:, :, None]) & (key[:, None, :] <= query[:, :, None])
+    turned = (key[:, :, None] >= starts[:, None, :]) & (key[:, :, None] <= query[:, None, :])
+    return jnp.where(straight, 0.0, NEGATIVE), jnp.where(turned, 0.0, NEGATIVE)
+
+
+def on_device_whole(
+    tokens,
+    lengths,
+    cotangent,
+    ln_one_gain,
+    ln_one_bias,
+    qkv_weight,
+    out_weight,
+    out_bias,
+    ln_two_gain,
+    ln_two_bias,
+    up_weight,
+    up_bias,
+    down_weight,
+    down_bias,
+):
+    f32, low = jnp.float32, jnp.bfloat16
+    vmem = pltpu.VMEM
+    core, rep, part = place()
+    vec = jnp.concatenate([ln_one_gain, ln_one_bias, out_bias, ln_two_gain, ln_two_bias, down_bias, up_bias, jnp.zeros_like(up_bias)])
+    lens = lax.dynamic_index_in_dim(lengths, part, 0, keepdims=False)
+    bias, bias_turned = mask_terms(lens, core)
+    x_rows, dy_rows, qkv_all, out_all, up_all, down_all, vec_all = call(
+        gather_kernel,
+        "gather",
+        (tokens, cotangent, qkv_weight.reshape(WIDTH, 384), out_weight[0], up_weight[0], down_weight[0], vec),
+        (
+            ((2, BLOCK, WIDTH), low),
+            ((2, BLOCK, WIDTH), low),
+            ((2, PARTS, 512, 384), low),
+            ((2, PARTS, 128, 512), low),
+            ((2, PARTS, 512, 512), low),
+            ((2, PARTS, 512, 512), low),
+            ((2, PARTS, 8, 512), f32),
+        ),
+        ((2, 4), (2, 2), (5, 3), (5, 3), (4, 3, 3), (4, 3, 3), (5,), (5,), (5,)),
+        collective=0,
+        space=pl.ANY,
+    )
+    inputs = x_rows.reshape(OWN, WIDTH)
+    saved, produced = [], []
+    for layer in range(2):
+        signed = layer == 0
+        qkv, out, up, down, vecs = qkv_all[layer], out_all[layer], up_all[layer], down_all[layer], vec_all[layer]
+        normed_one_t, queries, kv = call(
+            project,
+            f"project{layer}",
+            (inputs, vecs, qkv),
+            (((WIDTH, OWN), low), ((PAIRS, 2, OWN, 128), low), ((2, PAIRS, OWN, 128), low)),
+            (vmem((OWN, WIDTH), low),),
+        )
+        (kv_all,) = call(
+            exchange_kernel, f"exchange{layer}", (kv,), (((2, PAIRS, 1024, 128), low),), ((2,), (2,), (2,)), collective=1 + layer, space=pl.ANY
+        )
+        attended, attended_t, logs = call(
+            partial(attend_rows, signed),
+            f"attend{layer}",
+            (queries, kv_all, bias),
+            (((PAIRS, OWN, 128), f32), ((PAIRS, 128, OWN), low), ((2, 8, BLOCK), f32)),
+            (vmem((TASKS, BLOCK, BLOCK), f32), vmem((TASKS, BLOCK, BLOCK), f32), vmem((2, BLOCK, 128), f32)),
+        )
+        hidden, normed_two_t, act, slope, y = call(
+            feed,
+            f"feed{layer}",
+            (inputs, attended, vecs, out, up, down),
+            (((OWN, WIDTH), f32), ((WIDTH, OWN), low), ((PARTS, OWN, 512), low), ((PARTS, OWN, 512), low), ((OWN, WIDTH), low)),
+            (vmem((OWN, WIDTH), low), vmem((OWN, 512), f32), vmem((OWN, WIDTH), f32)),
+        )
+        saved.append((inputs, normed_one_t, queries, kv_all, attended, attended_t, logs, hidden, normed_two_t, act, slope))
+        produced.append(y)
+        inputs = y
+    dy = dy_rows.reshape(OWN, WIDTH).astype(f32)
+    early, late, vec_grads, input_grads = [None, None], [None, None], [None, None], [None, None]
+    for layer in (1, 0):
+        signed = layer == 0
+        qkv, out, up, down, vecs = qkv_all[layer], out_all[layer], up_all[layer], down_all[layer], vec_all[layer]
+        inputs, normed_one_t, queries, kv_all, attended, attended_t, logs, hidden, normed_two_t, act, slope = saved[layer]
+        grad_hidden, grad_att, centres, early[layer], vec_one = call(
+            feed_back,
+            f"feed_back{layer}",
+            (dy, act, slope, down, up, hidden, normed_two_t, vecs, out, attended, attended_t),
+            (((OWN, WIDTH), f32), ((PAIRS, 2, OWN, 128), low), ((PAIRS, 8, OWN), f32), ((PARTS, PARTS, 128, 1152), low), ((16, 512), f32)),
+            (vmem((OWN, WIDTH), low), vmem((WIDTH, OWN), low), vmem((OWN, 512), low), vmem((OWN, WIDTH), f32)),
+        )
+        grad_query, grad_kv, grad_kv_low = call(
+            partial(attend_rows_back, signed),
+            f"attend_back{layer}",
+            (queries, kv_all, grad_att, bias_turned, logs, centres),
+            (((PAIRS, OWN, 128), low), ((2, PAIRS, 1024, 128), f32), ((2, PAIRS, 1024, 128), low)),
+        )
+        (other,) = call(
+            return_kernel, f"return{layer}", (grad_kv_low,), (((2, PAIRS, OWN, 128), low),), ((2,), (2,)), collective=3 + layer, space=pl.ANY
+        )
+        dy, late[layer], vec_two = call(
+            project_back,
+            f"project_back{layer}",
+            (grad_query, grad_kv, other, inputs, grad_hidden, normed_one_t, qkv, vecs),
+            (((OWN, WIDTH), f32), ((PARTS, PARTS, 128, 384), low), ((16, 512), f32)),
+            (vmem((OWN, WIDTH), f32),),
+        )
+        vec_grads[layer] = vec_one + vec_two
+        input_grads[layer] = dy.astype(low)
+    grads, vec_sum = call(
+        reduce_kernel,
+        "reduce",
+        (early[0], early[1], late[0], late[1], jnp.stack(vec_grads)),
+        (((128, 1536), f32), ((16, 512), f32)),
+        (
+            vmem((2, PARTS, PARTS, 64, 1536), low),
+            vmem((2, PARTS, PARTS, 64, 1536), low),
+            vmem((2, 3, PARTS, 64, 1536), low),
+            vmem((2, PARTS, 64, 1536), low),
+            vmem((2, 3, 64, 1536), low),
+            vmem((2, 64, 1536), f32),
+            vmem((16, 512), f32),
+            vmem((16, 512), f32),
+            vmem((3, 16, 512), f32),
+            vmem((16, 512), f32),
+            vmem((3, 16, 512), f32),
+            (2, 2),
+            (2, 2),
+            (2, 3),
+            (2, 3),
+            (2, 3),
+            (2, 3),
+            (7,),
+            (7,),
+            pltpu.SemaphoreType.DMA,
+            pltpu.SemaphoreType.DMA,
+        ),
+        collective=5,
+    )
+    block_outputs, grad_inputs = call(
+        deliver_kernel,
+        "deliver",
+        (produced[0], produced[1], input_grads[1], input_grads[0]),
+        (((PARTS, BLOCK, WIDTH), low), ((PARTS, BLOCK, WIDTH), low)),
+        ((2, 2, 2), (2, 4)),
+        collective=6,
+        space=pl.ANY,
+    )
+    spread = lax.dynamic_slice_in_dim(vec_sum, (rep * PARTS + part) * 32, 32, 1)
+    up_bias_grad = lax.dynamic_slice(vec_sum, (6 + part, rep * 128), (1, 128))
+    return (
+        block_outputs[None],
+        grad_inputs.astype(f32)[None],
+        spread[0:1],
+        spread[1:2],
+        grads[:, 1152:].reshape(1, 128, 3, 128),
+        grads[None, :, 1024:1152],
+        spread[2:3],
+        spread[3:4],
+        spread[4:5],
+        grads[None, :, 512:1024],
+        up_bias_grad[None],
+        grads[:, :512].T[None],
+        spread[5:6],
+    )
+
+
 def solution(mesh):
     return jax.shard_map(
-        on_device,
+        on_device_whole if whole_batch_fits(mesh) else on_device,
         mesh=mesh,
         in_specs=(
             P("dp", "tensor", None),

time: 2140 us -> 518 us (0.24)
  waiting for transfers between devices: 1440 us -> 0 us
  Pallas kernels: 0 us -> 481 us
  matrix products: 307 us -> 0 us
  local copies, waits for them, and re-layouts: 155 us -> 24.8 us
  other arithmetic: 123 us -> 11.1 us
  between operations: 43.4 us -> 0.89 us
  blocking collectives: 39.1 us -> 0 us
    all_gather x23 -> x0, waiting for transfers between devices: 549 us -> none  [the longest x10 223 us: forward_layer(): lax.all_gather(values, 'tensor', axis=0, tiled=True)]
    unnamed x58 -> x0, waiting for transfers between devices: 519 us -> none
    pallas_call x0 -> x19, Pallas kernels: none -> 481 us  [call(): pl.pallas_call(body, out_shape=[jax.ShapeDtypeStruct(shape, kind) for sha...]
    reduce_scatter x15 -> x0, waiting for transfers between devices: 368 us -> none  [the longest x5 161 us: backward_layer(): lax.psum_scatter(grad_values.astype(jnp.bfloat16), 'tensor', scatter_dime...]
    dot_general x120 -> x0, matrix products: 307 us -> none  [the longest x10 54 us: accumulate(): jnp.einsum('hqk,khe->qhe', weights, value_rows, preferred_element_type=jn...]
    unnamed x772 -> x32, local copies, waits for them, and re-layouts: 79.8 us -> 3.86 us
    reduce_sum x85 -> x0, other arithmetic: 60 us -> none  [the longest x10 23.5 us: measure(): jnp.sum(jnp.where(allowed, jnp.exp(masked - new_max[:, :, None]), 0.0), a...]
    slice x49 -> x3, local copies, waits for them, and re-layouts: 33.9 us -> 2.57 us  [the longest x1 1.51 us: on_device_whole(): spread[5:6]]
  transfers between devices with their start and end apart: 56 -> 0, of which waited for: 49 -> 0; matrix products, arithmetic and copies ran while one was open for 15% -> 0% of each run, Pallas kernels for 0% -> 0%
where the time goes in v1:
time: 518 us
  Pallas kernels  481 us (93%)
  local copies, waits for them, and re-layouts  24.8 us (5%)
  other arithmetic  11.1 us (2%)
    pallas_call x19, Pallas kernels, call(): pl.pallas_call(body, out_shape=[jax.ShapeDtypeStruct(shape, kind) for sha...  481 us

profile of v1, /device:TPU:0, one launch (start us, length us, event | category | flops | bytes accessed | tf_op | source)
XLA Modules:
  0.0 517.9 jit_solution(5455687263670261587)
XLA Ops:
  0.6 0.0 copy-start
  0.7 1.2 copy.39
  1.8 0.9 copy.40.qkv
  2.8 1.4 concatenate.3.vec
  4.2 105.4 %gather.1 = (bf16[2,256,512]{2,1,0:T(8,128)(2,1)}, bf16[2,256,512]{2,1,0:T(8,128)(2,1)}, bf16[2,4,512,384]{3,2,1,0:T(8,128)(2,1)}, bf16[2,4,128,512]{3,2,1,0:T(8...) custom-call(bf16[4,256,512]{2,1,0:T(8,128)(2,1)} %tokens.1, ...), custom_call_target="tpu_custom_call" | custom-call | tf_op jit(solution)/shard_map/gather/pallas_call | solution.py:1159
  109.6 1.5 slice_bitcast_fusion.11
  111.1 3.9 slice_bitcast_fusion.4
  115.0 5.7 %project0.1 = (bf16[512,512]{1,0:T(8,128)(2,1)}, bf16[4,2,512,128]{3,2,1,0:T(8,128)(2,1)}, bf16[2,4,512,128]{3,2,1,0:T(8,128)(2,1)}) custom-call(bf16[512,512]{1,0:T(8,128)(2,1)} %bitcast.50, f32[4,8,512]{2,1,0:T(8,128)} %get-tuple-element.173.vec_ref, bf16[4,512,384]{2,1,0:T(8,128)(2,1)} %get-tuple-element.167.weight_ref), custom_call_target="tpu_custom_call" | custom-call | tf_op jit(solution)/shard_map/project0/pallas_call | solution.py:1159
  120.7 33.1 %exchange0.1.kv_ref = bf16[2,4,1024,128]{3,2,1,0:T(8,128)(2,1)} custom-call(bf16[2,4,512,128]{3,2,1,0:T(8,128)(2,1)} %get-tuple-element.72.own_ref), custom_call_target="tpu_custom_call" | custom-call | tf_op jit(solution)/shard_map/exchange0/pallas_call | solution.py:1159
  153.8 0.0 copy-done.10
  153.9 0.0 copy-done.11
  153.9 0.0 copy-done.12
  153.9 0.0 copy-done.13
  153.9 0.1 iota_add_fusion
  154.0 0.0 copy-done
  154.0 0.2 reduce-window.8
  154.2 0.1 select_reduce_fusion
  154.3 0.1 iota_add_fusion.1
  154.3 1.8 and_select_fusion
  156.2 11.2 %attend0.1 = (f32[4,512,128]{2,1,0:T(8,128)}, bf16[4,128,512]{2,1,0:T(8,128)(2,1)}, f32[2,8,256]{2,1,0:T(8,128)}) custom-call(bf16[4,2,512,128]{3,2,1,0:T(8,128)(2,1)} %get-tuple-element.71.query_ref, bf16[2,4,1024,128]{3,2,1,0:T(8,128)(2,1)} %exchange0.1.kv_ref, f32[5,256,256]{2,1,0:T(8,128)} %get-tuple-element.181.bias_ref), custom_call_target="tpu_custom_call" | custom-call | tf_op jit(solution)/shard_map/attend0/pallas_call | solution.py:1159
  167.3 0.0 copy-done.4
  167.3 1.1 slice_bitcast_fusion.6
  168.4 0.0 copy-done.2
  168.4 5.0 slice_bitcast_fusion
  173.4 13.5 %feed0.1 = (f32[512,512]{1,0:T(8,128)}, bf16[512,512]{1,0:T(8,128)(2,1)}, bf16[4,512,512]{2,1,0:T(8,128)(2,1)}, bf16[4,512,512]{2,1,0:T(8,128)(2,1)}, bf16[512,512]{1,0:T(8,128)(2,1)}) custom-call(bf16[512,512]{1,0:T(8,128)(2,1)} %bitcast.51, f32[4,512,128]{2,1,0:T(8,128)} %get-tuple-element.73.attended_ref, f32[4,8,512]{2,1,0:T(8,128)} %get-tuple-element.173.vec_ref, ...), custom_call_target="tpu_custom_call" | custom-call | tf_op jit(solution)/shard_map/feed0/pallas_call | solution.py:1159
  186.9 5.7 %project1.1 = (bf16[512,512]{1,0:T(8,128)(2,1)}, bf16[4,2,512,128]{3,2,1,0:T(8,128)(2,1)}, bf16[2,4,512,128]{3,2,1,0:T(8,128)(2,1)}) custom-call(bf16[512,512]{1,0:T(8,128)(2,1)} %get-tuple-element.77.x_ref.first_y, f32[4,8,512]{2,1,0:T(8,128)} %get-tuple-element.172.vec_ref, bf16[4,512,384]{2,1,0:T(8,128)(2,1)} %get-tuple-element.166.weight_ref), custom_call_target="tpu_custom_call" | custom-call | tf_op jit(solution)/shard_map/project1/pallas_call | solution.py:1159
  192.6 33.3 %exchange1.1.kv_ref = bf16[2,4,1024,128]{3,2,1,0:T(8,128)(2,1)} custom-call(bf16[2,4,512,128]{3,2,1,0:T(8,128)(2,1)} %get-tuple-element.79.own_ref), custom_call_target="tpu_custom_call" | custom-call | tf_op jit(solution)/shard_map/exchange1/pallas_call | solution.py:1159
  225.9 9.5 %attend1.1 = (f32[4,512,128]{2,1,0:T(8,128)}, bf16[4,128,512]{2,1,0:T(8,128)(2,1)}, f32[2,8,256]{2,1,0:T(8,128)}) custom-call(bf16[4,2,512,128]{3,2,1,0:T(8,128)(2,1)} %get-tuple-element.78.query_ref, bf16[2,4,1024,128]{3,2,1,0:T(8,128)(2,1)} %exchange1.1.kv_ref, f32[5,256,256]{2,1,0:T(8,128)} %get-tuple-element.181.bias_ref), custom_call_target="tpu_custom_call" | custom-call | tf_op jit(solution)/shard_map/attend1/pallas_call | solution.py:1159
  235.4 13.5 %feed1.1 = (f32[512,512]{1,0:T(8,128)}, bf16[512,512]{1,0:T(8,128)(2,1)}, bf16[4,512,512]{2,1,0:T(8,128)(2,1)}, bf16[4,512,512]{2,1,0:T(8,128)(2,1)}, bf16[512,512]{1,0:T(8,128)(2,1)}) custom-call(bf16[512,512]{1,0:T(8,128)(2,1)} %get-tuple-element.77.x_ref.first_y, f32[4,512,128]{2,1,0:T(8,128)} %get-tuple-element.80.attended_ref, ...), custom_call_target="tpu_custom_call" | custom-call | tf_op jit(solution)/shard_map/feed1/pallas_call | solution.py:1159
  248.9 0.0 copy-done.5
  248.9 1.2 bitcast_convert_fusion.1.dy_ref
  250.1 17.3 %feed_back1.1 = (f32[512,512]{1,0:T(8,128)}, bf16[4,2,512,128]{3,2,1,0:T(8,128)(2,1)}, f32[4,8,512]{2,1,0:T(8,128)}, bf16[4,4,128,1152]{3,2,1,0:T(8,128)(2,1)}, f32[16,512]{1,0:T(8,128)}) custom-call(f32[512,512]{1,0:T(8,128)} %bitcast_convert_fusion.1.dy_ref, bf16[4,512,512]{2,1,0:T(8,128)(2,1)} %get-tuple-element.83.act_ref, ...), custom_call_target="tpu_custom_call" | custom-call | tf_op jit(solution)/shard_map/feed_back1/pallas_call | solution.py:1159
  267.4 19.8 %attend_back1.1 = (bf16[4,512,128]{2,1,0:T(8,128)(2,1)}, f32[2,4,1024,128]{3,2,1,0:T(8,128)}, bf16[2,4,1024,128]{3,2,1,0:T(8,128)(2,1)}) custom-call(bf16[4,2,512,128]{3,2,1,0:T(8,128)(2,1)} %get-tuple-element.78.query_ref, bf16[2,4,1024,128]{3,2,1,0:T(8,128)(2,1)} %exchange1.1.kv_ref, bf16[4,2,512,128]{3,2,1,0:T(8,128)(2,1)} %get-tuple-element.88.grad_att_ref, ...), custom_call_target="tpu_custom_call" | custom-call | tf_op jit(solution)/shard_map/attend_back1/pallas_call | solution.py:1159
  287.2 3.0 return1.1.other_ref
  290.2 9.2 %project_back1.1 = (f32[512,512]{1,0:T(8,128)}, bf16[4,4,128,384]{3,2,1,0:T(8,128)(2,1)}, f32[16,512]{1,0:T(8,128)}) custom-call(bf16[4,512,128]{2,1,0:T(8,128)(2,1)} %get-tuple-element.91.grad_query_ref, f32[2,4,1024,128]{3,2,1,0:T(8,128)} %get-tuple-element.92.grad_kv_ref, bf16[2,4,512,128]{3,2,1,0:T(8,128)(2,1)} %return1.1.other_ref, ...), custom_call_target="tpu_custom_call" | custom-call | tf_op jit(solution)/shard_map/project_back1/pallas_call | solution.py:1159
  299.4 2.1 convert_element_type.14.second_grad
  301.5 17.4 %feed_back0.1 = (f32[512,512]{1,0:T(8,128)}, bf16[4,2,512,128]{3,2,1,0:T(8,128)(2,1)}, f32[4,8,512]{2,1,0:T(8,128)}, bf16[4,4,128,1152]{3,2,1,0:T(8,128)(2,1)}, f32[16,512]{1,0:T(8,128)}) custom-call(f32[512,512]{1,0:T(8,128)} %get-tuple-element.96.dy_ref, bf16[4,512,512]{2,1,0:T(8,128)(2,1)} %get-tuple-element.97.act_ref, ...), custom_call_target="tpu_custom_call" | custom-call | tf_op jit(solution)/shard_map/feed_back0/pallas_call | solution.py:1159
  318.9 19.8 %attend_back0.1 = (bf16[4,512,128]{2,1,0:T(8,128)(2,1)}, f32[2,4,1024,128]{3,2,1,0:T(8,128)}, bf16[2,4,1024,128]{3,2,1,0:T(8,128)(2,1)}) custom-call(bf16[4,2,512,128]{3,2,1,0:T(8,128)(2,1)} %get-tuple-element.71.query_ref, bf16[2,4,1024,128]{3,2,1,0:T(8,128)(2,1)} %exchange0.1.kv_ref, bf16[4,2,512,128]{3,2,1,0:T(8,128)(2,1)} %get-tuple-element.102.grad_att_ref, ...), custom_call_target="tpu_custom_call" | custom-call | tf_op jit(solution)/shard_map/attend_back0/pallas_call | solution.py:1159
  338.7 3.0 return0.1.other_ref
  341.8 9.2 %project_back0.1 = (f32[512,512]{1,0:T(8,128)}, bf16[4,4,128,384]{3,2,1,0:T(8,128)(2,1)}, f32[16,512]{1,0:T(8,128)}) custom-call(bf16[4,512,128]{2,1,0:T(8,128)(2,1)} %get-tuple-element.105.grad_query_ref, f32[2,4,1024,128]{3,2,1,0:T(8,128)} %get-tuple-element.106.grad_kv_ref, bf16[2,4,512,128]{3,2,1,0:T(8,128)(2,1)} %return0.1.other_ref, ...), custom_call_target="tpu_custom_call" | custom-call | tf_op jit(solution)/shard_map/project_back0/pallas_call | solution.py:1159
  350.9 2.1 convert_element_type.15.first_grad
  353.0 44.2 %deliver.1 = (bf16[4,256,512]{2,1,0:T(8,128)(2,1)}, bf16[4,256,512]{2,1,0:T(8,128)(2,1)}) custom-call(bf16[512,512]{1,0:T(8,128)(2,1)} %get-tuple-element.77.x_ref.first_y, bf16[512,512]{1,0:T(8,128)(2,1)} %get-tuple-element.81.second_y, bf16[512,512]{1,0:T(8,128)(2,1)} %convert_element_type.14.second_grad, bf16[512,512]{1,0:T(8,128)(2,1)} %convert_element_type.15.first_grad), custom_call_target="tpu_custom_call" | custom-call | tf_op jit(solution)/shard_map/deliver/pallas_call | solution.py:1159
  397.2 0.0 copy-start.6
  397.2 0.0 copy-start.7
  397.2 0.0 copy-start.8
  397.2 0.0 copy-start.9
  397.3 2.9 bitcast_convert_fusion
  400.1 0.0 copy-done.6
  400.1 0.0 copy-done.7
  400.1 0.0 copy-done.8
  400.1 0.0 copy-done.9
  400.2 0.6 pad_maximum_fusion.vec_ref
  400.8 107.4 %reduce.1 = (f32[128,1536]{1,0:T(8,128)}, f32[16,512]{1,0:T(8,128)}) custom-call(bf16[4,4,128,1152]{3,2,1,0:T(8,128)(2,1)} %get-tuple-element.113.early_one, bf16[4,4,128,1152]{3,2,1,0:T(8,128)(2,1)} %get-tuple-element.114.early_two, bf16[4,4,128,384]{3,2,1,0:T(8,128)(2,1)} %get-tuple-element.115.late_one, ...), custom_call_target="tpu_custom_call" | custom-call | tf_op jit(solution)/shard_map/reduce/pallas_call | solution.py:1159
  508.2 0.0 copy-start.3
  508.2 1.5 fusion.2
  509.7 0.9 slice.82
  510.7 0.1 copy.41
  510.8 0.0 copy-start.1
  510.8 0.8 copy.42
  511.6 1.5 slice_bitcast_fusion.10
  513.1 1.8 slice_bitcast_fusion.8
  514.8 1.3 dynamic-slice_bitcast_fusion
  516.1 0.8 copy.43
  516.9 1.0 copy.45
  (14 shorter events, 0.0 us)
Async XLA Ops:
  0.6 153.3 %copy-start = (s32[4,8]{1,0:T(4,128)S(1)}, s32[4,8]{1,0:T(4,128)}, u32[]{:S(2)}) copy-start(s32[4,8]{1,0:T(4,128)} %param.19) | copy-start | bytes 388
  120.7 33.1 %copy-start.10 = (s32[5]{0:T(128)S(1)}, s32[5]{0:T(128)}, u32[]{:S(2)}) copy-start(s32[5]{0:T(128)} %constant.57.clone) | copy-start | bytes 64
  120.7 33.1 %copy-start.11 = (s32[5]{0:T(128)S(1)}, s32[5]{0:T(128)}, u32[]{:S(2)}) copy-start(s32[5]{0:T(128)} %constant.58.clone) | copy-start | bytes 64
  120.7 33.1 %copy-start.12 = (s32[5]{0:T(128)S(1)}, s32[5]{0:T(128)}, u32[]{:S(2)}) copy-start(s32[5]{0:T(128)} %constant.55.clone) | copy-start | bytes 64
  120.7 33.1 %copy-start.13 = (s32[5]{0:T(128)S(1)}, s32[5]{0:T(128)}, u32[]{:S(2)}) copy-start(s32[5]{0:T(128)} %constant.56.clone) | copy-start | bytes 64
  154.3 13.0 %copy-start.4 = (bf16[2,4,128,512]{3,2,1,0:T(8,128)(2,1)S(1)}, bf16[2,4,128,512]{3,2,1,0:T(8,128)(2,1)}, u32[]{:S(2)}) copy-start(bf16[2,4,128,512]{3,2,1,0:T(8,128)(2,1)} %get-tuple-element.74) | copy-start | bytes 3145732
  156.2 12.3 %copy-start.2 = (bf16[2,4,512,512]{3,2,1,0:T(8,128)(2,1)S(1)}, bf16[2,4,512,512]{3,2,1,0:T(8,128)(2,1)}, u32[]{:S(2)}) copy-start(bf16[2,4,512,512]{3,2,1,0:T(8,128)(2,1)} %get-tuple-element.75) | copy-start | bytes 12582916
  235.4 13.5 %copy-start.5 = (bf16[2,256,512]{2,1,0:T(8,128)(2,1)S(1)}, bf16[2,256,512]{2,1,0:T(8,128)(2,1)}, u32[]{:S(2)}) copy-start(bf16[2,256,512]{2,1,0:T(8,128)(2,1)} %get-tuple-element.82) | copy-start | bytes 1572868
  397.2 2.9 copy-start.6
  397.2 2.9 copy-start.7
  397.2 2.9 copy-start.8
  397.2 2.9 copy-start.9
  508.2 8.8 %copy-start.3 = (bf16[4,256,512]{2,1,0:T(8,128)(2,1)S(1)}, bf16[4,256,512]{2,1,0:T(8,128)(2,1)}, u32[]{:S(2)}) copy-start(bf16[4,256,512]{2,1,0:T(8,128)(2,1)} %get-tuple-element.111) | copy-start | bytes 3145732
  510.8 7.1 %copy-start.1 = (s32[4,8]{1,0:T(4,128)S(1)}, s32[4,8]{1,0:T(4,128)}, u32[]{:S(2)}) copy-start(s32[4,8]{1,0:T(4,128)} %param.19) | copy-start | bytes 388

commit v2 on v1

--- a/solution.py
+++ b/solution.py
@@ -606,7 +606,8 @@
     return jnp.where((lane < HEAD) == (parity == 0), values, 0.0)
 
 
-def project(x_ref, vec_ref, weight_ref, normed_t_ref, query_ref, kv_ref, normed_ref):
+def project(x_ref, vec_ref, weight_ref, normed_t_ref, query_ref, kv_ref, normed_ref, between, after_pair):
+    core = lax.axis_index("section")
     gain, bias = vec_ref[0, 0:1, :], vec_ref[0, 1:2, :]
 
     def norm_rows(index, carry):
@@ -617,14 +618,18 @@
 
     lax.fori_loop(0, OWN // 128, norm_rows, 0)
     normed_t_ref[...] = normed_ref[...].T
+    between()
 
     def pair_step(pair, carry):
         out = dot(normed_ref[...], weight_ref[pair])
         queries = out[:, :128] * 0.125
         for parity in range(2):
             query_ref[pair, parity] = keep_head(queries, parity).astype(jnp.bfloat16)
-        kv_ref[0, pair] = out[:, 128:256].astype(jnp.bfloat16)
-        kv_ref[1, pair] = out[:, 256:].astype(jnp.bfloat16)
+        for slot, block in enumerate(blocks_of(core)):
+            part = out[slot * BLOCK : (slot + 1) * BLOCK, :]
+            kv_ref[0, pair, tile_rows(block * BLOCK, BLOCK), :] = part[:, 128:256].astype(jnp.bfloat16)
+            kv_ref[1, pair, tile_rows(block * BLOCK, BLOCK), :] = part[:, 256:].astype(jnp.bfloat16)
+        after_pair(pair)
         return carry
 
     lax.fori_loop(0, PAIRS, pair_step, 0)
@@ -637,13 +642,14 @@
     return slots, keys
 
 
-def attend_rows(signed, query_ref, kv_ref, bias_ref, attended_ref, attended_t_ref, log_ref, logit_ref, factor_ref, stat_ref):
+def attend_rows(signed, query_ref, kv_ref, bias_ref, attended_ref, attended_t_ref, log_ref, logit_ref, factor_ref, stat_ref, before_pair):
     core = lax.axis_index("section")
     slots, keys = task_plan(core)
     middle_late = core == 0
     lane = lax.broadcasted_iota(jnp.int32, (BLOCK, 128), 1)
 
     def pair_step(pair, carry):
+        before_pair(pair)
         outs = [[None, None], [None, None]]
         for parity in range(2):
             tops = []
@@ -701,7 +707,7 @@
     return values * lower, lower + values * density
 
 
-def feed(x_ref, attended_ref, vec_ref, out_ref, up_ref, down_ref, hidden_ref, normed_t_ref, act_ref, slope_ref, y_ref, normed_ref, wide_ref, sum_ref):
+def feed(x_ref, attended_ref, vec_ref, out_ref, up_ref, down_ref, hidden_ref, normed_t_ref, act_ref, slope_ref, y_ref, normed_ref, wide_ref, sum_ref, between):
     out_bias = vec_ref[0, 2:3, :]
     gain, bias = vec_ref[0, 3:4, :], vec_ref[0, 4:5, :]
     down_bias = vec_ref[0, 5:6, :]
@@ -724,6 +730,7 @@
 
     lax.fori_loop(0, OWN // 128, norm_rows, 0)
     normed_t_ref[...] = normed_ref[...].T
+    between()
 
     def chunk_step(chunk, carry):
         wide_ref[...] = dot(normed_ref[...], up_ref[chunk])
@@ -799,7 +806,7 @@
     lax.fori_loop(0, PAIRS, pair_step, 0)
 
 
-def attend_rows_back(signed, query_ref, kv_ref, grad_att_ref, bias_ref, log_ref, centre_ref, grad_query_ref, grad_kv_ref, grad_kv_low_ref):
+def attend_rows_back(signed, query_ref, kv_ref, grad_att_ref, bias_ref, log_ref, centre_ref, grad_query_ref, grad_kv_ref, send_ref, before_pair, after_pair):
     core = lax.axis_index("section")
     slots, keys = task_plan(core)
     early = jnp.where(core == 0, 0.0, 1.0)
@@ -807,6 +814,7 @@
     grad_kv_ref[...] = jnp.zeros_like(grad_kv_ref)
 
     def pair_step(pair, carry):
+        before_pair(pair)
         parts = [[None] * TASKS, [None] * TASKS]
         for task in range(TASKS):
             rows = tile_rows(slots[task] * BLOCK, BLOCK)
@@ -844,20 +852,23 @@
             merged.append(jnp.where(lane < HEAD, parts[0][task], parts[1][task]))
         grad_query_ref[pair, :BLOCK, :] = ((merged[0] + merged[1] * early) * 0.125).astype(jnp.bfloat16)
         grad_query_ref[pair, BLOCK:, :] = ((merged[1] * (1.0 - early) + merged[2] + merged[3] + merged[4]) * 0.125).astype(jnp.bfloat16)
-        grad_kv_low_ref[0, pair] = grad_kv_ref[0, pair].astype(jnp.bfloat16)
-        grad_kv_low_ref[1, pair] = grad_kv_ref[1, pair].astype(jnp.bfloat16)
+        for slot, block in enumerate(blocks_of(1 - core)):
+            for kind in range(2):
+                rows = grad_kv_ref[kind, pair, tile_rows(block * BLOCK, BLOCK), :]
+                send_ref[kind, pair, slot * BLOCK : (slot + 1) * BLOCK, :] = rows.astype(jnp.bfloat16)
+        after_pair(pair)
         return carry
 
     lax.fori_loop(0, PAIRS, pair_step, 0)
 
 
-def project_back(grad_query_ref, grad_kv_ref, other_ref, x_ref, grad_hidden_ref, normed_t_ref, weight_ref, vec_ref, grad_x_ref, grads_ref, vec_grad_ref, sum_ref):
+def project_back(grad_query_ref, grad_kv_ref, other_ref, x_ref, grad_hidden_ref, normed_t_ref, weight_ref, vec_ref, grad_x_ref, grad_x_low_ref, grads_ref, vec_grad_ref, sum_ref, before_pair, after_pair, between):
     core = lax.axis_index("section")
     gain = vec_ref[0, 0:1, :]
     sum_ref[...] = jnp.zeros_like(sum_ref)
-    vec_grad_ref[...] = jnp.zeros_like(vec_grad_ref)
 
     def pair_step(pair, carry):
+        before_pair(pair)
         parts = [grad_query_ref[pair]]
         for kind in range(2):
             halves = []
@@ -868,17 +879,21 @@
         grads = jnp.concatenate(parts, axis=1)
         term = dot(normed_t_ref[...], grads).astype(jnp.bfloat16)
         for part in range(PARTS):
-            grads_ref[part, pair] = term[part * 128 : (part + 1) * 128, :]
+            grads_ref[part, pair, :, 1152:1536] = term[part * 128 : (part + 1) * 128, :]
+        after_pair(pair)
         sum_ref[...] += dot(grads, weight_ref[pair], BOTH_LAST)
         return carry
 
     lax.fori_loop(0, PAIRS, pair_step, 0)
+    between()
 
     def norm_rows(index, carry):
         rows = tile_rows(index * 128, 128)
         grads = sum_ref[rows, :]
         units, inverse = standard(x_ref[rows, :].astype(jnp.float32))
-        grad_x_ref[rows, :] = grad_hidden_ref[rows, :] + standard_back(grads, gain, units, inverse)
+        grad_x = grad_hidden_ref[rows, :] + standard_back(grads, gain, units, inverse)
+        grad_x_ref[rows, :] = grad_x
+        grad_x_low_ref[rows, :] = grad_x.astype(jnp.bfloat16)
         vec_grad_ref[0:1, :] += column_sum(grads * units)
         vec_grad_ref[1:2, :] += column_sum(grads)
         return carry
@@ -916,270 +931,474 @@
     return pltpu.make_async_remote_copy(src_ref=source, dst_ref=target, send_sem=send, recv_sem=receive, device_id=device, device_id_type=MESH)
 
 
-def gather_kernel(tokens, cotangent, qkv, out, up, down, vec, x_ref, dy_ref, qkv_all, out_all, up_all, down_all, vec_all, tok_send, tok_recv, z_send, z_recv, xy_send, xy_recv, sib_send, sib_recv, local):
+def fill_masks(lens_ref, bias_ref, turned):
+    core, rep, part = place()
+    slots, keys = task_plan(core)
+    bounds, bound = [], 0
+    for index in range(lens_ref.shape[1]):
+        bound = bound + lens_ref[part, index]
+        bounds.append(bound)
+    for task in range(TASKS):
+        block = jnp.where(slots[task] == 0, core, 3 - core)
+        shape = (1, BLOCK) if turned else (BLOCK, 1)
+        query = block * BLOCK + lax.broadcasted_iota(jnp.int32, shape, 1 if turned else 0)
+        start = jnp.zeros(shape, jnp.int32)
+        for bound in bounds:
+            start = jnp.where(query >= bound, bound, start)
+        key = keys[task] * BLOCK + lax.broadcasted_iota(jnp.int32, (BLOCK, BLOCK), 0 if turned else 1)
+        bias_ref[task] = jnp.where((key >= start) & (key <= query), 0.0, NEGATIVE)
+
+
+def quarter_rows(array, which):
+    count = array.shape[0] // PARTS
+    return tile_rows(which * count, count)
+
+
+SAVED = (
+    ((OWN, WIDTH), jnp.bfloat16),
+    ((WIDTH, OWN), jnp.bfloat16),
+    ((PAIRS, 2, OWN, 128), jnp.bfloat16),
+    ((2, PAIRS, 1024, 128), jnp.bfloat16),
+    ((PAIRS, OWN, 128), jnp.float32),
+    ((PAIRS, 128, OWN), jnp.bfloat16),
+    ((2, 8, BLOCK), jnp.float32),
+    ((OWN, WIDTH), jnp.float32),
+    ((WIDTH, OWN), jnp.bfloat16),
+    ((PARTS, OWN, 512), jnp.bfloat16),
+    ((PARTS, OWN, 512), jnp.bfloat16),
+)
+WEIGHTS = (
+    ((PARTS, 512, 384), jnp.bfloat16),
+    ((PARTS, 128, 512), jnp.bfloat16),
+    ((PARTS, 512, 512), jnp.bfloat16),
+    ((PARTS, 512, 512), jnp.bfloat16),
+    ((PARTS, 8, 512), jnp.float32),
+)
+QKV, OUT, UP, DOWN, VEC = range(5)
+
+
+def forward_kernel(lens_ref, tokens, cotangent, *refs):
+    shards, refs = refs[:5], refs[5:]
+    dy_out, y_out, saved_out, weights_out, refs = refs[0], refs[1], refs[2:13], refs[13:18], refs[18:]
+    saved, weights, refs = refs[:11], refs[11:16], refs[16:]
+    y_ref, bias_ref, normed, logit, factor, stat, wide, total, refs = *refs[:8], refs[8:]
+    row_send, row_recv, row_local, z_send, z_recv, xy_send, xy_recv, sib_send, sib_recv, local, kv_send, kv_recv, save_sem = refs
     core, rep, part = place()
     greet(all_partners())
+
+    def z_copy(index, step):
+        slot = (index, step - 1)
+        if index == VEC:
+            return remote(shards[index], weights[index].at[core, part], z_send.at[slot], z_recv.at[slot], along_tensor(step))
+        rows = quarter_rows(shards[index], rep)
+        return remote(shards[index].at[rows], weights[index].at[core, part, rows], z_send.at[slot], z_recv.at[slot], along_tensor(step))
+
+    def own_copy(index):
+        return pltpu.make_async_copy(shards[index], weights[index].at[core, part], local.at[index])
+
+    def xy_copy(index, step, far):
+        slot = (index, step - 1, far - 1)
+        view = weights[index].at[core, lax.rem(part + far, PARTS), quarter_rows(shards[index], rep)]
+        return remote(view, view, xy_send.at[slot], xy_recv.at[slot], along_dp(step))
+
+    def sib_copy(index):
+        view = weights[index].at[core]
+        return remote(view, view, sib_send.at[index], sib_recv.at[index], sibling())
+
+    steps = (1, 2, 3)
+
+    def z_start(*which):
+        for index in which:
+            own_copy(index).start()
+            for step in steps:
+                z_copy(index, step).start()
+
+    def xy_start(*which):
+        for index in which:
+            for step in steps:
+                z_copy(index, step).wait_recv()
+            for step in steps:
+                for far in steps:
+                    xy_copy(index, step, far).start()
+
+    def sib_start(*which):
+        for index in which:
+            own_copy(index).wait()
+            for step in steps:
+                for far in steps:
+                    xy_copy(index, step, far).wait_recv()
+            sib_copy(index).start()
+
+    def need(layer, *which):
+        @pl.when(core != layer)
+        def _():
+            for index in which:
+                sib_copy(index).wait_recv()
+
     owner = jnp.where((part == 0) | (part == 3), 0, 1)
-    slot = jnp.where(part < 2, 0, 1)
-    shards = (qkv, out, up, down, vec)
-    wholes = (qkv_all, out_all, up_all, down_all, vec_all)
-
-    def row_copies(array, source, target, batch):
-        there = remote(source.at[batch], target.at[slot], tok_send.at[array, batch], tok_recv.at[array, slot], (core, rep, batch))
-        here = pltpu.make_async_copy(source.at[batch], target.at[slot], tok_send.at[array, batch])
+    place_here = jnp.where(part < 2, 0, 1)
+    row_pairs = ((tokens, saved[0].at[0]), (cotangent, dy_out))
+
+    def row_targets(array, batch):
+        source, target = row_pairs[array]
+        rows = target.at[tile_rows(place_here * BLOCK, BLOCK)]
+        there = remote(source.at[batch], rows, row_send.at[array, batch], row_recv.at[array, place_here], (core, rep, batch))
+        here = pltpu.make_async_copy(source.at[batch], rows, row_local.at[array])
         return there, here
 
-    def each_row_copy(act):
-        for array, (source, target) in enumerate(((tokens, x_ref), (cotangent, dy_ref))):
-            for batch in range(PARTS):
-                there, here = row_copies(array, source, target, batch)
-
-                @pl.when((core == owner) & (part != batch))
-                def _():
-                    if act == "start":
-                        there.start()
-                    else:
-                        there.wait_send()
-
-                @pl.when((core == owner) & (part == batch))
-                def _():
-                    if act == "start":
-                        here.start()
-                    else:
-                        here.wait()
-
-    each_row_copy("start")
-
-    def quarter(index, which):
-        count = shards[index].shape[0] // PARTS
-        return pl.ds(pl.multiple_of(which * count, count), count)
-
-    z_copies = []
-    for index in range(5):
-        own = pltpu.make_async_copy(shards[index], wholes[index].at[core, part], local.at[index])
-        own.start()
-        row = []
-        for step in (1, 2, 3):
-            if index < 4:
-                rows = quarter(index, rep)
-                copy = remote(shards[index].at[rows], wholes[index].at[core, part, rows], z_send.at[index, step - 1], z_recv.at[index, step - 1], along_tensor(step))
-            else:
-                copy = remote(shards[index], wholes[index].at[core, part], z_send.at[index, step - 1], z_recv.at[index, step - 1], along_tensor(step))
-            copy.start()
-            row.append(copy)
-        z_copies.append(row)
-    xy_copies = []
-    for index in range(5):
-        pltpu.make_async_copy(shards[index], wholes[index].at[core, part], local.at[index]).wait()
-        for copy in z_copies[index]:
-            copy.wait_recv()
-        row = []
-        if index < 4:
-            rows = quarter(index, rep)
-            for step in (1, 2, 3):
-                for far in (1, 2, 3):
-                    other = lax.rem(part + far, PARTS)
-                    view = wholes[index].at[core, other, rows]
-                    copy = remote(view, view, xy_send.at[index, step - 1, far - 1], xy_recv.at[index, step - 1, far - 1], along_dp(step))
-                    copy.start()
-                    row.append(copy)
-        xy_copies.append(row)
-    sib_copies = []
-    for index in range(5):
-        for copy in xy_copies[index]:
-            copy.wait_recv()
-        view = wholes[index].at[core]
-        copy = remote(view, view, sib_send.at[index], sib_recv.at[index], sibling())
-        copy.start()
-        sib_copies.append(copy)
-    for array, (source, target) in enumerate(((tokens, x_ref), (cotangent, dy_ref))):
-        for place_of, block in enumerate(blocks_of(core)):
+    def rows_each(array, act):
+        for batch in range(PARTS):
+            there, here = row_targets(array, batch)
+
+            @pl.when((core == owner) & (part != batch))
+            def _():
+                there.start() if act == "start" else there.wait_send()
+
+            @pl.when((core == owner) & (part == batch))
+            def _():
+                here.start() if act == "start" else here.wait()
+
+    def rows_arrived(array):
+        for slot, block in enumerate(blocks_of(core)):
 
             @pl.when(block != part)
             def _():
-                remote(source.at[0], target.at[place_of], tok_send.at[array, 0], tok_recv.at[array, place_of], sibling()).wait_recv()
-
-    each_row_copy("wait")
-    for row in z_copies:
-        for copy in row:
-            copy.wait_send()
-    for row in xy_copies:
-        for copy in row:
-            copy.wait_send()
-    for copy in sib_copies:
-        copy.wait_send()
-        copy.wait_recv()
-
-
-def exchange_kernel(own_ref, all_ref, send, receive, local):
-    core = lax.axis_index("section")
-    greet([sibling()])
-    copies = []
-    for slot, block in enumerate(blocks_of(core)):
-        source = own_ref.at[:, :, slot * BLOCK : (slot + 1) * BLOCK, :]
-        target = all_ref.at[:, :, tile_rows(block * BLOCK, BLOCK), :]
-        copies.append(remote(source, target, send.at[slot], receive.at[slot], sibling()))
-        copies.append(pltpu.make_async_copy(source, target, local.at[slot]))
-    for copy in copies:
+                source, target = row_pairs[array]
+                rows = target.at[slot * BLOCK : (slot + 1) * BLOCK]
+                remote(source.at[0], rows, row_send.at[array, 0], row_recv.at[array, slot], sibling()).wait_recv()
+
+    def save(layer, *which):
+        for index in which:
+            pltpu.make_async_copy(saved[index].at[layer], saved_out[index].at[layer], save_sem.at[layer, index]).start()
+
+    def kv_copies(layer, pair, receiving):
+        copies = []
+        for slot, block in enumerate(blocks_of(1 - core if receiving else core)):
+            view = saved[3].at[layer, :, pair, tile_rows(block * BLOCK, BLOCK), :]
+            copies.append(remote(view, view, kv_send.at[layer, pair, slot], kv_recv.at[layer, pair, slot], sibling()))
+        return copies
+
+    def on(layer, action, *which):
+        @pl.when(core == layer)
+        def _():
+            action(*which)
+
+    on(0, z_start, QKV)
+    for step in steps:
+        z_copy(VEC, step).start()
+    own_copy(VEC).start()
+    rows_each(0, "start")
+    on(0, z_start, OUT, UP, DOWN)
+    fill_masks(lens_ref, bias_ref, False)
+    on(0, xy_start, QKV)
+    own_copy(VEC).wait()
+    for step in steps:
+        z_copy(VEC, step).wait_recv()
+    sib_copy(VEC).start()
+    rows_each(0, "wait")
+    rows_arrived(0)
+    sib_copy(VEC).wait_recv()
+    for layer in range(2):
+        signed = layer == 0
+        held = [item.at[layer] for item in saved]
+        qkv, out, up, down, vec = [item.at[layer] for item in weights]
+        x_ref, normed_one_t, queries, kv, attended, attended_t, logs, hidden, normed_two_t, act, slope = held
+
+        def before_project():
+            on(layer, sib_start, QKV)
+            need(layer, QKV)
+            if layer == 1:
+                rows_each(1, "start")
+
+        def push_kv(pair):
+            for copy in kv_copies(layer, pair, False):
+                copy.start()
+
+        def before_attend(pair):
+            for copy in kv_copies(layer, pair, True):
+                copy.wait_recv()
+            if layer == 0:
+
+                @pl.when((pair == 2) & (core == 0))
+                def _():
+                    sib_start(OUT)
+
+                @pl.when((pair == 2) & (core == 1))
+                def _():
+                    xy_start(QKV)
+
+            else:
+
+                @pl.when((pair == 2) & (core == 1))
+                def _():
+                    sib_start(UP, DOWN)
+
+        project(x_ref, vec, qkv, normed_one_t, queries, kv, normed, before_project, push_kv)
+        save(layer, 0, 1, 2)
+        if layer == 0:
+            on(0, xy_start, OUT, UP, DOWN)
+            on(1, z_start, QKV, OUT, UP, DOWN)
+        else:
+            on(1, sib_start, OUT)
+        attend_rows(signed, queries, kv, bias_ref, attended, attended_t, logs, logit, factor, stat, before_attend)
+        save(layer, 3, 4, 5, 6)
+        if layer == 0:
+            on(0, sib_start, UP, DOWN)
+            on(1, xy_start, OUT, UP, DOWN)
+        need(layer, OUT)
+
+        def before_feed():
+            need(layer, UP, DOWN)
+
+        target = saved[0].at[1] if layer == 0 else y_ref
+        feed(x_ref, attended, vec, out, up, down, hidden, normed_two_t, act, slope, target, normed, wide, total, before_feed)
+        save(layer, 7, 8, 9, 10)
+    y_copy = pltpu.make_async_copy(y_ref, y_out, row_local.at[0])
+    y_copy.start()
+    weight_copies = [pltpu.make_async_copy(weights[index], weights_out[index], local.at[index]) for index in range(5)]
+    for copy in weight_copies:
         copy.start()
-    for copy in copies:
+    rows_each(1, "wait")
+    rows_arrived(1)
+    for index in range(5):
+        for step in steps:
+            z_copy(index, step).wait_send()
+            if index != VEC:
+                for far in steps:
+                    xy_copy(index, step, far).wait_send()
+        sib_copy(index).wait_send()
+    for layer in range(2):
+        for pair in range(PAIRS):
+            for copy in kv_copies(layer, pair, False):
+                copy.wait_send()
+        for index in range(11):
+            pltpu.make_async_copy(saved[index].at[layer], saved_out[index].at[layer], save_sem.at[layer, index]).wait()
+    y_copy.wait()
+    for copy in weight_copies:
         copy.wait()
 
 
-def return_kernel(all_ref, got_ref, send, receive):
-    core = lax.axis_index("section")
-    greet([sibling()])
-    copies = []
-    for slot, block in enumerate(blocks_of(1 - core)):
-        source = all_ref.at[:, :, tile_rows(block * BLOCK, BLOCK), :]
-        target = got_ref.at[:, :, slot * BLOCK : (slot + 1) * BLOCK, :]
-        copies.append(remote(source, target, send.at[slot], receive.at[slot], sibling()))
-    for copy in copies:
-        copy.start()
-    for copy in copies:
-        copy.wait()
-
-
-GRAD_COLUMNS = ((0, 1152), (1152, 1536))
-
-
-def reduce_kernel(early_one, early_two, late_one, late_two, vec_ref, out_ref, vec_out_ref, got_core, chip, got_dp, part_sum, got_part, final, vec_core, vec_chip, vec_dp, vec_rep, vec_part, core_send, core_recv, dp_send, dp_recv, part_send, part_recv, vec_send, vec_recv, last_send, last_recv):
+GROUPS = ((0, 1152), (1152, 1536))
+
+
+def backward_kernel(lens_ref, dy_in, y_in, *refs):
+    saved_in, weights_in, refs = refs[:11], refs[11:16], refs[16:]
+    grads_out, vec_out, blocks_out, rows_out, refs = *refs[:4], refs[4:]
+    held, weights, refs = refs[:11], refs[11:16], refs[16:]
+    dy_low, dy_ref, bias_ref, grads_ref, vec_grad, low, low_t, chunk, total, grad_hidden, grad_att, centres, grad_query, grad_kv, kv_out, kv_got, grad_low, refs = *refs[:17], refs[17:]
+    got_core, got_dp, part_sum, got_part, final, vec_core, vec_chip, vec_dp, vec_rep, vec_part, refs = *refs[:10], refs[10:]
+    load_sem, weight_sem, dy_sem, y_send, y_recv, row_send, row_recv, kv_send, kv_recv, core_send, core_recv, dp_send, dp_recv, part_send, part_recv, vec_send, vec_recv, last_send, last_recv = refs
     core, rep, part = place()
-    greet(all_partners())
-    grads = ((early_one, late_one), (early_two, late_two))
+    steps = (1, 2, 3)
     mine, theirs = tile_rows(core * 64, 64), tile_rows((1 - core) * 64, 64)
-    vec_copy = remote(vec_ref.at[1 - core], vec_core, vec_send.at[0], vec_recv.at[0], sibling())
-    vec_copy.start()
-    copies = {}
-    for layer in (1, 0):
-        for kind, (first, last) in enumerate(GRAD_COLUMNS):
-            copy = remote(grads[layer][kind].at[:, :, theirs, :], got_core.at[layer, :, :, :, first:last], core_send.at[layer, kind], core_recv.at[layer, kind], sibling())
+
+    def load(layer, which=(), matrices=()):
+        copies = [pltpu.make_async_copy(saved_in[index].at[layer], held[index], load_sem.at[index]) for index in which]
+        return copies + [pltpu.make_async_copy(weights_in[index].at[layer], weights[index], weight_sem.at[index]) for index in matrices]
+
+    def start(copies):
+        for copy in copies:
             copy.start()
-            copies["core", layer, kind] = copy
-    for layer in (1, 0):
-        for kind, (first, last) in enumerate(GRAD_COLUMNS):
-            copies["core", layer, kind].wait_recv()
-
-            def add_core(index, carry):
-                major, minor = index // PARTS, lax.rem(index, PARTS)
-                own = grads[layer][kind][major, minor, mine, :].astype(jnp.float32)
-                total = own + got_core[layer, major, minor, :, first:last].astype(jnp.float32)
-                chip[layer, major, minor, :, first:last] = total.astype(jnp.bfloat16)
-                return carry
-
-            lax.fori_loop(0, PARTS * PARTS, add_core, 0)
-        for step in (1, 2, 3):
-            copy = remote(chip.at[layer, lax.bitwise_xor(rep, step)], got_dp.at[layer, step - 1], dp_send.at[layer, step - 1], dp_recv.at[layer, step - 1], along_dp(step))
-            copy.start()
-            copies["dp", layer, step] = copy
-    vec_copy.wait()
-    vec_chip[...] = vec_ref[core] + vec_core[...]
-    vec_copies = [remote(vec_chip, vec_dp.at[step - 1], vec_send.at[step], vec_recv.at[step], along_dp(step)) for step in (1, 2, 3)]
-    for copy in vec_copies:
-        copy.start()
-    for layer in (1, 0):
-        for step in (1, 2, 3):
-            copies["dp", layer, step].wait_recv()
-        for minor in range(PARTS):
-            total = chip[layer, rep, minor].astype(jnp.float32)
-            for step in (1, 2, 3):
-                total = total + got_dp[layer, step - 1, minor].astype(jnp.float32)
-            part_sum[layer, minor] = total.astype(jnp.bfloat16)
-        for step in (1, 2, 3):
-            copy = remote(part_sum.at[layer, lax.rem(part + step, PARTS)], got_part.at[layer, step - 1], part_send.at[layer, step - 1], part_recv.at[layer, step - 1], along_tensor(step))
-            copy.start()
-            copies["part", layer, step] = copy
-    for copy in vec_copies:
-        copy.wait()
-    vec_rep[...] = vec_chip[...] + vec_dp[0] + vec_dp[1] + vec_dp[2]
-    vec_copies = [remote(vec_rep, vec_part.at[step - 1], vec_send.at[3 + step], vec_recv.at[3 + step], along_tensor(step)) for step in (1, 2, 3)]
-    for copy in vec_copies:
-        copy.start()
-    for layer in (1, 0):
-        for step in (1, 2, 3):
-            copies["part", layer, step].wait_recv()
-        total = part_sum[layer, part].astype(jnp.float32)
-        for step in (1, 2, 3):
-            total = total + got_part[layer, step - 1].astype(jnp.float32)
-        final[layer] = total
-    last_copy = remote(final.at[1 - core], out_ref.at[mine], last_send, last_recv, sibling())
-    last_copy.start()
-    out_ref[mine, :] = final[core]
-    for copy in vec_copies:
-        copy.wait()
-    vec_out_ref[...] = vec_rep[...] + vec_part[0] + vec_part[1] + vec_part[2]
-    for copy in copies.values():
-        copy.wait_send()
-    last_copy.wait()
-
-
-def deliver_kernel(first_y, second_y, second_grad, first_grad, y_ref, grad_ref, send, receive):
-    core, rep, part = place()
-    greet([along_tensor(step) for step in (1, 2, 3)] + [(1 - core, rep, lax.rem(part + step, PARTS)) for step in range(4)])
-    sources = ((first_y, second_y), (first_grad, second_grad))
-    targets = (y_ref, grad_ref)
-
-    def each(act):
-        for kind in range(2):
-            for layer in range(2):
-                for slot, block in enumerate(blocks_of(core)):
-                    source = sources[kind][layer].at[slot * BLOCK : (slot + 1) * BLOCK]
-                    target = targets[kind].at[part]
-                    semaphore = send.at[kind, layer, slot]
-                    stays = (core == layer) & (block == part)
-
-                    @pl.when(stays)
-                    def _():
-                        copy = pltpu.make_async_copy(source, target, semaphore)
-                        copy.start() if act == "start" else copy.wait()
-
-                    @pl.when(jnp.logical_not(stays))
-                    def _():
-                        copy = remote(source, target, semaphore, receive.at[kind, part], (layer, rep, block))
-                        copy.start() if act == "start" else copy.wait_send()
-
-    each("start")
+
+    def wait(copies):
+        for copy in copies:
+            copy.wait()
+
+    feed_set = ((9, 10, 7, 8, 4, 5), (DOWN, UP, VEC, OUT))
+    attend_set = ((2, 3, 6), ())
+    project_set = ((0, 1), (QKV,))
+    dy_copy = pltpu.make_async_copy(dy_in, dy_low, dy_sem.at[0])
+    dy_copy.start()
+    for group in (feed_set, attend_set, project_set):
+        start(load(1, *group))
+    greet(all_partners() + [(1 - core, rep, lax.rem(part + step, PARTS)) for step in steps])
+
     owner = jnp.where((part == 0) | (part == 3), 0, 1)
-    for kind in range(2):
+
+    def deliver(source, layer, target, send, receive, act):
+        for slot, block in enumerate(blocks_of(core)):
+            rows = source.at[slot * BLOCK : (slot + 1) * BLOCK]
+            stays = (core == layer) & (block == part)
+
+            @pl.when(stays)
+            def _():
+                copy = pltpu.make_async_copy(rows, target.at[part], send.at[layer, slot])
+                copy.start() if act == "start" else copy.wait()
+
+            @pl.when(jnp.logical_not(stays))
+            def _():
+                copy = remote(rows, target.at[part], send.at[layer, slot], receive.at[part], (layer, rep, block))
+                copy.start() if act == "start" else copy.wait_send()
+
+    def delivered(target, source, send, receive):
         for batch in range(PARTS):
 
             @pl.when((core != owner) | (part != batch))
             def _():
-                remote(sources[kind][0].at[:BLOCK], targets[kind].at[batch], send.at[kind, 0, 0], receive.at[kind, batch], sibling()).wait_recv()
-
-    each("wait")
-
-
-def call(body, name, ins, outs, scratch=(), collective=None, space=pltpu.VMEM):
+                remote(source.at[:BLOCK], target.at[batch], send.at[0, 0], receive.at[batch], sibling()).wait_recv()
+
+    deliver(saved_in[0].at[1], 0, blocks_out, y_send, y_recv, "start")
+    deliver(y_in, 1, blocks_out, y_send, y_recv, "start")
+
+    def core_copy(layer, group):
+        first, last = GROUPS[group]
+        return remote(grads_ref.at[:, :, theirs, first:last], got_core.at[layer, :, :, :, first:last], core_send.at[layer, group], core_recv.at[layer, group], sibling())
+
+    def dp_copy(layer, group, step):
+        first, last = GROUPS[group]
+        slot = (layer, group, step - 1)
+        return remote(got_core.at[layer, lax.bitwise_xor(rep, step), :, :, first:last], got_dp.at[layer, step - 1, :, :, first:last], dp_send.at[slot], dp_recv.at[slot], along_dp(step))
+
+    def part_copy(layer, group, step):
+        first, last = GROUPS[group]
+        slot = (layer, group, step - 1)
+        return remote(part_sum.at[layer, lax.rem(part + step, PARTS), :, first:last], got_part.at[layer, step - 1, :, first:last], part_send.at[slot], part_recv.at[slot], along_tensor(step))
+
+    def dp_start(layer, group):
+        first, last = GROUPS[group]
+        core_copy(layer, group).wait()
+
+        def add(index, carry):
+            major, minor = index // PARTS, lax.rem(index, PARTS)
+            own = grads_ref[major, minor, mine, first:last].astype(jnp.float32)
+            sum_here = own + got_core[layer, major, minor, :, first:last].astype(jnp.float32)
+            got_core[layer, major, minor, :, first:last] = sum_here.astype(jnp.bfloat16)
+            return carry
+
+        lax.fori_loop(0, PARTS * PARTS, add, 0)
+        start(dp_copy(layer, group, step) for step in steps)
+
+    def part_start(layer, group):
+        first, last = GROUPS[group]
+        for step in steps:
+            dp_copy(layer, group, step).wait()
+
+        def add(minor, carry):
+            sum_here = got_core[layer, rep, minor, :, first:last].astype(jnp.float32)
+            for step in steps:
+                sum_here = sum_here + got_dp[layer, step - 1, minor, :, first:last].astype(jnp.float32)
+            part_sum[layer, minor, :, first:last] = sum_here.astype(jnp.bfloat16)
+            return carry
+
+        lax.fori_loop(0, PARTS, add, 0)
+        start(part_copy(layer, group, step) for step in steps)
+
+    def finish(layer, group):
+        first, last = GROUPS[group]
+        for step in steps:
+            part_copy(layer, group, step).wait()
+        sum_here = part_sum[layer, part, :, first:last].astype(jnp.float32)
+        for step in steps:
+            sum_here = sum_here + got_part[layer, step - 1, :, first:last].astype(jnp.float32)
+        final[layer, :, first:last] = sum_here
+
+    def last_copy(layer):
+        return remote(final.at[layer], grads_out.at[mine], last_send.at[0], last_recv.at[0], sibling())
+
+    def hand_over(layer):
+        @pl.when(core == layer)
+        def _():
+            grads_out[mine, :] = final[layer]
+
+        @pl.when(core != layer)
+        def _():
+            last_copy(layer).start()
+
+    def kv_copy(layer, pair):
+        return remote(kv_out.at[:, pair], kv_got.at[layer, :, pair], kv_send.at[layer, pair], kv_recv.at[layer, pair], sibling())
+
+    fill_masks(lens_ref, bias_ref, True)
+    for layer in (1, 0):
+        signed = layer == 0
+        x_ref, normed_one_t, queries, kv, attended, attended_t, logs, hidden, normed_two_t, act, slope = held
+        qkv, out, up, down, vec = weights
+        if layer == 1:
+            dy_copy.wait()
+            dy_ref[...] = dy_low[...].astype(jnp.float32)
+        wait(load(layer, *feed_set))
+        feed_back(dy_ref, act, slope, down, up, hidden, normed_two_t, vec, out, attended, attended_t, grad_hidden, grad_att, centres, grads_ref, vec_grad.at[layer], low, low_t, chunk, total)
+        core_copy(layer, 0).start()
+        if layer == 1:
+            start(load(0, (9, 10, 7, 8, 4, 5), (DOWN, UP, OUT)))
+        else:
+            part_start(1, 0)
+            part_start(1, 1)
+        wait(load(layer, *attend_set))
+
+        def before_attend(pair):
+            @pl.when(pair == 2)
+            def _():
+                dp_start(layer, 0)
+                if layer == 0:
+                    finish(1, 0)
+                    finish(1, 1)
+                    hand_over(1)
+
+        def push_kv(pair):
+            kv_copy(layer, pair).start()
+
+        attend_rows_back(signed, queries, kv, grad_att, bias_ref, logs, centres, grad_query, grad_kv, kv_out, before_attend, push_kv)
+        if layer == 1:
+            start(load(0, *attend_set))
+        wait(load(layer, *project_set))
+
+        def before_project(pair):
+            kv_copy(layer, pair).wait()
+
+        def between():
+            core_copy(layer, 1).start()
+
+        project_back(grad_query, grad_kv, kv_got.at[layer], x_ref, grad_hidden, normed_one_t, qkv, vec, dy_ref, grad_low.at[layer], grads_ref, vec_grad.at[layer], total, before_project, lambda pair: None, between)
+        if layer == 1:
+            start(load(0, (0, 1), (QKV, VEC)))
+        deliver(grad_low.at[layer], layer, rows_out, row_send, row_recv, "start")
+        dp_start(layer, 1)
+    vec_copy = remote(vec_grad.at[1 - core], vec_core, vec_send.at[0], vec_recv.at[0], sibling())
+    vec_copy.start()
+    part_start(0, 0)
+    vec_copy.wait()
+    vec_chip[...] = vec_grad[core] + vec_core[...]
+    vec_copies = [remote(vec_chip, vec_dp.at[step - 1], vec_send.at[step], vec_recv.at[step], along_dp(step)) for step in steps]
+    start(vec_copies)
+    part_start(0, 1)
+    wait(vec_copies)
+    vec_rep[...] = vec_chip[...] + vec_dp[0] + vec_dp[1] + vec_dp[2]
+    vec_copies = [remote(vec_rep, vec_part.at[step - 1], vec_send.at[3 + step], vec_recv.at[3 + step], along_tensor(step)) for step in steps]
+    start(vec_copies)
+    finish(0, 0)
+    finish(0, 1)
+    hand_over(0)
+    wait(vec_copies)
+    vec_out[...] = vec_rep[...] + vec_part[0] + vec_part[1] + vec_part[2]
+    deliver(saved_in[0].at[1], 0, blocks_out, y_send, y_recv, "wait")
+    deliver(y_in, 1, blocks_out, y_send, y_recv, "wait")
+    delivered(blocks_out, y_in, y_send, y_recv)
+    for layer in range(2):
+        deliver(grad_low.at[layer], layer, rows_out, row_send, row_recv, "wait")
+    delivered(rows_out, grad_low.at[0], row_send, row_recv)
+    last_copy(0).wait_recv()
+    last_copy(0).wait_send()
+
+
+def specs(space, count):
+    return [pl.BlockSpec(memory_space=space)] * count
+
+
+def kernel_call(body, name, ins, in_specs, outs, out_specs, scratch, collective):
     dma = pltpu.SemaphoreType.DMA
-    shapes = [dma(item) if isinstance(item, tuple) else item for item in scratch]
-    params = dict(vmem_limit_bytes=56 * 2**20)
-    if collective is not None:
-        params.update(collective_id=collective, has_side_effects=True)
     return pl.pallas_call(
         body,
         out_shape=[jax.ShapeDtypeStruct(shape, kind) for shape, kind in outs],
-        in_specs=[pl.BlockSpec(memory_space=space)] * len(ins),
-        out_specs=[pl.BlockSpec(memory_space=space)] * len(outs),
-        scratch_shapes=shapes,
-        compiler_params=pltpu.CompilerParams(**params),
+        in_specs=in_specs,
+        out_specs=out_specs,
+        scratch_shapes=[pltpu.VMEM(*item) if len(item) == 2 and isinstance(item[0], tuple) else dma(item) for item in scratch],
+        compiler_params=pltpu.CompilerParams(collective_id=collective, has_side_effects=True, vmem_limit_bytes=60 * 2**20),
         name=name,
     )(*ins)
 
 
-def mask_terms(lens, core):
-    bounds = jnp.cumsum(lens)
-    first = core == 0
-    slots = jnp.where(first, jnp.array([0, 1, 1, 1, 1]), jnp.array([0, 0, 1, 1, 1]))
-    keys = jnp.where(first, jnp.array([0, 0, 1, 2, 3]), jnp.array([0, 1, 0, 1, 2]))
-    blocks = jnp.where(slots == 0, core, 3 - core)
-    places = jnp.arange(BLOCK, dtype=jnp.int32)
-    query = blocks[:, None] * BLOCK + places[None, :]
-    key = keys[:, None] * BLOCK + places[None, :]
-    starts = jnp.max(jnp.where(bounds[None, None, :] <= query[:, :, None], bounds[None, None, :], 0), axis=-1)
-    straight = (key[:, None, :] >= starts[:, :, None]) & (key[:, None, :] <= query[:, :, None])
-    turned = (key[:, :, None] >= starts[:, None, :]) & (key[:, :, None] <= query[:, None, :])
-    return jnp.where(straight, 0.0, NEGATIVE), jnp.where(turned, 0.0, NEGATIVE)
+def twice(items):
+    return tuple(((2, *shape), kind) for shape, kind in items)
 
 
 def on_device_whole(
@@ -1199,135 +1418,108 @@
     down_bias,
 ):
     f32, low = jnp.float32, jnp.bfloat16
-    vmem = pltpu.VMEM
     core, rep, part = place()
     vec = jnp.concatenate([ln_one_gain, ln_one_bias, out_bias, ln_two_gain, ln_two_bias, down_bias, up_bias, jnp.zeros_like(up_bias)])
-    lens = lax.dynamic_index_in_dim(lengths, part, 0, keepdims=False)
-    bias, bias_turned = mask_terms(lens, core)
-    x_rows, dy_rows, qkv_all, out_all, up_all, down_all, vec_all = call(
-        gather_kernel,
-        "gather",
-        (tokens, cotangent, qkv_weight.reshape(WIDTH, 384), out_weight[0], up_weight[0], down_weight[0], vec),
+    rows, rows_low = ((OWN, WIDTH), f32), ((OWN, WIDTH), low)
+    square = ((BLOCK, BLOCK), f32)
+    results = kernel_call(
+        forward_kernel,
+        "forward",
+        (lengths, tokens, cotangent, qkv_weight.reshape(WIDTH, 384), out_weight[0], up_weight[0], down_weight[0], vec),
+        specs(pltpu.SMEM, 1) + specs(pl.ANY, 7),
+        (rows_low, rows_low, *twice(SAVED), *twice(WEIGHTS)),
+        specs(pl.ANY, 18),
         (
-            ((2, BLOCK, WIDTH), low),
-            ((2, BLOCK, WIDTH), low),
-            ((2, PARTS, 512, 384), low),
-            ((2, PARTS, 128, 512), low),
-            ((2, PARTS, 512, 512), low),
-            ((2, PARTS, 512, 512), low),
-            ((2, PARTS, 8, 512), f32),
+            *twice(SAVED),
+            *twice(WEIGHTS),
+            rows_low,
+            ((TASKS, BLOCK, BLOCK), f32),
+            rows_low,
+            ((TASKS, BLOCK, BLOCK), f32),
+            ((TASKS, BLOCK, BLOCK), f32),
+            ((2, BLOCK, 128), f32),
+            rows,
+            rows,
+            (2, 4),
+            (2, 2),
+            (2,),
+            (5, 3),
+            (5, 3),
+            (4, 3, 3),
+            (4, 3, 3),
+            (5,),
+            (5,),
+            (5,),
+            (2, PAIRS, 2),
+            (2, PAIRS, 2),
+            (2, 11),
         ),
-        ((2, 4), (2, 2), (5, 3), (5, 3), (4, 3, 3), (4, 3, 3), (5,), (5,), (5,)),
-        collective=0,
-        space=pl.ANY,
-    )
-    inputs = x_rows.reshape(OWN, WIDTH)
-    saved, produced = [], []
-    for layer in range(2):
-        signed = layer == 0
-        qkv, out, up, down, vecs = qkv_all[layer], out_all[layer], up_all[layer], down_all[layer], vec_all[layer]
-        normed_one_t, queries, kv = call(
-            project,
-            f"project{layer}",
-            (inputs, vecs, qkv),
-            (((WIDTH, OWN), low), ((PAIRS, 2, OWN, 128), low), ((2, PAIRS, OWN, 128), low)),
-            (vmem((OWN, WIDTH), low),),
-        )
-        (kv_all,) = call(
-            exchange_kernel, f"exchange{layer}", (kv,), (((2, PAIRS, 1024, 128), low),), ((2,), (2,), (2,)), collective=1 + layer, space=pl.ANY
-        )
-        attended, attended_t, logs = call(
-            partial(attend_rows, signed),
-            f"attend{layer}",
-            (queries, kv_all, bias),
-            (((PAIRS, OWN, 128), f32), ((PAIRS, 128, OWN), low), ((2, 8, BLOCK), f32)),
-            (vmem((TASKS, BLOCK, BLOCK), f32), vmem((TASKS, BLOCK, BLOCK), f32), vmem((2, BLOCK, 128), f32)),
-        )
-        hidden, normed_two_t, act, slope, y = call(
-            feed,
-            f"feed{layer}",
-            (inputs, attended, vecs, out, up, down),
-            (((OWN, WIDTH), f32), ((WIDTH, OWN), low), ((PARTS, OWN, 512), low), ((PARTS, OWN, 512), low), ((OWN, WIDTH), low)),
-            (vmem((OWN, WIDTH), low), vmem((OWN, 512), f32), vmem((OWN, WIDTH), f32)),
-        )
-        saved.append((inputs, normed_one_t, queries, kv_all, attended, attended_t, logs, hidden, normed_two_t, act, slope))
-        produced.append(y)
-        inputs = y
-    dy = dy_rows.reshape(OWN, WIDTH).astype(f32)
-    early, late, vec_grads, input_grads = [None, None], [None, None], [None, None], [None, None]
-    for layer in (1, 0):
-        signed = layer == 0
-        qkv, out, up, down, vecs = qkv_all[layer], out_all[layer], up_all[layer], down_all[layer], vec_all[layer]
-        inputs, normed_one_t, queries, kv_all, attended, attended_t, logs, hidden, normed_two_t, act, slope = saved[layer]
-        grad_hidden, grad_att, centres, early[layer], vec_one = call(
-            feed_back,
-            f"feed_back{layer}",
-            (dy, act, slope, down, up, hidden, normed_two_t, vecs, out, attended, attended_t),
-            (((OWN, WIDTH), f32), ((PAIRS, 2, OWN, 128), low), ((PAIRS, 8, OWN), f32), ((PARTS, PARTS, 128, 1152), low), ((16, 512), f32)),
-            (vmem((OWN, WIDTH), low), vmem((WIDTH, OWN), low), vmem((OWN, 512), low), vmem((OWN, WIDTH), f32)),
-        )
-        grad_query, grad_kv, grad_kv_low = call(
-            partial(attend_rows_back, signed),
-            f"attend_back{layer}",
-            (queries, kv_all, grad_att, bias_turned, logs, centres),
-            (((PAIRS, OWN, 128), low), ((2, PAIRS, 1024, 128), f32), ((2, PAIRS, 1024, 128), low)),
-        )
-        (other,) = call(
-            return_kernel, f"return{layer}", (grad_kv_low,), (((2, PAIRS, OWN, 128), low),), ((2,), (2,)), collective=3 + layer, space=pl.ANY
-        )
-        dy, late[layer], vec_two = call(
-            project_back,
-            f"project_back{layer}",
-            (grad_query, grad_kv, other, inputs, grad_hidden, normed_one_t, qkv, vecs),
-            (((OWN, WIDTH), f32), ((PARTS, PARTS, 128, 384), low), ((16, 512), f32)),
-            (vmem((OWN, WIDTH), f32),),
-        )
-        vec_grads[layer] = vec_one + vec_two
-        input_grads[layer] = dy.astype(low)
-    grads, vec_sum = call(
-        reduce_kernel,
-        "reduce",
-        (early[0], early[1], late[0], late[1], jnp.stack(vec_grads)),
-        (((128, 1536), f32), ((16, 512), f32)),
+        0,
+    )
+    grads, vec_sum, block_outputs, grad_rows = kernel_call(
+        backward_kernel,
+        "backward",
+        (lengths, *results),
+        specs(pltpu.SMEM, 1) + specs(pl.ANY, 18),
+        (((128, 1536), f32), ((16, 512), f32), ((PARTS, BLOCK, WIDTH), low), ((PARTS, BLOCK, WIDTH), low)),
+        specs(pltpu.VMEM, 2) + specs(pl.ANY, 2),
         (
-            vmem((2, PARTS, PARTS, 64, 1536), low),
-            vmem((2, PARTS, PARTS, 64, 1536), low),
-            vmem((2, 3, PARTS, 64, 1536), low),
-            vmem((2, PARTS, 64, 1536), low),
-            vmem((2, 3, 64, 1536), low),
-            vmem((2, 64, 1536), f32),
-            vmem((16, 512), f32),
-            vmem((16, 512), f32),
-            vmem((3, 16, 512), f32),
-            vmem((16, 512), f32),
-            vmem((3, 16, 512), f32),
+            *SAVED,
+            *WEIGHTS,
+            rows_low,
+            rows,
+            ((TASKS, BLOCK, BLOCK), f32),
+            ((PARTS, PARTS, 128, 1536), low),
+            ((2, 16, 512), f32),
+            rows_low,
+            ((WIDTH, OWN), low),
+            ((OWN, 512), low),
+            rows,
+            rows,
+            ((PAIRS, 2, OWN, 128), low),
+            ((PAIRS, 8, OWN), f32),
+            ((PAIRS, OWN, 128), low),
+            ((2, PAIRS, 1024, 128), f32),
+            ((2, PAIRS, OWN, 128), low),
+            ((2, 2, PAIRS, OWN, 128), low),
+            ((2, OWN, WIDTH), low),
+            ((2, PARTS, PARTS, 64, 1536), low),
+            ((2, 3, PARTS, 64, 1536), low),
+            ((2, PARTS, 64, 1536), low),
+            ((2, 3, 64, 1536), low),
+            ((2, 64, 1536), f32),
+            ((16, 512), f32),
+            ((16, 512), f32),
+            ((3, 16, 512), f32),
+            ((16, 512), f32),
+            ((3, 16, 512), f32),
+            (11,),
+            (5,),
+            (1,),
+            (2, 2),
+            (PARTS,),
+            (2, 2),
+            (PARTS,),
+            (2, PAIRS),
+            (2, PAIRS),
             (2, 2),
             (2, 2),
-            (2, 3),
-            (2, 3),
-            (2, 3),
-            (2, 3),
+            (2, 2, 3),
+            (2, 2, 3),
+            (2, 2, 3),
+            (2, 2, 3),
             (7,),
             (7,),
-            pltpu.SemaphoreType.DMA,
-            pltpu.SemaphoreType.DMA,
+            (1,),
+            (1,),
         ),
-        collective=5,
-    )
-    block_outputs, grad_inputs = call(
-        deliver_kernel,
-        "deliver",
-        (produced[0], produced[1], input_grads[1], input_grads[0]),
-        (((PARTS, BLOCK, WIDTH), low), ((PARTS, BLOCK, WIDTH), low)),
-        ((2, 2, 2), (2, 4)),
-        collective=6,
-        space=pl.ANY,
+        1,
     )
     spread = lax.dynamic_slice_in_dim(vec_sum, (rep * PARTS + part) * 32, 32, 1)
     up_bias_grad = lax.dynamic_slice(vec_sum, (6 + part, rep * 128), (1, 128))
     return (
         block_outputs[None],
-        grad_inputs.astype(f32)[None],
+        grad_rows.astype(f32)[None],
         spread[0:1],
         spread[1:2],
         grads[:, 1152:].reshape(1, 128, 3, 128),

time: 518 us -> 234 us (0.45)
  Pallas kernels: 481 us -> 219 us
  local copies, waits for them, and re-layouts: 24.8 us -> 10.4 us
  other arithmetic: 11.1 us -> 2.96 us
    pallas_call x19 -> x2, Pallas kernels: 481 us -> 219 us  [kernel_call(): pl.pallas_call(body, out_shape=[jax.ShapeDtypeStruct(shape, kind) for sha...]
    squeeze x4 -> x0, local copies, waits for them, and re-layouts: 11.5 us -> none  [the longest x1 4.99 us: on_device_whole(): down_all[layer]]
    convert_element_type x3 -> x0, other arithmetic: 5.32 us -> none  [the longest x2 4.16 us: on_device_whole(): input_grads[layer] = dy.astype(low)]
where the time goes in v2:
time: 234 us; the launch traced here: 233 us
  Pallas kernels  219 us (94%)
  local copies, waits for them, and re-layouts  10.4 us (4%)
  other arithmetic  2.96 us (1%)
    pallas_call x2, Pallas kernels, kernel_call(): pl.pallas_call(body, out_shape=[jax.ShapeDtypeStruct(shape, kind) for sha...  219 us

profile of v2, /device:TPU:0, one launch (start us, length us, event | category | flops | bytes accessed | tf_op | source)
XLA Modules:
  0.0 233.4 jit_solution(362288895786322419)
XLA Ops:
  0.6 1.2 copy.30
  1.8 0.9 copy.31.refs_0_
  2.7 1.4 concatenate.3.refs_4_
  4.1 101.9 %forward.1 = (bf16[512,512]{1,0:T(8,128)(2,1)}, bf16[512,512]{1,0:T(8,128)(2,1)}, bf16[2,512,512]{2,1,0:T(8,128)(2,1)}, bf16[2,512,512]{2,1,0:T(8,128)(2,1)}, bf...) custom-call(s32[4,8]{1,0:T(4,128)} %lens_ref.3, ...), custom_call_target="tpu_custom_call" | custom-call | tf_op jit(solution)/shard_map/forward/pallas_call | solution.py:1389
  106.1 117.4 %backward.1 = (f32[128,1536]{1,0:T(8,128)}, f32[16,512]{1,0:T(8,128)}, bf16[4,256,512]{2,1,0:T(8,128)(2,1)}, bf16[4,256,512]{2,1,0:T(8,128)(2,1)}) custom-call(s32[4,8]{1,0:T(4,128)} %lens_ref.3, bf16[512,512]{1,0:T(8,128)(2,1)} %get-tuple-element.35.dy_in, bf16[512,512]{1,0:T(8,128)(2,1)} %get-tuple-element.36.y_in, ...), custom_call_target="tpu_custom_call" | custom-call | tf_op jit(solution)/shard_map/backward/pallas_call | solution.py:1389
  223.5 0.0 copy-start.1
  223.5 0.0 copy-start
  223.5 3.0 %bitcast_convert_fusion = f32[1,4,256,512]{3,2,1,0:T(8,128)} fusion(bf16[4,256,512]{2,1,0:T(8,128)(2,1)} %get-tuple-element.54), kind=kLoop, calls=%fused_computation | loop fusion | flops 524288 | bytes 3145728 | tf_op jit(solution)/shard_map/broadcast_in_dim | solution.py:1522
  226.5 0.0 copy-done.1
  226.5 0.7 slice_bitcast_fusion
  227.2 0.8 copy.34
  228.1 0.1 copy.32
  228.2 0.8 copy.33
  229.0 0.6 slice_bitcast_fusion.2
  229.7 1.5 fusion
  231.2 1.3 dynamic-slice_bitcast_fusion
  232.4 0.0 copy-done
  232.4 1.0 copy.36
  (2 shorter events, 0.0 us)
Async XLA Ops:
  223.5 3.0 %copy-start.1 = (f32[128,1536]{1,0:T(8,128)S(1)}, f32[128,1536]{1,0:T(8,128)}, u32[]{:S(2)}) copy-start(f32[128,1536]{1,0:T(8,128)} %get-tuple-element.56) | copy-start | bytes 2359300
  223.5 8.9 %copy-start = (bf16[4,256,512]{2,1,0:T(8,128)(2,1)S(1)}, bf16[4,256,512]{2,1,0:T(8,128)(2,1)}, u32[]{:S(2)}) copy-start(bf16[4,256,512]{2,1,0:T(8,128)(2,1)} %get-tuple-element.53) | copy-start | bytes 3145732

commit v3 on v2

--- a/solution.py
+++ b/solution.py
@@ -580,6 +580,10 @@
     return (core, 3 - core)
 
 
+def turn_part(turn):
+    return lax.rem(lax.axis_index("tensor") + turn, PARTS)
+
+
 def tile_rows(start, count):
     return pl.ds(pl.multiple_of(start, count), count)
 
@@ -606,7 +610,7 @@
     return jnp.where((lane < HEAD) == (parity == 0), values, 0.0)
 
 
-def project(x_ref, vec_ref, weight_ref, normed_t_ref, query_ref, kv_ref, normed_ref, between, after_pair):
+def project(x_ref, vec_ref, weight_ref, normed_t_ref, query_ref, kv_ref, normed_ref, between, before_pair, after_pair):
     core = lax.axis_index("section")
     gain, bias = vec_ref[0, 0:1, :], vec_ref[0, 1:2, :]
 
@@ -620,7 +624,9 @@
     normed_t_ref[...] = normed_ref[...].T
     between()
 
-    def pair_step(pair, carry):
+    def pair_step(turn, carry):
+        pair = turn_part(turn)
+        before_pair(turn)
         out = dot(normed_ref[...], weight_ref[pair])
         queries = out[:, :128] * 0.125
         for parity in range(2):
@@ -629,7 +635,7 @@
             part = out[slot * BLOCK : (slot + 1) * BLOCK, :]
             kv_ref[0, pair, tile_rows(block * BLOCK, BLOCK), :] = part[:, 128:256].astype(jnp.bfloat16)
             kv_ref[1, pair, tile_rows(block * BLOCK, BLOCK), :] = part[:, 256:].astype(jnp.bfloat16)
-        after_pair(pair)
+        after_pair(turn, pair)
         return carry
 
     lax.fori_loop(0, PAIRS, pair_step, 0)
@@ -648,8 +654,9 @@
     middle_late = core == 0
     lane = lax.broadcasted_iota(jnp.int32, (BLOCK, 128), 1)
 
-    def pair_step(pair, carry):
-        before_pair(pair)
+    def pair_step(turn, carry):
+        pair = turn_part(turn)
+        before_pair(turn, pair)
         outs = [[None, None], [None, None]]
         for parity in range(2):
             tops = []
@@ -707,13 +714,15 @@
     return values * lower, lower + values * density
 
 
-def feed(x_ref, attended_ref, vec_ref, out_ref, up_ref, down_ref, hidden_ref, normed_t_ref, act_ref, slope_ref, y_ref, normed_ref, wide_ref, sum_ref, between):
+def feed(x_ref, attended_ref, vec_ref, out_ref, up_ref, down_ref, hidden_ref, normed_t_ref, act_ref, slope_ref, y_ref, normed_ref, wide_ref, sum_ref, before_out, between, before_chunk, during_chunk):
     out_bias = vec_ref[0, 2:3, :]
     gain, bias = vec_ref[0, 3:4, :], vec_ref[0, 4:5, :]
     down_bias = vec_ref[0, 5:6, :]
     sum_ref[...] = jnp.zeros_like(sum_ref)
 
-    def out_step(pair, carry):
+    def out_step(turn, carry):
+        pair = turn_part(turn)
+        before_out(turn)
         sum_ref[...] += dot(attended_ref[pair].astype(jnp.bfloat16), out_ref[pair])
         return carry
 
@@ -732,7 +741,9 @@
     normed_t_ref[...] = normed_ref[...].T
     between()
 
-    def chunk_step(chunk, carry):
+    def chunk_step(turn, carry):
+        chunk = turn_part(turn)
+        before_chunk(turn)
         wide_ref[...] = dot(normed_ref[...], up_ref[chunk])
         up_bias = vec_ref[chunk, 6:7, :]
 
@@ -744,6 +755,7 @@
             return inner
 
         lax.fori_loop(0, OWN // 32, gelu_rows, 0)
+        during_chunk(turn)
         sum_ref[...] += dot(act_ref[chunk], down_ref[chunk])
         return carry
 
@@ -751,14 +763,14 @@
     y_ref[...] = sum_ref[...].astype(jnp.bfloat16)
 
 
-def feed_back(dy_ref, act_ref, slope_ref, down_ref, up_ref, hidden_ref, normed_t_ref, vec_ref, out_ref, attended_ref, attended_t_ref, grad_hidden_ref, grad_att_ref, centre_ref, grads_ref, vec_grad_ref, low_ref, low_t_ref, chunk_ref, sum_ref):
-    gain = vec_ref[0, 3:4, :]
+def feed_back(dy_ref, act_ref, slope_ref, down_ref, up_ref, hidden_ref, normed_t_ref, vec_ref, out_ref, attended_ref, attended_t_ref, grad_hidden_ref, grad_att_ref, centre_ref, grads_ref, vec_grad_ref, low_ref, low_t_ref, chunk_ref, sum_ref, during_chunk, after_chunk, before_norm, between):
     low_ref[...] = dy_ref[...].astype(jnp.bfloat16)
     low_t_ref[...] = low_ref[...].T
     vec_grad_ref[...] = jnp.zeros_like(vec_grad_ref)
     sum_ref[...] = jnp.zeros_like(sum_ref)
 
-    def chunk_step(chunk, carry):
+    def chunk_step(turn, carry):
+        chunk = turn_part(turn + 1)
         grad_act = dot(low_ref[...], down_ref[chunk], BOTH_LAST)
         grad_up = (grad_act * slope_ref[chunk].astype(jnp.float32)).astype(jnp.bfloat16)
         chunk_ref[...] = grad_up
@@ -768,10 +780,14 @@
         for part in range(PARTS):
             grads_ref[part, chunk, :, 0:512] = down_term[part * 128 : (part + 1) * 128, :]
             grads_ref[part, chunk, :, 512:1024] = up_term[part * 128 : (part + 1) * 128, :]
+        after_chunk(turn, chunk)
         sum_ref[...] += dot(chunk_ref[...], up_ref[chunk], BOTH_LAST)
+        during_chunk(turn)
         return carry
 
     lax.fori_loop(0, PARTS, chunk_step, 0)
+    before_norm()
+    gain = vec_ref[0, 3:4, :]
 
     def norm_rows(index, carry):
         rows = tile_rows(index * 128, 128)
@@ -787,6 +803,7 @@
         return carry
 
     lax.fori_loop(0, OWN // 128, norm_rows, 0)
+    between()
     row = lax.broadcasted_iota(jnp.int32, (8, 128), 0)
     lane = lax.broadcasted_iota(jnp.int32, (8, 128), 1)
     picks = jnp.where((row < 2) & ((lane < HEAD) == (row == 0)), 1.0, 0.0)
@@ -813,8 +830,9 @@
     lane = lax.broadcasted_iota(jnp.int32, (BLOCK, 128), 1)
     grad_kv_ref[...] = jnp.zeros_like(grad_kv_ref)
 
-    def pair_step(pair, carry):
-        before_pair(pair)
+    def pair_step(turn, carry):
+        pair = turn_part(turn + 1)
+        before_pair(turn)
         parts = [[None] * TASKS, [None] * TASKS]
         for task in range(TASKS):
             rows = tile_rows(slots[task] * BLOCK, BLOCK)
@@ -856,36 +874,30 @@
             for kind in range(2):
                 rows = grad_kv_ref[kind, pair, tile_rows(block * BLOCK, BLOCK), :]
                 send_ref[kind, pair, slot * BLOCK : (slot + 1) * BLOCK, :] = rows.astype(jnp.bfloat16)
-        after_pair(pair)
+        after_pair(turn, pair)
         return carry
 
     lax.fori_loop(0, PAIRS, pair_step, 0)
 
 
-def project_back(grad_query_ref, grad_kv_ref, other_ref, x_ref, grad_hidden_ref, normed_t_ref, weight_ref, vec_ref, grad_x_ref, grad_x_low_ref, grads_ref, vec_grad_ref, sum_ref, before_pair, after_pair, between):
-    core = lax.axis_index("section")
+def project_back_pair(pair, grad_query_ref, grad_kv_ref, other_ref, normed_t_ref, weight_ref, grads_ref, sum_ref, send):
+    parts = [grad_query_ref[pair]]
+    for kind in range(2):
+        halves = []
+        for slot, block in enumerate(blocks_of(lax.axis_index("section"))):
+            own = grad_kv_ref[kind, pair, tile_rows(block * BLOCK, BLOCK), :]
+            halves.append(own + other_ref[kind, pair, slot * BLOCK : (slot + 1) * BLOCK, :].astype(jnp.float32))
+        parts.append(jnp.concatenate(halves, axis=0).astype(jnp.bfloat16))
+    grads = jnp.concatenate(parts, axis=1)
+    term = dot(normed_t_ref[...], grads).astype(jnp.bfloat16)
+    for part in range(PARTS):
+        grads_ref[part, pair, :, 1152:1536] = term[part * 128 : (part + 1) * 128, :]
+    send()
+    sum_ref[...] += dot(grads, weight_ref[pair], BOTH_LAST)
+
+
+def project_back_norm(x_ref, grad_hidden_ref, vec_ref, grad_x_ref, grad_x_low_ref, vec_grad_ref, sum_ref):
     gain = vec_ref[0, 0:1, :]
-    sum_ref[...] = jnp.zeros_like(sum_ref)
-
-    def pair_step(pair, carry):
-        before_pair(pair)
-        parts = [grad_query_ref[pair]]
-        for kind in range(2):
-            halves = []
-            for slot, block in enumerate(blocks_of(core)):
-                own = grad_kv_ref[kind, pair, tile_rows(block * BLOCK, BLOCK), :]
-                halves.append(own + other_ref[kind, pair, slot * BLOCK : (slot + 1) * BLOCK, :].astype(jnp.float32))
-            parts.append(jnp.concatenate(halves, axis=0).astype(jnp.bfloat16))
-        grads = jnp.concatenate(parts, axis=1)
-        term = dot(normed_t_ref[...], grads).astype(jnp.bfloat16)
-        for part in range(PARTS):
-            grads_ref[part, pair, :, 1152:1536] = term[part * 128 : (part + 1) * 128, :]
-        after_pair(pair)
-        sum_ref[...] += dot(grads, weight_ref[pair], BOTH_LAST)
-        return carry
-
-    lax.fori_loop(0, PAIRS, pair_step, 0)
-    between()
 
     def norm_rows(index, carry):
         rows = tile_rows(index * 128, 128)
@@ -977,14 +989,58 @@
 QKV, OUT, UP, DOWN, VEC = range(5)
 
 
+ALL = (1, 2, 3)
+FORWARD_PLAN = (
+    ("masks", None, 0, "near", ALL, (QKV,)),
+    ("masks", None, 0, "z", ALL, (OUT,)),
+    ("masks", None, 0, "z", (1,), (UP, DOWN)),
+    ("masks", None, 0, "own", None, (QKV, OUT, UP, DOWN)),
+    ("vec", None, 0, "far", ALL, (QKV,)),
+    ("vec", None, 0, "z", (2,), (UP, DOWN)),
+    ("rows", None, 0, "z", (3,), (UP, DOWN)),
+    ("norm0", None, 0, "sib", ALL, (QKV,)),
+    ("norm0", None, 1, "own", None, (QKV, OUT, UP, DOWN)),
+    ("project0", 0, 0, "near", ALL, (OUT,)),
+    ("project0", 1, 0, "near", (1,), (UP, DOWN)),
+    ("project0", 3, 0, "far", ALL, (OUT,)),
+    ("project0", 3, 0, "near", (2,), (UP, DOWN)),
+    ("attend0", 0, 0, "far", (1,), (UP, DOWN)),
+    ("attend0", 1, 0, "sib", ALL, (OUT,)),
+    ("attend0", 1, 0, "near", (3,), (UP, DOWN)),
+    ("attend0", 2, 0, "far", (2,), (UP, DOWN)),
+    ("attend0", 2, 0, "sib", (1,), (UP, DOWN)),
+    ("attend0", 2, 1, "z", ALL, (QKV,)),
+    ("attend0", 3, 0, "far", (3,), (UP, DOWN)),
+    ("attended0", None, 0, "sib", (2,), (UP, DOWN)),
+    ("attended0", None, 1, "z", ALL, (OUT, UP, DOWN)),
+    ("second0", None, 0, "sib", (3,), (UP, DOWN)),
+    ("chunk0", 0, 1, "near", ALL, (QKV,)),
+    ("chunk0", 2, 1, "far", ALL, (QKV,)),
+    ("chunk0", 3, 1, "sib", ALL, (QKV,)),
+    ("project1", 0, 1, "near", ALL, (OUT,)),
+    ("project1", 1, 1, "near", (1,), (UP, DOWN)),
+    ("project1", 2, 1, "near", (2,), (UP, DOWN)),
+    ("project1", 3, 1, "near", (3,), (UP, DOWN)),
+    ("attend1", 1, None, "rows", None, ()),
+    ("attend1", 1, 1, "far", ALL, (OUT,)),
+    ("attend1", 2, 1, "far", (1, 2), (UP, DOWN)),
+    ("attend1", 3, 1, "far", (3,), (UP, DOWN)),
+    ("attend1", 3, 1, "sib", ALL, (OUT,)),
+    ("attended1", None, 1, "sib", (1, 2), (UP, DOWN)),
+    ("chunk1", 0, 1, "sib", (3,), (UP, DOWN)),
+)
+
+
 def forward_kernel(lens_ref, tokens, cotangent, *refs):
     shards, refs = refs[:5], refs[5:]
     dy_out, y_out, saved_out, weights_out, refs = refs[0], refs[1], refs[2:13], refs[13:18], refs[18:]
     saved, weights, refs = refs[:11], refs[11:16], refs[16:]
     y_ref, bias_ref, normed, logit, factor, stat, wide, total, refs = *refs[:8], refs[8:]
-    row_send, row_recv, row_local, z_send, z_recv, xy_send, xy_recv, sib_send, sib_recv, local, kv_send, kv_recv, save_sem = refs
+    row_send, row_recv, row_local, z_send, z_recv, xy_send, xy_recv, sib_send, sib_recv, local, kv_send, kv_recv, save_sem, keep_sem = refs
     core, rep, part = place()
     greet(all_partners())
+
+    steps = (1, 2, 3)
 
     def z_copy(index, step):
         slot = (index, step - 1)
@@ -996,44 +1052,83 @@
     def own_copy(index):
         return pltpu.make_async_copy(shards[index], weights[index].at[core, part], local.at[index])
 
-    def xy_copy(index, step, far):
-        slot = (index, step - 1, far - 1)
-        view = weights[index].at[core, lax.rem(part + far, PARTS), quarter_rows(shards[index], rep)]
+    def near_copy(index, step, far):
+        slot = (index, far - 1, step - 1)
+        view = weights[index].at[core, turn_part(far), quarter_rows(shards[index], rep)]
         return remote(view, view, xy_send.at[slot], xy_recv.at[slot], along_dp(step))
 
-    def sib_copy(index):
-        view = weights[index].at[core]
-        return remote(view, view, sib_send.at[index], sib_recv.at[index], sibling())
-
-    steps = (1, 2, 3)
-
-    def z_start(*which):
+    def far_copy(index, step, far):
+        slot = (index, far - 1, step + 1)
+        count = shards[index].shape[0] // PARTS
+        rows = tile_rows(lax.bitwise_xor(rep, 3 - step) * count + (2 - step) * (count // 2), count // 2)
+        view = weights[index].at[core, turn_part(far), rows]
+        return remote(view, view, xy_send.at[slot], xy_recv.at[slot], along_dp(step))
+
+    def sib_copy(index, far):
+        target = weights[index].at[core, turn_part(far)]
+        source = target if far else shards[index]
+        return remote(source, target, sib_send.at[index, far], sib_recv.at[index, far], sibling())
+
+    def vec_copy():
+        view = weights[VEC].at[core]
+        return remote(view, view, sib_send.at[VEC, 0], sib_recv.at[VEC, 0], sibling())
+
+    def own_start(*which):
         for index in which:
             own_copy(index).start()
-            for step in steps:
-                z_copy(index, step).start()
-
-    def xy_start(*which):
+            sib_copy(index, 0).start()
+
+    def z_start(far, *which):
         for index in which:
-            for step in steps:
-                z_copy(index, step).wait_recv()
-            for step in steps:
-                for far in steps:
-                    xy_copy(index, step, far).start()
-
-    def sib_start(*which):
+            z_copy(index, PARTS - far).start()
+
+    def xy_start(far, *which):
         for index in which:
-            own_copy(index).wait()
-            for step in steps:
-                for far in steps:
-                    xy_copy(index, step, far).wait_recv()
-            sib_copy(index).start()
-
-    def need(layer, *which):
+            z_copy(index, PARTS - far).wait_recv()
+            for step in (1, 2):
+                near_copy(index, step, far).start()
+
+    def far_start(far, *which):
+        for index in which:
+            for step in (2, 1):
+                near_copy(index, 3 - step, far).wait_recv()
+                far_copy(index, step, far).start()
+
+    def sib_start(far, *which):
+        for index in which:
+            for step in (1, 2):
+                far_copy(index, step, far).wait_recv()
+            sib_copy(index, far).start()
+
+    def need(layer, far, *which):
         @pl.when(core != layer)
         def _():
             for index in which:
-                sib_copy(index).wait_recv()
+                sib_copy(index, far).wait_recv()
+
+        if far == 0:
+
+            @pl.when(core == layer)
+            def _():
+                for index in which:
+                    own_copy(index).wait()
+
+    def need_turn(layer, turn, *which):
+        for far in range(PARTS):
+            pl.when(turn == far)(partial(need, layer, far, *which))
+
+    def keep_copy(layer, index):
+        return pltpu.make_async_copy(weights[index].at[layer], weights_out[index].at[layer], keep_sem.at[layer, index])
+
+    def keep(layer, *which):
+        for index in which:
+            keep_copy(layer, index).start()
+
+    def on(layer, action, *which):
+        pl.when(core == layer)(partial(action, *which))
+
+    def at(layer, turn, when, action, *which):
+        pl.when((core == layer) & (turn == when))(partial(action, *which))
 
     owner = jnp.where((part == 0) | (part == 3), 0, 1)
     place_here = jnp.where(part < 2, 0, 1)
@@ -1078,95 +1173,103 @@
             copies.append(remote(view, view, kv_send.at[layer, pair, slot], kv_recv.at[layer, pair, slot], sibling()))
         return copies
 
-    def on(layer, action, *which):
-        @pl.when(core == layer)
-        def _():
-            action(*which)
-
-    on(0, z_start, QKV)
-    for step in steps:
-        z_copy(VEC, step).start()
+    actions = {"own": own_start, "z": z_start, "near": xy_start, "far": far_start, "sib": sib_start}
+
+    def run(point, turn=None):
+        for where, when, owner_core, name, fars, which in FORWARD_PLAN:
+            if where != point:
+                continue
+
+            def act():
+                if name == "own":
+                    own_start(*which)
+                elif name == "rows":
+                    rows_each(1, "start")
+                else:
+                    for far in fars:
+                        actions[name](far, *which)
+
+            here = core == owner_core if owner_core is not None else None
+            if turn is not None:
+                here = turn == when if here is None else here & (turn == when)
+            act() if here is None else pl.when(here)(act)
+
+    for far in steps:
+        on(0, z_start, far, QKV)
+        z_start(far, VEC)
     own_copy(VEC).start()
     rows_each(0, "start")
-    on(0, z_start, OUT, UP, DOWN)
     fill_masks(lens_ref, bias_ref, False)
-    on(0, xy_start, QKV)
+    run("masks")
     own_copy(VEC).wait()
     for step in steps:
         z_copy(VEC, step).wait_recv()
-    sib_copy(VEC).start()
+    vec_copy().start()
+    run("vec")
     rows_each(0, "wait")
     rows_arrived(0)
-    sib_copy(VEC).wait_recv()
+    vec_copy().wait_recv()
+    run("rows")
     for layer in range(2):
         signed = layer == 0
         held = [item.at[layer] for item in saved]
         qkv, out, up, down, vec = [item.at[layer] for item in weights]
         x_ref, normed_one_t, queries, kv, attended, attended_t, logs, hidden, normed_two_t, act, slope = held
 
-        def before_project():
-            on(layer, sib_start, QKV)
-            need(layer, QKV)
-            if layer == 1:
-                rows_each(1, "start")
-
-        def push_kv(pair):
+        def after_norm():
+            run(f"norm{layer}")
+
+        def before_project(turn):
+            run(f"project{layer}", turn)
+            need_turn(layer, turn, QKV)
+
+        def push_kv(turn, pair):
             for copy in kv_copies(layer, pair, False):
                 copy.start()
 
-        def before_attend(pair):
+        def before_attend(turn, pair):
+            run(f"attend{layer}", turn)
             for copy in kv_copies(layer, pair, True):
                 copy.wait_recv()
-            if layer == 0:
-
-                @pl.when((pair == 2) & (core == 0))
-                def _():
-                    sib_start(OUT)
-
-                @pl.when((pair == 2) & (core == 1))
-                def _():
-                    xy_start(QKV)
-
-            else:
-
-                @pl.when((pair == 2) & (core == 1))
-                def _():
-                    sib_start(UP, DOWN)
-
-        project(x_ref, vec, qkv, normed_one_t, queries, kv, normed, before_project, push_kv)
+
+        def before_out(turn):
+            need_turn(layer, turn, OUT)
+
+        def before_feed():
+            run(f"second{layer}")
+
+        def before_chunk(turn):
+            need_turn(layer, turn, UP, DOWN)
+            if layer == 1:
+                pl.when(turn == PARTS - 1)(partial(keep, 1, OUT, UP, DOWN))
+
+        def during_chunk(turn):
+            run(f"chunk{layer}", turn)
+
+        project(x_ref, vec, qkv, normed_one_t, queries, kv, normed, after_norm, before_project, push_kv)
         save(layer, 0, 1, 2)
-        if layer == 0:
-            on(0, xy_start, OUT, UP, DOWN)
-            on(1, z_start, QKV, OUT, UP, DOWN)
-        else:
-            on(1, sib_start, OUT)
+        keep(layer, QKV, VEC)
         attend_rows(signed, queries, kv, bias_ref, attended, attended_t, logs, logit, factor, stat, before_attend)
         save(layer, 3, 4, 5, 6)
+        run(f"attended{layer}")
+        target = saved[0].at[1] if layer == 0 else y_ref
+        feed(x_ref, attended, vec, out, up, down, hidden, normed_two_t, act, slope, target, normed, wide, total, before_out, before_feed, before_chunk, during_chunk)
+        save(layer, 7, 8, 9, 10)
         if layer == 0:
-            on(0, sib_start, UP, DOWN)
-            on(1, xy_start, OUT, UP, DOWN)
-        need(layer, OUT)
-
-        def before_feed():
-            need(layer, UP, DOWN)
-
-        target = saved[0].at[1] if layer == 0 else y_ref
-        feed(x_ref, attended, vec, out, up, down, hidden, normed_two_t, act, slope, target, normed, wide, total, before_feed)
-        save(layer, 7, 8, 9, 10)
+            keep(0, OUT, UP, DOWN)
     y_copy = pltpu.make_async_copy(y_ref, y_out, row_local.at[0])
     y_copy.start()
-    weight_copies = [pltpu.make_async_copy(weights[index], weights_out[index], local.at[index]) for index in range(5)]
-    for copy in weight_copies:
-        copy.start()
     rows_each(1, "wait")
     rows_arrived(1)
     for index in range(5):
         for step in steps:
             z_copy(index, step).wait_send()
             if index != VEC:
-                for far in steps:
-                    xy_copy(index, step, far).wait_send()
-        sib_copy(index).wait_send()
+                for way in (1, 2):
+                    near_copy(index, way, step).wait_send()
+                    far_copy(index, way, step).wait_send()
+                sib_copy(index, step).wait_send()
+        sib_copy(index, 0).wait_send() if index != VEC else vec_copy().wait_send()
     for layer in range(2):
         for pair in range(PAIRS):
             for copy in kv_copies(layer, pair, False):
@@ -1174,11 +1277,13 @@
         for index in range(11):
             pltpu.make_async_copy(saved[index].at[layer], saved_out[index].at[layer], save_sem.at[layer, index]).wait()
     y_copy.wait()
-    for copy in weight_copies:
-        copy.wait()
-
-
-GROUPS = ((0, 1152), (1152, 1536))
+    for layer in range(2):
+        for index in range(5):
+            keep_copy(layer, index).wait()
+
+
+FEED, ATTEND = 0, 1
+GROUPS = ((0, 1024), (1024, 1536))
 
 
 def backward_kernel(lens_ref, dy_in, y_in, *refs):
@@ -1186,8 +1291,8 @@
     grads_out, vec_out, blocks_out, rows_out, refs = *refs[:4], refs[4:]
     held, weights, refs = refs[:11], refs[11:16], refs[16:]
     dy_low, dy_ref, bias_ref, grads_ref, vec_grad, low, low_t, chunk, total, grad_hidden, grad_att, centres, grad_query, grad_kv, kv_out, kv_got, grad_low, refs = *refs[:17], refs[17:]
-    got_core, got_dp, part_sum, got_part, final, vec_core, vec_chip, vec_dp, vec_rep, vec_part, refs = *refs[:10], refs[10:]
-    load_sem, weight_sem, dy_sem, y_send, y_recv, row_send, row_recv, kv_send, kv_recv, core_send, core_recv, dp_send, dp_recv, part_send, part_recv, vec_send, vec_recv, last_send, last_recv = refs
+    got_core, got_first, got_second, part_sum, got_part, final, vec_core, vec_chip, vec_dp, vec_rep, vec_part, refs = *refs[:11], refs[11:]
+    load_sem, weight_sem, dy_sem, y_send, y_recv, row_send, row_recv, kv_send, kv_recv, core_send, core_recv, first_send, first_recv, second_send, second_recv, part_send, part_recv, vec_send, vec_recv, last_send, last_recv = refs
     core, rep, part = place()
     steps = (1, 2, 3)
     mine, theirs = tile_rows(core * 64, 64), tile_rows((1 - core) * 64, 64)
@@ -1204,12 +1309,13 @@
         for copy in copies:
             copy.wait()
 
-    feed_set = ((9, 10, 7, 8, 4, 5), (DOWN, UP, VEC, OUT))
+    chunk_set = ((10, 9, 8), (DOWN, UP))
+    norm_set = ((7, 5, 4), (VEC, OUT))
     attend_set = ((2, 3, 6), ())
     project_set = ((0, 1), (QKV,))
     dy_copy = pltpu.make_async_copy(dy_in, dy_low, dy_sem.at[0])
     dy_copy.start()
-    for group in (feed_set, attend_set, project_set):
+    for group in (chunk_set, norm_set, attend_set, project_set):
         start(load(1, *group))
     greet(all_partners() + [(1 - core, rep, lax.rem(part + step, PARTS)) for step in steps])
 
@@ -1240,56 +1346,75 @@
     deliver(saved_in[0].at[1], 0, blocks_out, y_send, y_recv, "start")
     deliver(y_in, 1, blocks_out, y_send, y_recv, "start")
 
-    def core_copy(layer, group):
+    def core_copy(layer, group, turn):
         first, last = GROUPS[group]
-        return remote(grads_ref.at[:, :, theirs, first:last], got_core.at[layer, :, :, :, first:last], core_send.at[layer, group], core_recv.at[layer, group], sibling())
-
-    def dp_copy(layer, group, step):
+        other, slot = turn_part(turn + 1), (layer, group, turn)
+        return remote(grads_ref.at[:, other, theirs, first:last], got_core.at[layer, :, other, :, first:last], core_send.at[slot], core_recv.at[slot], sibling())
+
+    def halves(way):
+        return pl.ds(0, 32) if way == 1 else pl.ds(32, 32)
+
+    def first_copy(layer, group, turn, way, piece):
         first, last = GROUPS[group]
-        slot = (layer, group, step - 1)
-        return remote(got_core.at[layer, lax.bitwise_xor(rep, step), :, :, first:last], got_dp.at[layer, step - 1, :, :, first:last], dp_send.at[slot], dp_recv.at[slot], along_dp(step))
-
-    def part_copy(layer, group, step):
+        other, slot = turn_part(turn + 1), (layer, group, turn, way - 1, piece)
+        source = got_core.at[layer, lax.bitwise_xor(rep, 3 if piece else way), other, halves(way), first:last]
+        return remote(source, got_first.at[layer, way - 1, piece, other, :, first:last], first_send.at[slot], first_recv.at[slot], along_dp(way))
+
+    def second_copy(layer, group, turn, way):
         first, last = GROUPS[group]
-        slot = (layer, group, step - 1)
-        return remote(part_sum.at[layer, lax.rem(part + step, PARTS), :, first:last], got_part.at[layer, step - 1, :, first:last], part_send.at[slot], part_recv.at[slot], along_tensor(step))
-
-    def dp_start(layer, group):
+        other, slot = turn_part(turn + 1), (layer, group, turn, way - 1)
+        source = got_core.at[layer, lax.bitwise_xor(rep, 3 - way), other, halves(way), first:last]
+        return remote(source, got_second.at[layer, way - 1, other, :, first:last], second_send.at[slot], second_recv.at[slot], along_dp(3 - way))
+
+    def part_copy(layer, group, turn):
         first, last = GROUPS[group]
-        core_copy(layer, group).wait()
-
-        def add(index, carry):
-            major, minor = index // PARTS, lax.rem(index, PARTS)
-            own = grads_ref[major, minor, mine, first:last].astype(jnp.float32)
-            sum_here = own + got_core[layer, major, minor, :, first:last].astype(jnp.float32)
-            got_core[layer, major, minor, :, first:last] = sum_here.astype(jnp.bfloat16)
+        slot = (layer, group, turn)
+        return remote(part_sum.at[layer, turn, :, first:last], got_part.at[layer, turn, :, first:last], part_send.at[slot], part_recv.at[slot], along_tensor(turn + 1))
+
+    def dp_start(layer, group, turn):
+        first, last = GROUPS[group]
+        core_copy(layer, group, turn).wait()
+        other = turn_part(turn + 1)
+
+        def add(major, carry):
+            own = grads_ref[major, other, mine, first:last].astype(jnp.float32)
+            sum_here = own + got_core[layer, major, other, :, first:last].astype(jnp.float32)
+            got_core[layer, major, other, :, first:last] = sum_here.astype(jnp.bfloat16)
             return carry
 
-        lax.fori_loop(0, PARTS * PARTS, add, 0)
-        start(dp_copy(layer, group, step) for step in steps)
-
-    def part_start(layer, group):
+        lax.fori_loop(0, PARTS, add, 0)
+        start(first_copy(layer, group, turn, way, piece) for way in (1, 2) for piece in range(2))
+
+    def dp_next(layer, group, turn):
         first, last = GROUPS[group]
-        for step in steps:
-            dp_copy(layer, group, step).wait()
-
-        def add(minor, carry):
-            sum_here = got_core[layer, rep, minor, :, first:last].astype(jnp.float32)
-            for step in steps:
-                sum_here = sum_here + got_dp[layer, step - 1, minor, :, first:last].astype(jnp.float32)
-            part_sum[layer, minor, :, first:last] = sum_here.astype(jnp.bfloat16)
-            return carry
-
-        lax.fori_loop(0, PARTS, add, 0)
-        start(part_copy(layer, group, step) for step in steps)
+        other = turn_part(turn + 1)
+        for way in (1, 2):
+            for piece in (1, 0):
+                first_copy(layer, group, turn, way, piece).wait()
+                major = lax.bitwise_xor(rep, 3 - way) if piece else rep
+                own = got_core[layer, major, other, halves(way), first:last].astype(jnp.float32)
+                sum_here = own + got_first[layer, way - 1, piece, other, :, first:last].astype(jnp.float32)
+                got_core[layer, major, other, halves(way), first:last] = sum_here.astype(jnp.bfloat16)
+                if piece:
+                    second_copy(layer, group, turn, way).start()
+
+    def part_start(layer, group, turn):
+        first, last = GROUPS[group]
+        other = turn_part(turn + 1)
+        for way in (1, 2):
+            second_copy(layer, group, turn, way).wait()
+            own = got_core[layer, rep, other, halves(way), first:last].astype(jnp.float32)
+            sum_here = own + got_second[layer, way - 1, other, :, first:last].astype(jnp.float32)
+            part_sum[layer, turn, halves(way), first:last] = sum_here.astype(jnp.bfloat16)
+        if turn < PARTS - 1:
+            part_copy(layer, group, turn).start()
 
     def finish(layer, group):
         first, last = GROUPS[group]
-        for step in steps:
-            part_copy(layer, group, step).wait()
-        sum_here = part_sum[layer, part, :, first:last].astype(jnp.float32)
-        for step in steps:
-            sum_here = sum_here + got_part[layer, step - 1, :, first:last].astype(jnp.float32)
+        sum_here = part_sum[layer, PARTS - 1, :, first:last].astype(jnp.float32)
+        for turn in range(PARTS - 1):
+            part_copy(layer, group, turn).wait()
+            sum_here = sum_here + got_part[layer, turn, :, first:last].astype(jnp.float32)
         final[layer, :, first:last] = sum_here
 
     def last_copy(layer):
@@ -1315,58 +1440,91 @@
         if layer == 1:
             dy_copy.wait()
             dy_ref[...] = dy_low[...].astype(jnp.float32)
-        wait(load(layer, *feed_set))
-        feed_back(dy_ref, act, slope, down, up, hidden, normed_two_t, vec, out, attended, attended_t, grad_hidden, grad_att, centres, grads_ref, vec_grad.at[layer], low, low_t, chunk, total)
-        core_copy(layer, 0).start()
+        wait(load(layer, *chunk_set))
+
+        def at(turn, when, action, *which):
+            pl.when(turn == when)(partial(action, *which))
+
+        def during_chunk(turn):
+            pl.when(turn > 0)(lambda: dp_start(layer, FEED, turn - 1))
+            at(turn, 3, dp_next, layer, FEED, 0)
+            if layer == 0:
+                at(turn, 0, dp_next, 1, ATTEND, 1)
+                at(turn, 0, dp_next, 1, ATTEND, 2)
+                at(turn, 1, dp_next, 1, ATTEND, 3)
+                at(turn, 1, part_start, 1, ATTEND, 0)
+                at(turn, 2, part_start, 1, ATTEND, 1)
+                at(turn, 2, part_start, 1, ATTEND, 2)
+                at(turn, 2, finish, 1, FEED)
+                at(turn, 3, part_start, 1, ATTEND, 3)
+
+        def after_chunk(turn, chunk):
+            core_copy(layer, FEED, turn).start()
+
+        def before_norm():
+            wait(load(layer, *norm_set))
+
+        def after_norm():
+            dp_start(layer, FEED, 3)
+            dp_next(layer, FEED, 1)
+
+        feed_back(dy_ref, act, slope, down, up, hidden, normed_two_t, vec, out, attended, attended_t, grad_hidden, grad_att, centres, grads_ref, vec_grad.at[layer], low, low_t, chunk, total, during_chunk, after_chunk, before_norm, after_norm)
         if layer == 1:
             start(load(0, (9, 10, 7, 8, 4, 5), (DOWN, UP, OUT)))
-        else:
-            part_start(1, 0)
-            part_start(1, 1)
         wait(load(layer, *attend_set))
 
-        def before_attend(pair):
-            @pl.when(pair == 2)
-            def _():
-                dp_start(layer, 0)
-                if layer == 0:
-                    finish(1, 0)
-                    finish(1, 1)
-                    hand_over(1)
-
-        def push_kv(pair):
+        def before_attend(turn):
+            at(turn, 0, dp_next, layer, FEED, 2)
+            at(turn, 1, dp_next, layer, FEED, 3)
+            at(turn, 1, part_start, layer, FEED, 0)
+            at(turn, 1, part_start, layer, FEED, 1)
+            at(turn, 2, part_start, layer, FEED, 2)
+            at(turn, 3, part_start, layer, FEED, 3)
+            if layer == 0:
+                at(turn, 0, finish, 1, ATTEND)
+                at(turn, 0, hand_over, 1)
+
+        def project_turn(turn):
+            pair = turn_part(turn + 1)
+            kv_copy(layer, pair).wait()
+            project_back_pair(pair, grad_query, grad_kv, kv_got.at[layer], normed_one_t, qkv, grads_ref, total, core_copy(layer, ATTEND, turn).start)
+
+        def after_attend(turn, pair):
             kv_copy(layer, pair).start()
-
-        attend_rows_back(signed, queries, kv, grad_att, bias_ref, logs, centres, grad_query, grad_kv, kv_out, before_attend, push_kv)
+            at(turn, 2, dp_start, layer, ATTEND, 0)
+            at(turn, 3, dp_start, layer, ATTEND, 1)
+            at(turn, 3, dp_next, layer, ATTEND, 0)
+            pl.when(turn > 0)(lambda: project_turn(turn - 1))
+
+        wait(load(layer, *project_set))
+        total[...] = jnp.zeros_like(total)
+        attend_rows_back(signed, queries, kv, grad_att, bias_ref, logs, centres, grad_query, grad_kv, kv_out, before_attend, after_attend)
         if layer == 1:
             start(load(0, *attend_set))
-        wait(load(layer, *project_set))
-
-        def before_project(pair):
-            kv_copy(layer, pair).wait()
-
-        def between():
-            core_copy(layer, 1).start()
-
-        project_back(grad_query, grad_kv, kv_got.at[layer], x_ref, grad_hidden, normed_one_t, qkv, vec, dy_ref, grad_low.at[layer], grads_ref, vec_grad.at[layer], total, before_project, lambda pair: None, between)
+        dp_start(layer, ATTEND, 2)
+        project_turn(PAIRS - 1)
+        project_back_norm(x_ref, grad_hidden, vec, dy_ref, grad_low.at[layer], vec_grad.at[layer], total)
         if layer == 1:
             start(load(0, (0, 1), (QKV, VEC)))
         deliver(grad_low.at[layer], layer, rows_out, row_send, row_recv, "start")
-        dp_start(layer, 1)
+        dp_start(layer, ATTEND, 3)
     vec_copy = remote(vec_grad.at[1 - core], vec_core, vec_send.at[0], vec_recv.at[0], sibling())
     vec_copy.start()
-    part_start(0, 0)
+    dp_next(0, ATTEND, 1)
+    dp_next(0, ATTEND, 2)
+    finish(0, FEED)
     vec_copy.wait()
     vec_chip[...] = vec_grad[core] + vec_core[...]
     vec_copies = [remote(vec_chip, vec_dp.at[step - 1], vec_send.at[step], vec_recv.at[step], along_dp(step)) for step in steps]
     start(vec_copies)
-    part_start(0, 1)
+    dp_next(0, ATTEND, 3)
+    for turn in range(PARTS):
+        part_start(0, ATTEND, turn)
     wait(vec_copies)
     vec_rep[...] = vec_chip[...] + vec_dp[0] + vec_dp[1] + vec_dp[2]
     vec_copies = [remote(vec_rep, vec_part.at[step - 1], vec_send.at[3 + step], vec_recv.at[3 + step], along_tensor(step)) for step in steps]
     start(vec_copies)
-    finish(0, 0)
-    finish(0, 1)
+    finish(0, ATTEND)
     hand_over(0)
     wait(vec_copies)
     vec_out[...] = vec_rep[...] + vec_part[0] + vec_part[1] + vec_part[2]
@@ -1445,14 +1603,15 @@
             (2,),
             (5, 3),
             (5, 3),
-            (4, 3, 3),
-            (4, 3, 3),
-            (5,),
-            (5,),
+            (4, 3, 4),
+            (4, 3, 4),
+            (5, PARTS),
+            (5, PARTS),
             (5,),
             (2, PAIRS, 2),
             (2, PAIRS, 2),
             (2, 11),
+            (2, 5),
         ),
         0,
     )
@@ -1484,7 +1643,8 @@
             ((2, 2, PAIRS, OWN, 128), low),
             ((2, OWN, WIDTH), low),
             ((2, PARTS, PARTS, 64, 1536), low),
-            ((2, 3, PARTS, 64, 1536), low),
+            ((2, 2, 2, PARTS, 32, 1536), low),
+            ((2, 2, PARTS, 32, 1536), low),
             ((2, PARTS, 64, 1536), low),
             ((2, 3, 64, 1536), low),
             ((2, 64, 1536), f32),
@@ -1502,12 +1662,14 @@
             (PARTS,),
             (2, PAIRS),
             (2, PAIRS),
-            (2, 2),
-            (2, 2),
-            (2, 2, 3),
-            (2, 2, 3),
-            (2, 2, 3),
-            (2, 2, 3),
+            (2, 2, PARTS),
+            (2, 2, PARTS),
+            (2, 2, PARTS, 2, 2),
+            (2, 2, PARTS, 2, 2),
+            (2, 2, PARTS, 2),
+            (2, 2, PARTS, 2),
+            (2, 2, PARTS),
+            (2, 2, PARTS),
             (7,),
             (7,),
             (1,),

time: 234 us -> 208 us (0.89)
  Pallas kernels: 219 us -> 194 us
    pallas_call x2, Pallas kernels: 219 us -> 194 us  [kernel_call(): pl.pallas_call(body, out_shape=[jax.ShapeDtypeStruct(shape, kind) for sha...]
where the time goes in v3:
time: 208 us
  Pallas kernels  194 us (93%)
  local copies, waits for them, and re-layouts  10.4 us (5%)
  other arithmetic  2.96 us (1%)
    pallas_call x2, Pallas kernels, kernel_call(): pl.pallas_call(body, out_shape=[jax.ShapeDtypeStruct(shape, kind) for sha...  194 us

profile of v3, /device:TPU:0, one launch (start us, length us, event | category | flops | bytes accessed | tf_op | source)
XLA Modules:
  0.0 207.8 jit_solution(10327221847619757926)
XLA Ops:
  0.6 1.2 copy.30
  1.8 0.9 copy.31.refs_0_
  2.7 1.4 concatenate.3.refs_4_
  4.1 82.2 %forward.1 = (bf16[512,512]{1,0:T(8,128)(2,1)}, bf16[512,512]{1,0:T(8,128)(2,1)}, bf16[2,512,512]{2,1,0:T(8,128)(2,1)}, bf16[2,512,512]{2,1,0:T(8,128)(2,1)}, bf...) custom-call(s32[4,8]{1,0:T(4,128)} %lens_ref.3, ...), custom_call_target="tpu_custom_call" | custom-call | tf_op jit(solution)/shard_map/forward/pallas_call | solution.py:1547
  86.3 111.6 %backward.1 = (f32[128,1536]{1,0:T(8,128)}, f32[16,512]{1,0:T(8,128)}, bf16[4,256,512]{2,1,0:T(8,128)(2,1)}, bf16[4,256,512]{2,1,0:T(8,128)(2,1)}) custom-call(s32[4,8]{1,0:T(4,128)} %lens_ref.3, bf16[512,512]{1,0:T(8,128)(2,1)} %get-tuple-element.35.dy_in, bf16[512,512]{1,0:T(8,128)(2,1)} %get-tuple-element.36.y_in, ...), custom_call_target="tpu_custom_call" | custom-call | tf_op jit(solution)/shard_map/backward/pallas_call | solution.py:1547
  197.9 0.0 copy-start.1
  197.9 0.0 copy-start
  197.9 3.0 %bitcast_convert_fusion = f32[1,4,256,512]{3,2,1,0:T(8,128)} fusion(bf16[4,256,512]{2,1,0:T(8,128)(2,1)} %get-tuple-element.54), kind=kLoop, calls=%fused_computation | loop fusion | flops 524288 | bytes 3145728 | tf_op jit(solution)/shard_map/broadcast_in_dim | solution.py:1684
  200.9 0.0 copy-done.1
  200.9 0.7 slice_bitcast_fusion
  201.7 0.8 copy.34
  202.5 0.1 copy.32
  202.6 0.8 copy.33
  203.5 0.6 slice_bitcast_fusion.2
  204.1 1.5 fusion
  205.6 1.3 dynamic-slice_bitcast_fusion
  206.9 0.0 copy-done
  206.9 1.0 copy.36
  (2 shorter events, 0.0 us)
Async XLA Ops:
  197.9 3.0 %copy-start.1 = (f32[128,1536]{1,0:T(8,128)S(1)}, f32[128,1536]{1,0:T(8,128)}, u32[]{:S(2)}) copy-start(f32[128,1536]{1,0:T(8,128)} %get-tuple-element.56) | copy-start | bytes 2359300
  197.9 8.9 %copy-start = (bf16[4,256,512]{2,1,0:T(8,128)(2,1)S(1)}, bf16[4,256,512]{2,1,0:T(8,128)(2,1)}, u32[]{:S(2)}) copy-start(bf16[4,256,512]{2,1,0:T(8,128)(2,1)} %get-tuple-element.53) | copy-start | bytes 3145732

commit v4 on v3

--- a/solution.py
+++ b/solution.py
@@ -581,7 +581,7 @@
 
 
 def turn_part(turn):
-    return lax.rem(lax.axis_index("tensor") + turn, PARTS)
+    return lax.bitwise_xor(lax.axis_index("tensor"), lax.rem(turn, PARTS))
 
 
 def tile_rows(start, count):
@@ -610,6 +610,10 @@
     return jnp.where((lane < HEAD) == (parity == 0), values, 0.0)
 
 
+def side_by_side(weight_ref, pair):
+    return jnp.concatenate([weight_ref[pair, kind] for kind in range(3)], axis=1)
+
+
 def project(x_ref, vec_ref, weight_ref, normed_t_ref, query_ref, kv_ref, normed_ref, between, before_pair, after_pair):
     core = lax.axis_index("section")
     gain, bias = vec_ref[0, 0:1, :], vec_ref[0, 1:2, :]
@@ -627,7 +631,7 @@
     def pair_step(turn, carry):
         pair = turn_part(turn)
         before_pair(turn)
-        out = dot(normed_ref[...], weight_ref[pair])
+        out = dot(normed_ref[...], side_by_side(weight_ref, pair))
         queries = out[:, :128] * 0.125
         for parity in range(2):
             query_ref[pair, parity] = keep_head(queries, parity).astype(jnp.bfloat16)
@@ -893,7 +897,7 @@
     for part in range(PARTS):
         grads_ref[part, pair, :, 1152:1536] = term[part * 128 : (part + 1) * 128, :]
     send()
-    sum_ref[...] += dot(grads, weight_ref[pair], BOTH_LAST)
+    sum_ref[...] += dot(grads, side_by_side(weight_ref, pair), BOTH_LAST)
 
 
 def project_back_norm(x_ref, grad_hidden_ref, vec_ref, grad_x_ref, grad_x_low_ref, vec_grad_ref, sum_ref):
@@ -922,7 +926,7 @@
 
 def along_tensor(step):
     core, rep, part = place()
-    return (core, rep, lax.rem(part + step, PARTS))
+    return (core, rep, lax.bitwise_xor(part, step))
 
 
 def along_dp(step):
@@ -961,8 +965,12 @@
         bias_ref[task] = jnp.where((key >= start) & (key <= query), 0.0, NEGATIVE)
 
 
+def rows_view(array, rows, index):
+    return array.at[:, rows] if index == QKV else array.at[rows]
+
+
 def quarter_rows(array, which):
-    count = array.shape[0] // PARTS
+    count = array.shape[-2] // PARTS
     return tile_rows(which * count, count)
 
 
@@ -980,7 +988,7 @@
     ((PARTS, OWN, 512), jnp.bfloat16),
 )
 WEIGHTS = (
-    ((PARTS, 512, 384), jnp.bfloat16),
+    ((PARTS, 3, 512, 128), jnp.bfloat16),
     ((PARTS, 128, 512), jnp.bfloat16),
     ((PARTS, 512, 512), jnp.bfloat16),
     ((PARTS, 512, 512), jnp.bfloat16),
@@ -990,54 +998,53 @@
 
 
 ALL = (1, 2, 3)
+DIRECT = (QKV,)
 FORWARD_PLAN = (
     ("masks", None, 0, "near", ALL, (QKV,)),
-    ("masks", None, 0, "z", ALL, (OUT,)),
-    ("masks", None, 0, "z", (1,), (UP, DOWN)),
     ("masks", None, 0, "own", None, (QKV, OUT, UP, DOWN)),
-    ("vec", None, 0, "far", ALL, (QKV,)),
-    ("vec", None, 0, "z", (2,), (UP, DOWN)),
-    ("rows", None, 0, "z", (3,), (UP, DOWN)),
+    ("vec", None, 0, "z", (1, 2), (OUT, UP, DOWN)),
+    ("rows", None, 0, "z", (3,), (OUT, UP, DOWN)),
     ("norm0", None, 0, "sib", ALL, (QKV,)),
     ("norm0", None, 1, "own", None, (QKV, OUT, UP, DOWN)),
-    ("project0", 0, 0, "near", ALL, (OUT,)),
-    ("project0", 1, 0, "near", (1,), (UP, DOWN)),
-    ("project0", 3, 0, "far", ALL, (OUT,)),
-    ("project0", 3, 0, "near", (2,), (UP, DOWN)),
-    ("attend0", 0, 0, "far", (1,), (UP, DOWN)),
-    ("attend0", 1, 0, "sib", ALL, (OUT,)),
-    ("attend0", 1, 0, "near", (3,), (UP, DOWN)),
-    ("attend0", 2, 0, "far", (2,), (UP, DOWN)),
-    ("attend0", 2, 0, "sib", (1,), (UP, DOWN)),
+    ("project0", 0, 0, "near", (1,), (OUT, UP, DOWN)),
+    ("project0", 2, 0, "near", (2,), (OUT, UP, DOWN)),
+    ("attend0", 0, 0, "far", (1,), (OUT, UP, DOWN)),
+    ("attend0", 1, 0, "near", (3,), (OUT, UP, DOWN)),
+    ("attend0", 1, 0, "far", (2,), (OUT, UP, DOWN)),
     ("attend0", 2, 1, "z", ALL, (QKV,)),
-    ("attend0", 3, 0, "far", (3,), (UP, DOWN)),
-    ("attended0", None, 0, "sib", (2,), (UP, DOWN)),
-    ("attended0", None, 1, "z", ALL, (OUT, UP, DOWN)),
-    ("second0", None, 0, "sib", (3,), (UP, DOWN)),
-    ("chunk0", 0, 1, "near", ALL, (QKV,)),
+    ("attend0", 2, 0, "sib", (1,), (OUT, UP, DOWN)),
+    ("attend0", 3, 0, "far", (3,), (OUT, UP, DOWN)),
+    ("attend0", 3, 0, "sib", (2,), (OUT, UP, DOWN)),
+    ("attended0", None, 1, "z", (1, 2), (OUT, UP, DOWN)),
+    ("second0", None, 1, "near", ALL, (QKV,)),
+    ("attended0", None, 0, "sib", (3,), (OUT, UP, DOWN)),
+    ("chunk0", 0, 1, "z", (3,), (OUT, UP, DOWN)),
+    ("chunk0", 2, 1, "near", (1,), (OUT, UP, DOWN)),
+    ("chunk0", 3, 1, "near", (2,), (OUT, UP, DOWN)),
     ("chunk0", 2, 1, "far", ALL, (QKV,)),
+    ("chunk0", 2, None, "rows", None, ()),
     ("chunk0", 3, 1, "sib", ALL, (QKV,)),
-    ("project1", 0, 1, "near", ALL, (OUT,)),
-    ("project1", 1, 1, "near", (1,), (UP, DOWN)),
-    ("project1", 2, 1, "near", (2,), (UP, DOWN)),
-    ("project1", 3, 1, "near", (3,), (UP, DOWN)),
-    ("attend1", 1, None, "rows", None, ()),
-    ("attend1", 1, 1, "far", ALL, (OUT,)),
-    ("attend1", 2, 1, "far", (1, 2), (UP, DOWN)),
-    ("attend1", 3, 1, "far", (3,), (UP, DOWN)),
-    ("attend1", 3, 1, "sib", ALL, (OUT,)),
-    ("attended1", None, 1, "sib", (1, 2), (UP, DOWN)),
-    ("chunk1", 0, 1, "sib", (3,), (UP, DOWN)),
+    ("project1", 1, 1, "near", (3,), (OUT, UP, DOWN)),
+    ("project1", 2, 1, "far", (1,), (OUT, UP, DOWN)),
+    ("attend1", 0, 1, "far", (2,), (OUT, UP, DOWN)),
+    ("attend1", 1, 1, "sib", (1,), (OUT, UP, DOWN)),
+    ("attend1", 2, 1, "far", (3,), (OUT, UP, DOWN)),
+    ("attend1", 3, 1, "sib", (2,), (OUT, UP, DOWN)),
+    ("attended1", None, 1, "sib", (3,), (OUT, UP, DOWN)),
 )
 
 
 def forward_kernel(lens_ref, tokens, cotangent, *refs):
-    shards, refs = refs[:5], refs[5:]
+    shards, vectors, refs = refs[:4], refs[4:11], refs[11:]
     dy_out, y_out, saved_out, weights_out, refs = refs[0], refs[1], refs[2:13], refs[13:18], refs[18:]
     saved, weights, refs = refs[:11], refs[11:16], refs[16:]
-    y_ref, bias_ref, normed, logit, factor, stat, wide, total, refs = *refs[:8], refs[8:]
-    row_send, row_recv, row_local, z_send, z_recv, xy_send, xy_recv, sib_send, sib_recv, local, kv_send, kv_recv, save_sem, keep_sem = refs
+    y_ref, bias_ref, normed, logit, factor, stat, wide, total, vec_own, refs = *refs[:9], refs[9:]
+    row_send, row_recv, row_local, z_send, z_recv, xy_send, xy_recv, sib_send, sib_recv, local, kv_send, kv_recv, save_sem, keep_sem, pass_send = refs
     core, rep, part = place()
+    shards = (*shards, vec_own)
+    vec_own[...] = jnp.zeros_like(vec_own)
+    for row, vector in enumerate(vectors):
+        vec_own[row : row + 1, :] = vector[...]
     greet(all_partners())
 
     steps = (1, 2, 3)
@@ -1047,22 +1054,34 @@
         if index == VEC:
             return remote(shards[index], weights[index].at[core, part], z_send.at[slot], z_recv.at[slot], along_tensor(step))
         rows = quarter_rows(shards[index], rep)
-        return remote(shards[index].at[rows], weights[index].at[core, part, rows], z_send.at[slot], z_recv.at[slot], along_tensor(step))
+        return remote(rows_view(shards[index], rows, index), rows_view(weights[index].at[core, part], rows, index), z_send.at[slot], z_recv.at[slot], along_tensor(step))
+
+    def ends():
+        return (part == 0) | (part == 3)
+
+    def pass_copy(index):
+        view = rows_view(weights[index].at[core, turn_part(2)], quarter_rows(shards[index], rep), index)
+        return remote(view, view, pass_send.at[index], z_recv.at[index, 2], along_tensor(1))
 
     def own_copy(index):
         return pltpu.make_async_copy(shards[index], weights[index].at[core, part], local.at[index])
 
     def near_copy(index, step, far):
         slot = (index, far - 1, step - 1)
-        view = weights[index].at[core, turn_part(far), quarter_rows(shards[index], rep)]
+        view = rows_view(weights[index].at[core, turn_part(far)], quarter_rows(shards[index], rep), index)
         return remote(view, view, xy_send.at[slot], xy_recv.at[slot], along_dp(step))
 
     def far_copy(index, step, far):
         slot = (index, far - 1, step + 1)
-        count = shards[index].shape[0] // PARTS
+        count = shards[index].shape[-2] // PARTS
         rows = tile_rows(lax.bitwise_xor(rep, 3 - step) * count + (2 - step) * (count // 2), count // 2)
-        view = weights[index].at[core, turn_part(far), rows]
+        view = rows_view(weights[index].at[core, turn_part(far)], rows, index)
         return remote(view, view, xy_send.at[slot], xy_recv.at[slot], along_dp(step))
+
+    def across_copy(index, far):
+        slot = (index, far - 1, 2)
+        view = rows_view(weights[index].at[core, turn_part(far)], quarter_rows(shards[index], rep), index)
+        return remote(view, view, xy_send.at[slot], xy_recv.at[slot], along_dp(3))
 
     def sib_copy(index, far):
         target = weights[index].at[core, turn_part(far)]
@@ -1080,13 +1099,20 @@
 
     def z_start(far, *which):
         for index in which:
-            z_copy(index, PARTS - far).start()
-
-    def xy_start(far, *which):
+            if far < 3 or index == VEC:
+                z_copy(index, far).start()
+            else:
+                pl.when(jnp.logical_not(ends()))(z_copy(index, far).start)
+
+    def near_start(far, *which):
         for index in which:
-            z_copy(index, PARTS - far).wait_recv()
+            z_copy(index, far).wait_recv()
+            if far == 2:
+                pl.when(jnp.logical_not(ends()))(pass_copy(index).start)
             for step in (1, 2):
                 near_copy(index, step, far).start()
+            if index in DIRECT:
+                pl.when(core == 0)(across_copy(index, far).start)
 
     def far_start(far, *which):
         for index in which:
@@ -1094,11 +1120,25 @@
                 near_copy(index, 3 - step, far).wait_recv()
                 far_copy(index, step, far).start()
 
-    def sib_start(far, *which):
+    def sib_direct(far, *which):
+        for index in which:
+            for step in (1, 2):
+                near_copy(index, step, far).wait_recv()
+            across_copy(index, far).wait_recv()
+            sib_copy(index, far).start()
+
+    def sib_passed(far, *which):
         for index in which:
             for step in (1, 2):
                 far_copy(index, step, far).wait_recv()
             sib_copy(index, far).start()
+
+    def sib_start(far, *which):
+        direct = [index for index in which if index in DIRECT]
+        passed = [index for index in which if index not in DIRECT]
+        pl.when(core == 0)(partial(sib_direct, far, *direct))
+        pl.when(core == 0)(partial(sib_passed, far, *passed))
+        pl.when(core == 1)(partial(sib_passed, far, *which))
 
     def need(layer, far, *which):
         @pl.when(core != layer)
@@ -1173,7 +1213,7 @@
             copies.append(remote(view, view, kv_send.at[layer, pair, slot], kv_recv.at[layer, pair, slot], sibling()))
         return copies
 
-    actions = {"own": own_start, "z": z_start, "near": xy_start, "far": far_start, "sib": sib_start}
+    actions = {"own": own_start, "z": z_start, "near": near_start, "far": far_start, "sib": sib_start}
 
     def run(point, turn=None):
         for where, when, owner_core, name, fars, which in FORWARD_PLAN:
@@ -1263,11 +1303,20 @@
     rows_arrived(1)
     for index in range(5):
         for step in steps:
-            z_copy(index, step).wait_send()
+            if step < 3 or index == VEC:
+                z_copy(index, step).wait_send()
+            else:
+                pl.when(jnp.logical_not(ends()))(z_copy(index, step).wait_send)
+                pl.when(jnp.logical_not(ends()))(pass_copy(index).wait_send)
             if index != VEC:
                 for way in (1, 2):
                     near_copy(index, way, step).wait_send()
-                    far_copy(index, way, step).wait_send()
+                    if index in DIRECT:
+                        pl.when(core == 1)(far_copy(index, way, step).wait_send)
+                    else:
+                        far_copy(index, way, step).wait_send()
+                if index in DIRECT:
+                    pl.when(core == 0)(across_copy(index, step).wait_send)
                 sib_copy(index, step).wait_send()
         sib_copy(index, 0).wait_send() if index != VEC else vec_copy().wait_send()
     for layer in range(2):
@@ -1288,10 +1337,10 @@
 
 def backward_kernel(lens_ref, dy_in, y_in, *refs):
     saved_in, weights_in, refs = refs[:11], refs[11:16], refs[16:]
-    grads_out, vec_out, blocks_out, rows_out, refs = *refs[:4], refs[4:]
+    down_out, up_out, out_out, qkv_out, vec_out, bias_out, blocks_out, rows_out, refs = *refs[:8], refs[8:]
     held, weights, refs = refs[:11], refs[11:16], refs[16:]
     dy_low, dy_ref, bias_ref, grads_ref, vec_grad, low, low_t, chunk, total, grad_hidden, grad_att, centres, grad_query, grad_kv, kv_out, kv_got, grad_low, refs = *refs[:17], refs[17:]
-    got_core, got_first, got_second, part_sum, got_part, final, vec_core, vec_chip, vec_dp, vec_rep, vec_part, refs = *refs[:11], refs[11:]
+    got_core, got_first, got_second, part_sum, got_part, final, vec_core, vec_chip, vec_dp, vec_rep, vec_part, grads_out, vec_total, refs = *refs[:13], refs[13:]
     load_sem, weight_sem, dy_sem, y_send, y_recv, row_send, row_recv, kv_send, kv_recv, core_send, core_recv, first_send, first_recv, second_send, second_recv, part_send, part_recv, vec_send, vec_recv, last_send, last_recv = refs
     core, rep, part = place()
     steps = (1, 2, 3)
@@ -1317,7 +1366,7 @@
     dy_copy.start()
     for group in (chunk_set, norm_set, attend_set, project_set):
         start(load(1, *group))
-    greet(all_partners() + [(1 - core, rep, lax.rem(part + step, PARTS)) for step in steps])
+    greet(all_partners() + [(1 - core, rep, lax.bitwise_xor(part, step)) for step in steps])
 
     owner = jnp.where((part == 0) | (part == 3), 0, 1)
 
@@ -1447,7 +1496,6 @@
 
         def during_chunk(turn):
             pl.when(turn > 0)(lambda: dp_start(layer, FEED, turn - 1))
-            at(turn, 3, dp_next, layer, FEED, 0)
             if layer == 0:
                 at(turn, 0, dp_next, 1, ATTEND, 1)
                 at(turn, 0, dp_next, 1, ATTEND, 2)
@@ -1455,7 +1503,6 @@
                 at(turn, 1, part_start, 1, ATTEND, 0)
                 at(turn, 2, part_start, 1, ATTEND, 1)
                 at(turn, 2, part_start, 1, ATTEND, 2)
-                at(turn, 2, finish, 1, FEED)
                 at(turn, 3, part_start, 1, ATTEND, 3)
 
         def after_chunk(turn, chunk):
@@ -1466,7 +1513,7 @@
 
         def after_norm():
             dp_start(layer, FEED, 3)
-            dp_next(layer, FEED, 1)
+            dp_next(layer, FEED, 0)
 
         feed_back(dy_ref, act, slope, down, up, hidden, normed_two_t, vec, out, attended, attended_t, grad_hidden, grad_att, centres, grads_ref, vec_grad.at[layer], low, low_t, chunk, total, during_chunk, after_chunk, before_norm, after_norm)
         if layer == 1:
@@ -1474,15 +1521,13 @@
         wait(load(layer, *attend_set))
 
         def before_attend(turn):
-            at(turn, 0, dp_next, layer, FEED, 2)
-            at(turn, 1, dp_next, layer, FEED, 3)
-            at(turn, 1, part_start, layer, FEED, 0)
-            at(turn, 1, part_start, layer, FEED, 1)
-            at(turn, 2, part_start, layer, FEED, 2)
-            at(turn, 3, part_start, layer, FEED, 3)
+            for index in range(3):
+                at(turn, index, dp_next, layer, FEED, index + 1)
+                at(turn, index + 1, part_start, layer, FEED, index)
             if layer == 0:
-                at(turn, 0, finish, 1, ATTEND)
-                at(turn, 0, hand_over, 1)
+                at(turn, 3, finish, 1, FEED)
+                at(turn, 3, finish, 1, ATTEND)
+                at(turn, 3, hand_over, 1)
 
         def project_turn(turn):
             pair = turn_part(turn + 1)
@@ -1502,6 +1547,7 @@
         if layer == 1:
             start(load(0, *attend_set))
         dp_start(layer, ATTEND, 2)
+        part_start(layer, FEED, 3)
         project_turn(PAIRS - 1)
         project_back_norm(x_ref, grad_hidden, vec, dy_ref, grad_low.at[layer], vec_grad.at[layer], total)
         if layer == 1:
@@ -1527,7 +1573,12 @@
     finish(0, ATTEND)
     hand_over(0)
     wait(vec_copies)
-    vec_out[...] = vec_rep[...] + vec_part[0] + vec_part[1] + vec_part[2]
+    vec_total[...] = vec_rep[...] + vec_part[0] + vec_part[1] + vec_part[2]
+    own = rep * PARTS + part
+    vec_out[...] = pltpu.roll(vec_total[:8, :], 512 - own * 32, 1)[:, :128]
+    columns = vec_total[:, tile_rows(rep * 128, 128)]
+    row = lax.broadcasted_iota(jnp.int32, columns.shape, 0)
+    bias_out[...] = column_sum(jnp.where(row == 6 + part, columns, 0.0))
     deliver(saved_in[0].at[1], 0, blocks_out, y_send, y_recv, "wait")
     deliver(y_in, 1, blocks_out, y_send, y_recv, "wait")
     delivered(blocks_out, y_in, y_send, y_recv)
@@ -1536,6 +1587,11 @@
     delivered(rows_out, grad_low.at[0], row_send, row_recv)
     last_copy(0).wait_recv()
     last_copy(0).wait_send()
+    down_out[...] = grads_out[:, :512].T
+    up_out[...] = grads_out[:, 512:1024]
+    out_out[...] = grads_out[:, 1024:1152]
+    for kind in range(3):
+        qkv_out[kind] = grads_out[:, 1152 + kind * 128 : 1280 + kind * 128]
 
 
 def specs(space, count):
@@ -1577,14 +1633,14 @@
 ):
     f32, low = jnp.float32, jnp.bfloat16
     core, rep, part = place()
-    vec = jnp.concatenate([ln_one_gain, ln_one_bias, out_bias, ln_two_gain, ln_two_bias, down_bias, up_bias, jnp.zeros_like(up_bias)])
+    vectors = (ln_one_gain, ln_one_bias, out_bias, ln_two_gain, ln_two_bias, down_bias, up_bias)
     rows, rows_low = ((OWN, WIDTH), f32), ((OWN, WIDTH), low)
     square = ((BLOCK, BLOCK), f32)
     results = kernel_call(
         forward_kernel,
         "forward",
-        (lengths, tokens, cotangent, qkv_weight.reshape(WIDTH, 384), out_weight[0], up_weight[0], down_weight[0], vec),
-        specs(pltpu.SMEM, 1) + specs(pl.ANY, 7),
+        (lengths, tokens, cotangent, qkv_weight[0].transpose(1, 0, 2), out_weight[0], up_weight[0], down_weight[0], *vectors),
+        specs(pltpu.SMEM, 1) + specs(pl.ANY, 6) + specs(pltpu.VMEM, 7),
         (rows_low, rows_low, *twice(SAVED), *twice(WEIGHTS)),
         specs(pl.ANY, 18),
         (
@@ -1598,6 +1654,7 @@
             ((2, BLOCK, 128), f32),
             rows,
             rows,
+            ((8, 512), f32),
             (2, 4),
             (2, 2),
             (2,),
@@ -1612,16 +1669,26 @@
             (2, PAIRS, 2),
             (2, 11),
             (2, 5),
+            (4,),
         ),
         0,
     )
-    grads, vec_sum, block_outputs, grad_rows = kernel_call(
+    down_grad, up_grad, out_grad, qkv_grad, spread, up_bias_grad, block_outputs, grad_rows = kernel_call(
         backward_kernel,
         "backward",
         (lengths, *results),
         specs(pltpu.SMEM, 1) + specs(pl.ANY, 18),
-        (((128, 1536), f32), ((16, 512), f32), ((PARTS, BLOCK, WIDTH), low), ((PARTS, BLOCK, WIDTH), low)),
-        specs(pltpu.VMEM, 2) + specs(pl.ANY, 2),
+        (
+            ((512, 128), f32),
+            ((128, 512), f32),
+            ((128, 128), f32),
+            ((3, 128, 128), f32),
+            ((8, 128), f32),
+            ((1, 128), f32),
+            ((PARTS, BLOCK, WIDTH), low),
+            ((PARTS, BLOCK, WIDTH), low),
+        ),
+        specs(pltpu.VMEM, 6) + specs(pl.ANY, 2),
         (
             *SAVED,
             *WEIGHTS,
@@ -1653,6 +1720,8 @@
             ((3, 16, 512), f32),
             ((16, 512), f32),
             ((3, 16, 512), f32),
+            ((128, 1536), f32),
+            ((16, 512), f32),
             (11,),
             (5,),
             (1,),
@@ -1677,22 +1746,21 @@
         ),
         1,
     )
-    spread = lax.dynamic_slice_in_dim(vec_sum, (rep * PARTS + part) * 32, 32, 1)
-    up_bias_grad = lax.dynamic_slice(vec_sum, (6 + part, rep * 128), (1, 128))
+    vector_grads = [spread[row : row + 1, :32] for row in range(6)]
     return (
         block_outputs[None],
         grad_rows.astype(f32)[None],
-        spread[0:1],
-        spread[1:2],
-        grads[:, 1152:].reshape(1, 128, 3, 128),
-        grads[None, :, 1024:1152],
-        spread[2:3],
-        spread[3:4],
-        spread[4:5],
-        grads[None, :, 512:1024],
+        vector_grads[0],
+        vector_grads[1],
+        qkv_grad.transpose(1, 0, 2)[None],
+        out_grad[None],
+        vector_grads[2],
+        vector_grads[3],
+        vector_grads[4],
+        up_grad[None],
         up_bias_grad[None],
-        grads[:, :512].T[None],
-        spread[5:6],
+        down_grad[None],
+        vector_grads[5],
     )
 
 

time: 208 us -> 196 us (0.942)
  Pallas kernels: 194 us -> 187 us
  local copies, waits for them, and re-layouts: 10.4 us -> 5.65 us
    pallas_call x2, Pallas kernels: 194 us -> 187 us  [kernel_call(): pl.pallas_call(body, out_shape=[jax.ShapeDtypeStruct(shape, kind) for sha...]
    broadcast_in_dim x4 -> x0, local copies, waits for them, and re-layouts: 2.64 us -> none  [the longest x1 1.26 us: on_device_whole(): up_bias_grad[None]]
    unnamed x8 -> x18, local copies, waits for them, and re-layouts: 3.8 us -> 4.22 us
where the time goes in v4:
time: 196 us
  Pallas kernels  187 us (95%)
  local copies, waits for them, and re-layouts  5.65 us (3%)
  other arithmetic  2.88 us (1%)
    pallas_call x2, Pallas kernels, kernel_call(): pl.pallas_call(body, out_shape=[jax.ShapeDtypeStruct(shape, kind) for sha...  187 us
    unnamed x18, local copies, waits for them, and re-layouts  4.22 us

profile of v4, /device:TPU:0, one launch (start us, length us, event | category | flops | bytes accessed | tf_op | source)
XLA Modules:
  0.0 196.2 jit_solution(2489623994035945655)
XLA Ops:
  0.6 86.1 %forward.1 = (bf16[512,512]{1,0:T(8,128)(2,1)}, bf16[512,512]{1,0:T(8,128)(2,1)}, bf16[2,512,512]{2,1,0:T(8,128)(2,1)}, bf16[2,512,512]{2,1,0:T(8,128)(2,1)}, bf...) custom-call(s32[4,8]{1,0:T(4,128)} %lens_ref.3, ...), custom_call_target="tpu_custom_call" | custom-call | tf_op jit(solution)/shard_map/forward/pallas_call | solution.py:1603
  86.8 100.9 %backward.1 = (f32[512,128]{1,0:T(8,128)}, f32[128,512]{1,0:T(8,128)}, f32[128,128]{1,0:T(8,128)}, f32[3,128,128]{2,1,0:T(8,128)}, f32[8,128]{1,0:T(8,128)}, /*i...) custom-call(s32[4,8]{1,0:T(4,128)} %lens_ref.3, ...), custom_call_target="tpu_custom_call" | custom-call | tf_op jit(solution)/shard_map/backward/pallas_call | solution.py:1603
  187.7 0.0 copy-start
  187.7 0.0 copy-start.3
  187.7 0.0 copy-start.4
  187.7 0.0 copy-start.2
  187.7 1.4 fusion
  189.1 0.0 copy-start.5
  189.1 0.0 copy-start.1
  189.1 2.9 %bitcast_convert_fusion = f32[1,4,256,512]{3,2,1,0:T(8,128)} fusion(bf16[4,256,512]{2,1,0:T(8,128)(2,1)} %get-tuple-element.58), kind=kLoop, calls=%fused_computation | loop fusion | flops 524288 | bytes 3145728 | tf_op jit(solution)/shard_map/broadcast_in_dim | solution.py:1752
  192.0 0.0 copy-done
  192.0 1.0 copy.33
  193.0 0.0 copy-done.3
  193.0 0.7 copy.34
  193.7 0.0 copy-done.4
  193.7 0.6 copy.35
  194.3 0.0 copy-done.2
  194.3 0.7 copy.36
  195.0 0.0 copy-done.5
  195.0 0.5 copy.37
  195.5 0.0 copy-done.1
  195.5 0.7 copy.38
Async XLA Ops:
  187.7 4.4 %copy-start = (bf16[4,256,512]{2,1,0:T(8,128)(2,1)S(1)}, bf16[4,256,512]{2,1,0:T(8,128)(2,1)}, u32[]{:S(2)}) copy-start(bf16[4,256,512]{2,1,0:T(8,128)(2,1)} %get-tuple-element.57) | copy-start | bytes 3145732
  187.7 5.3 %copy-start.3 = (f32[3,128,128]{2,1,0:T(8,128)S(1)}, f32[3,128,128]{2,1,0:T(8,128)}, u32[]{:S(2)}) copy-start(f32[3,128,128]{2,1,0:T(8,128)} %get-tuple-element.60) | copy-start | bytes 589828
  187.7 6.0 %copy-start.4 = (f32[128,128]{1,0:T(8,128)S(1)}, f32[128,128]{1,0:T(8,128)}, u32[]{:S(2)}) copy-start(f32[128,128]{1,0:T(8,128)} %get-tuple-element.61) | copy-start | bytes 196612
  187.7 6.6 %copy-start.2 = (f32[128,512]{1,0:T(8,128)S(1)}, f32[128,512]{1,0:T(8,128)}, u32[]{:S(2)}) copy-start(f32[128,512]{1,0:T(8,128)} %get-tuple-element.62) | copy-start | bytes 786436
  189.1 5.9 %copy-start.5 = (f32[1,128]{1,0:T(1,128)S(1)}, f32[1,128]{1,0:T(1,128)}, u32[]{:S(2)}) copy-start(f32[1,128]{1,0:T(1,128)} %get-tuple-element.63) | copy-start | bytes 1540
  189.1 6.4 %copy-start.1 = (f32[512,128]{1,0:T(8,128)S(1)}, f32[512,128]{1,0:T(8,128)}, u32[]{:S(2)}) copy-start(f32[512,128]{1,0:T(8,128)} %get-tuple-element.64) | copy-start | bytes 786436

commit v5 on v4

--- a/solution.py
+++ b/solution.py
@@ -661,47 +661,46 @@
     def pair_step(turn, carry):
         pair = turn_part(turn)
         before_pair(turn, pair)
-        outs = [[None, None], [None, None]]
-        for parity in range(2):
-            tops = []
-            for task in range(TASKS):
-                rows = tile_rows(slots[task] * BLOCK, BLOCK)
-                key_rows = tile_rows(keys[task] * BLOCK, BLOCK)
-                scores = dot(query_ref[pair, parity, rows, :], kv_ref[0, pair, key_rows, :], BOTH_LAST)
-                if signed:
-                    raised = scores * scores + 1.0
-                    inverse = lax.rsqrt(raised)
-                    factor_ref[task] = scores * inverse
-                    scores = raised * inverse
-                logits = scores + bias_ref[task]
-                logit_ref[task] = logits
-                tops.append(jnp.maximum(logits[:, :128], logits[:, 128:]))
-            low = jnp.full((BLOCK, 128), NEGATIVE, jnp.float32)
-            top_early = jnp.maximum(tops[0], jnp.where(middle_late, low, tops[1]))
-            top_late = jnp.maximum(jnp.maximum(tops[2], tops[3]), jnp.maximum(tops[4], jnp.where(middle_late, tops[1], low)))
-            max_early = jnp.max(top_early, axis=-1, keepdims=True)
-            max_late = jnp.max(top_late, axis=-1, keepdims=True)
-            max_middle = jnp.where(middle_late, max_late, max_early)
-            shifts = (max_early, max_middle, max_late, max_late, max_late)
-            sums, terms = [], []
-            for task in range(TASKS):
-                key_rows = tile_rows(keys[task] * BLOCK, BLOCK)
-                powers = jnp.exp(logit_ref[task] - shifts[task])
-                sums.append(powers[:, :128] + powers[:, 128:])
-                if signed:
-                    powers = powers * factor_ref[task]
-                terms.append(dot(powers.astype(jnp.bfloat16), kv_ref[1, pair, key_rows, :]))
-            early = jnp.where(middle_late, 0.0, 1.0)
-            late = 1.0 - early
-            totals = (sums[0] + sums[1] * early, sums[2] + sums[3] + sums[4] + sums[1] * late)
-            values = (terms[0] + terms[1] * early, terms[2] + terms[3] + terms[4] + terms[1] * late)
-            for slot, top in enumerate((max_early, max_late)):
-                total = jnp.sum(totals[slot], axis=-1, keepdims=True)
-                outs[slot][parity] = values[slot] / total
-                head = pair * 2 + parity
-                stat_ref[slot] = jnp.where(lane == head, top + jnp.log(total), stat_ref[slot])
-        for slot in range(2):
-            merged = jnp.where(lane < HEAD, outs[slot][0], outs[slot][1])
+        tops = []
+        for task in range(TASKS):
+            rows = tile_rows(slots[task] * BLOCK, BLOCK)
+            key_rows = tile_rows(keys[task] * BLOCK, BLOCK)
+            queries = query_ref[pair, :, rows, :].reshape(2 * BLOCK, 128)
+            scores = dot(queries, kv_ref[0, pair, key_rows, :], BOTH_LAST)
+            if signed:
+                raised = scores * scores + 1.0
+                inverse = lax.rsqrt(raised)
+                factor_ref[task] = scores * inverse
+                scores = raised * inverse
+            logits = scores + jnp.concatenate([bias_ref[task]] * 2, axis=0)
+            logit_ref[task] = logits
+            tops.append(jnp.maximum(logits[:, :128], logits[:, 128:]))
+        low = jnp.full((2 * BLOCK, 128), NEGATIVE, jnp.float32)
+        top_early = jnp.maximum(tops[0], jnp.where(middle_late, low, tops[1]))
+        top_late = jnp.maximum(jnp.maximum(tops[2], tops[3]), jnp.maximum(tops[4], jnp.where(middle_late, tops[1], low)))
+        max_early = jnp.max(top_early, axis=-1, keepdims=True)
+        max_late = jnp.max(top_late, axis=-1, keepdims=True)
+        max_middle = jnp.where(middle_late, max_late, max_early)
+        shifts = (max_early, max_middle, max_late, max_late, max_late)
+        sums, terms = [], []
+        for task in range(TASKS):
+            key_rows = tile_rows(keys[task] * BLOCK, BLOCK)
+            powers = jnp.exp(logit_ref[task] - shifts[task])
+            sums.append(powers[:, :128] + powers[:, 128:])
+            if signed:
+                powers = powers * factor_ref[task]
+            terms.append(dot(powers.astype(jnp.bfloat16), kv_ref[1, pair, key_rows, :]))
+        early = jnp.where(middle_late, 0.0, 1.0)
+        late = 1.0 - early
+        totals = (sums[0] + sums[1] * early, sums[2] + sums[3] + sums[4] + sums[1] * late)
+        values = (terms[0] + terms[1] * early, terms[2] + terms[3] + terms[4] + terms[1] * late)
+        for slot, top in enumerate((max_early, max_late)):
+            total = jnp.sum(totals[slot], axis=-1, keepdims=True)
+            outs = values[slot] / total
+            logs = top + jnp.log(total)
+            for parity in range(2):
+                stat_ref[slot] = jnp.where(lane == pair * 2 + parity, logs[parity * BLOCK : (parity + 1) * BLOCK], stat_ref[slot])
+            merged = jnp.where(lane < HEAD, outs[:BLOCK], outs[BLOCK:])
             attended_ref[pair, slot * BLOCK : (slot + 1) * BLOCK, :] = merged
             attended_t_ref[pair, :, slot * BLOCK : (slot + 1) * BLOCK] = merged.T.astype(jnp.bfloat16)
         return carry
@@ -810,7 +809,7 @@
     between()
     row = lax.broadcasted_iota(jnp.int32, (8, 128), 0)
     lane = lax.broadcasted_iota(jnp.int32, (8, 128), 1)
-    picks = jnp.where((row < 2) & ((lane < HEAD) == (row == 0)), 1.0, 0.0)
+    picks = jnp.where((row < 2) & ((lane < HEAD) == (row == 0)), 1.0, 0.0).astype(jnp.bfloat16)
 
     def pair_step(pair, carry):
         out_term = dot(attended_t_ref[pair], low_ref[...]).astype(jnp.bfloat16)
@@ -820,8 +819,10 @@
         wide = grad_att.astype(jnp.float32)
         for parity in range(2):
             grad_att_ref[pair, parity] = keep_head(wide, parity).astype(jnp.bfloat16)
-        centres = lax.dot_general(picks, wide * attended_ref[pair], BOTH_LAST, precision=lax.Precision.HIGHEST, preferred_element_type=jnp.float32)
-        centre_ref[pair] = centres
+        products = wide * attended_ref[pair]
+        upper = products.astype(jnp.bfloat16)
+        lower = (products - upper.astype(jnp.float32)).astype(jnp.bfloat16)
+        centre_ref[pair] = dot(picks, upper, BOTH_LAST) + dot(picks, lower, BOTH_LAST)
         return carry
 
     lax.fori_loop(0, PAIRS, pair_step, 0)
@@ -832,51 +833,45 @@
     slots, keys = task_plan(core)
     early = jnp.where(core == 0, 0.0, 1.0)
     lane = lax.broadcasted_iota(jnp.int32, (BLOCK, 128), 1)
-    grad_kv_ref[...] = jnp.zeros_like(grad_kv_ref)
 
     def pair_step(turn, carry):
         pair = turn_part(turn + 1)
+        held = lax.rem(turn, 2)
         before_pair(turn)
-        parts = [[None] * TASKS, [None] * TASKS]
+        grad_kv_ref[held] = jnp.zeros(grad_kv_ref.shape[1:], jnp.float32)
+        merged = []
         for task in range(TASKS):
             rows = tile_rows(slots[task] * BLOCK, BLOCK)
             key_rows = tile_rows(keys[task] * BLOCK, BLOCK)
             key_part, value_part = kv_ref[0, pair, key_rows, :], kv_ref[1, pair, key_rows, :]
-            key_term, value_term = None, None
-            for parity in range(2):
-                queries = query_ref[pair, parity, rows, :]
-                grad_att = grad_att_ref[pair, parity, rows, :]
-                scores = dot(key_part, queries, BOTH_LAST)
-                grad_weights = dot(value_part, grad_att, BOTH_LAST)
-                log_row = log_ref[slots[task], pl.ds(pair * 2 + parity, 1), :]
-                centre = centre_ref[pair, parity : parity + 1, rows]
-                if signed:
-                    raised = scores * scores + 1.0
-                    inverse = lax.rsqrt(raised)
-                    factor = scores * inverse
-                    probs = jnp.exp(raised * inverse + bias_ref[task] - log_row)
-                    weights = factor * probs
-                    grad_scores = weights * (factor * grad_weights - centre)
-                    grad_scores = grad_scores + probs * grad_weights * (inverse * inverse * inverse)
-                else:
-                    weights = jnp.exp(scores + bias_ref[task] - log_row)
-                    grad_scores = weights * (grad_weights - centre)
-                grad_low = grad_scores.astype(jnp.bfloat16)
-                new_key = dot(grad_low, queries)
-                new_value = dot(weights.astype(jnp.bfloat16), grad_att)
-                key_term = new_key if parity == 0 else key_term + new_key
-                value_term = new_value if parity == 0 else value_term + new_value
-                parts[parity][task] = dot(grad_low, key_part, BOTH_FIRST)
-            grad_kv_ref[0, pair, key_rows, :] += key_term
-            grad_kv_ref[1, pair, key_rows, :] += value_term
-        merged = []
-        for task in range(TASKS):
-            merged.append(jnp.where(lane < HEAD, parts[0][task], parts[1][task]))
+            queries = query_ref[pair, :, rows, :].reshape(2 * BLOCK, 128)
+            grad_att = grad_att_ref[pair, :, rows, :].reshape(2 * BLOCK, 128)
+            scores = dot(key_part, queries, BOTH_LAST)
+            grad_weights = dot(value_part, grad_att, BOTH_LAST)
+            log_row = jnp.concatenate([log_ref[slots[task], pl.ds(pair * 2 + parity, 1), :] for parity in range(2)], axis=1)
+            centre = jnp.concatenate([centre_ref[pair, parity : parity + 1, rows] for parity in range(2)], axis=1)
+            bias = jnp.concatenate([bias_ref[task]] * 2, axis=1)
+            if signed:
+                raised = scores * scores + 1.0
+                inverse = lax.rsqrt(raised)
+                factor = scores * inverse
+                probs = jnp.exp(raised * inverse + bias - log_row)
+                weights = factor * probs
+                grad_scores = weights * (factor * grad_weights - centre)
+                grad_scores = grad_scores + probs * grad_weights * (inverse * inverse * inverse)
+            else:
+                weights = jnp.exp(scores + bias - log_row)
+                grad_scores = weights * (grad_weights - centre)
+            grad_low = grad_scores.astype(jnp.bfloat16)
+            grad_kv_ref[held, 0, key_rows, :] += dot(grad_low, queries)
+            grad_kv_ref[held, 1, key_rows, :] += dot(weights.astype(jnp.bfloat16), grad_att)
+            grad_query = dot(grad_low, key_part, BOTH_FIRST)
+            merged.append(jnp.where(lane < HEAD, grad_query[:BLOCK], grad_query[BLOCK:]))
         grad_query_ref[pair, :BLOCK, :] = ((merged[0] + merged[1] * early) * 0.125).astype(jnp.bfloat16)
         grad_query_ref[pair, BLOCK:, :] = ((merged[1] * (1.0 - early) + merged[2] + merged[3] + merged[4]) * 0.125).astype(jnp.bfloat16)
         for slot, block in enumerate(blocks_of(1 - core)):
             for kind in range(2):
-                rows = grad_kv_ref[kind, pair, tile_rows(block * BLOCK, BLOCK), :]
+                rows = grad_kv_ref[held, kind, tile_rows(block * BLOCK, BLOCK), :]
                 send_ref[kind, pair, slot * BLOCK : (slot + 1) * BLOCK, :] = rows.astype(jnp.bfloat16)
         after_pair(turn, pair)
         return carry
@@ -884,12 +879,12 @@
     lax.fori_loop(0, PAIRS, pair_step, 0)
 
 
-def project_back_pair(pair, grad_query_ref, grad_kv_ref, other_ref, normed_t_ref, weight_ref, grads_ref, sum_ref, send):
+def project_back_pair(pair, held, grad_query_ref, grad_kv_ref, other_ref, normed_t_ref, weight_ref, grads_ref, sum_ref, send):
     parts = [grad_query_ref[pair]]
     for kind in range(2):
         halves = []
         for slot, block in enumerate(blocks_of(lax.axis_index("section"))):
-            own = grad_kv_ref[kind, pair, tile_rows(block * BLOCK, BLOCK), :]
+            own = grad_kv_ref[held, kind, tile_rows(block * BLOCK, BLOCK), :]
             halves.append(own + other_ref[kind, pair, slot * BLOCK : (slot + 1) * BLOCK, :].astype(jnp.float32))
         parts.append(jnp.concatenate(halves, axis=0).astype(jnp.bfloat16))
     grads = jnp.concatenate(parts, axis=1)
@@ -998,7 +993,7 @@
 
 
 ALL = (1, 2, 3)
-DIRECT = (QKV,)
+DIRECT = ((0, QKV),)
 FORWARD_PLAN = (
     ("masks", None, 0, "near", ALL, (QKV,)),
     ("masks", None, 0, "own", None, (QKV, OUT, UP, DOWN)),
@@ -1039,7 +1034,7 @@
     dy_out, y_out, saved_out, weights_out, refs = refs[0], refs[1], refs[2:13], refs[13:18], refs[18:]
     saved, weights, refs = refs[:11], refs[11:16], refs[16:]
     y_ref, bias_ref, normed, logit, factor, stat, wide, total, vec_own, refs = *refs[:9], refs[9:]
-    row_send, row_recv, row_local, z_send, z_recv, xy_send, xy_recv, sib_send, sib_recv, local, kv_send, kv_recv, save_sem, keep_sem, pass_send = refs
+    row_send, row_recv, row_local, z_send, z_recv, xy_send, xy_recv, sib_send, sib_recv, local, kv_send, kv_recv, save_sem, keep_sem, pass_send, chunk_sem = refs
     core, rep, part = place()
     shards = (*shards, vec_own)
     vec_own[...] = jnp.zeros_like(vec_own)
@@ -1111,8 +1106,9 @@
                 pl.when(jnp.logical_not(ends()))(pass_copy(index).start)
             for step in (1, 2):
                 near_copy(index, step, far).start()
-            if index in DIRECT:
-                pl.when(core == 0)(across_copy(index, far).start)
+            for layer in range(2):
+                if (layer, index) in DIRECT:
+                    pl.when(core == layer)(across_copy(index, far).start)
 
     def far_start(far, *which):
         for index in which:
@@ -1134,11 +1130,9 @@
             sib_copy(index, far).start()
 
     def sib_start(far, *which):
-        direct = [index for index in which if index in DIRECT]
-        passed = [index for index in which if index not in DIRECT]
-        pl.when(core == 0)(partial(sib_direct, far, *direct))
-        pl.when(core == 0)(partial(sib_passed, far, *passed))
-        pl.when(core == 1)(partial(sib_passed, far, *which))
+        for layer in range(2):
+            pl.when(core == layer)(partial(sib_direct, far, *[index for index in which if (layer, index) in DIRECT]))
+            pl.when(core == layer)(partial(sib_passed, far, *[index for index in which if (layer, index) not in DIRECT]))
 
     def need(layer, far, *which):
         @pl.when(core != layer)
@@ -1205,6 +1199,13 @@
     def save(layer, *which):
         for index in which:
             pltpu.make_async_copy(saved[index].at[layer], saved_out[index].at[layer], save_sem.at[layer, index]).start()
+
+    def chunk_copies(layer, turn):
+        chunk = turn_part(turn)
+        return [
+            pltpu.make_async_copy(saved[index].at[layer, chunk], saved_out[index].at[layer, chunk], chunk_sem.at[layer, index - 9, turn])
+            for index in (9, 10)
+        ]
 
     def kv_copies(layer, pair, receiving):
         copies = []
@@ -1227,7 +1228,7 @@
                     rows_each(1, "start")
                 else:
                     for far in fars:
-                        actions[name](far, *which)
+                        actions[name](far, *[index for index in which if name != "far" or (owner_core, index) not in DIRECT])
 
             here = core == owner_core if owner_core is not None else None
             if turn is not None:
@@ -1276,6 +1277,7 @@
             need_turn(layer, turn, OUT)
 
         def before_feed():
+            save(layer, 7, 8)
             run(f"second{layer}")
 
         def before_chunk(turn):
@@ -1284,6 +1286,8 @@
                 pl.when(turn == PARTS - 1)(partial(keep, 1, OUT, UP, DOWN))
 
         def during_chunk(turn):
+            for copy in chunk_copies(layer, turn):
+                copy.start()
             run(f"chunk{layer}", turn)
 
         project(x_ref, vec, qkv, normed_one_t, queries, kv, normed, after_norm, before_project, push_kv)
@@ -1294,7 +1298,6 @@
         run(f"attended{layer}")
         target = saved[0].at[1] if layer == 0 else y_ref
         feed(x_ref, attended, vec, out, up, down, hidden, normed_two_t, act, slope, target, normed, wide, total, before_out, before_feed, before_chunk, during_chunk)
-        save(layer, 7, 8, 9, 10)
         if layer == 0:
             keep(0, OUT, UP, DOWN)
     y_copy = pltpu.make_async_copy(y_ref, y_out, row_local.at[0])
@@ -1311,20 +1314,23 @@
             if index != VEC:
                 for way in (1, 2):
                     near_copy(index, way, step).wait_send()
-                    if index in DIRECT:
-                        pl.when(core == 1)(far_copy(index, way, step).wait_send)
-                    else:
-                        far_copy(index, way, step).wait_send()
-                if index in DIRECT:
-                    pl.when(core == 0)(across_copy(index, step).wait_send)
+                    for layer in range(2):
+                        if (layer, index) not in DIRECT:
+                            pl.when(core == layer)(far_copy(index, way, step).wait_send)
+                for layer in range(2):
+                    if (layer, index) in DIRECT:
+                        pl.when(core == layer)(across_copy(index, step).wait_send)
                 sib_copy(index, step).wait_send()
         sib_copy(index, 0).wait_send() if index != VEC else vec_copy().wait_send()
     for layer in range(2):
         for pair in range(PAIRS):
             for copy in kv_copies(layer, pair, False):
                 copy.wait_send()
-        for index in range(11):
+        for index in range(9):
             pltpu.make_async_copy(saved[index].at[layer], saved_out[index].at[layer], save_sem.at[layer, index]).wait()
+        for turn in range(PARTS):
+            for copy in chunk_copies(layer, turn):
+                copy.wait()
     y_copy.wait()
     for layer in range(2):
         for index in range(5):
@@ -1426,9 +1432,8 @@
         other = turn_part(turn + 1)
 
         def add(major, carry):
-            own = grads_ref[major, other, mine, first:last].astype(jnp.float32)
-            sum_here = own + got_core[layer, major, other, :, first:last].astype(jnp.float32)
-            got_core[layer, major, other, :, first:last] = sum_here.astype(jnp.bfloat16)
+            own = grads_ref[major, other, mine, first:last]
+            got_core[layer, major, other, :, first:last] = own + got_core[layer, major, other, :, first:last]
             return carry
 
         lax.fori_loop(0, PARTS, add, 0)
@@ -1441,9 +1446,8 @@
             for piece in (1, 0):
                 first_copy(layer, group, turn, way, piece).wait()
                 major = lax.bitwise_xor(rep, 3 - way) if piece else rep
-                own = got_core[layer, major, other, halves(way), first:last].astype(jnp.float32)
-                sum_here = own + got_first[layer, way - 1, piece, other, :, first:last].astype(jnp.float32)
-                got_core[layer, major, other, halves(way), first:last] = sum_here.astype(jnp.bfloat16)
+                own = got_core[layer, major, other, halves(way), first:last]
+                got_core[layer, major, other, halves(way), first:last] = own + got_first[layer, way - 1, piece, other, :, first:last]
                 if piece:
                     second_copy(layer, group, turn, way).start()
 
@@ -1452,9 +1456,8 @@
         other = turn_part(turn + 1)
         for way in (1, 2):
             second_copy(layer, group, turn, way).wait()
-            own = got_core[layer, rep, other, halves(way), first:last].astype(jnp.float32)
-            sum_here = own + got_second[layer, way - 1, other, :, first:last].astype(jnp.float32)
-            part_sum[layer, turn, halves(way), first:last] = sum_here.astype(jnp.bfloat16)
+            own = got_core[layer, rep, other, halves(way), first:last]
+            part_sum[layer, turn, halves(way), first:last] = own + got_second[layer, way - 1, other, :, first:last]
         if turn < PARTS - 1:
             part_copy(layer, group, turn).start()
 
@@ -1513,7 +1516,6 @@
 
         def after_norm():
             dp_start(layer, FEED, 3)
-            dp_next(layer, FEED, 0)
 
         feed_back(dy_ref, act, slope, down, up, hidden, normed_two_t, vec, out, attended, attended_t, grad_hidden, grad_att, centres, grads_ref, vec_grad.at[layer], low, low_t, chunk, total, during_chunk, after_chunk, before_norm, after_norm)
         if layer == 1:
@@ -1521,9 +1523,10 @@
         wait(load(layer, *attend_set))
 
         def before_attend(turn):
-            for index in range(3):
-                at(turn, index, dp_next, layer, FEED, index + 1)
-                at(turn, index + 1, part_start, layer, FEED, index)
+            for index in range(4):
+                at(turn, index, dp_next, layer, FEED, index)
+            at(turn, 2, part_start, layer, FEED, 0)
+            at(turn, 3, part_start, layer, FEED, 1)
             if layer == 0:
                 at(turn, 3, finish, 1, FEED)
                 at(turn, 3, finish, 1, ATTEND)
@@ -1532,7 +1535,7 @@
         def project_turn(turn):
             pair = turn_part(turn + 1)
             kv_copy(layer, pair).wait()
-            project_back_pair(pair, grad_query, grad_kv, kv_got.at[layer], normed_one_t, qkv, grads_ref, total, core_copy(layer, ATTEND, turn).start)
+            project_back_pair(pair, lax.rem(turn, 2), grad_query, grad_kv, kv_got.at[layer], normed_one_t, qkv, grads_ref, total, core_copy(layer, ATTEND, turn).start)
 
         def after_attend(turn, pair):
             kv_copy(layer, pair).start()
@@ -1547,8 +1550,9 @@
         if layer == 1:
             start(load(0, *attend_set))
         dp_start(layer, ATTEND, 2)
+        part_start(layer, FEED, 2)
+        project_turn(PAIRS - 1)
         part_start(layer, FEED, 3)
-        project_turn(PAIRS - 1)
         project_back_norm(x_ref, grad_hidden, vec, dy_ref, grad_low.at[layer], vec_grad.at[layer], total)
         if layer == 1:
             start(load(0, (0, 1), (QKV, VEC)))
@@ -1649,8 +1653,8 @@
             rows_low,
             ((TASKS, BLOCK, BLOCK), f32),
             rows_low,
-            ((TASKS, BLOCK, BLOCK), f32),
-            ((TASKS, BLOCK, BLOCK), f32),
+            ((TASKS, 2 * BLOCK, BLOCK), f32),
+            ((TASKS, 2 * BLOCK, BLOCK), f32),
             ((2, BLOCK, 128), f32),
             rows,
             rows,
@@ -1670,6 +1674,7 @@
             (2, 11),
             (2, 5),
             (4,),
+            (2, 2, PARTS),
         ),
         0,
     )
@@ -1705,7 +1710,7 @@
             ((PAIRS, 2, OWN, 128), low),
             ((PAIRS, 8, OWN), f32),
             ((PAIRS, OWN, 128), low),
-            ((2, PAIRS, 1024, 128), f32),
+            ((2, 2, 1024, 128), f32),
             ((2, PAIRS, OWN, 128), low),
             ((2, 2, PAIRS, OWN, 128), low),
             ((2, OWN, WIDTH), low),

time: 196 us -> 187 us (0.954)
  Pallas kernels: 187 us -> 178 us
    pallas_call x2, Pallas kernels: 187 us -> 178 us  [kernel_call(): pl.pallas_call(body, out_shape=[jax.ShapeDtypeStruct(shape, kind) for sha...]
where the time goes in v5:
time: 187 us
  Pallas kernels  178 us (95%)
  local copies, waits for them, and re-layouts  5.65 us (3%)
  other arithmetic  2.88 us (2%)
    pallas_call x2, Pallas kernels, kernel_call(): pl.pallas_call(body, out_shape=[jax.ShapeDtypeStruct(shape, kind) for sha...  178 us
    unnamed x18, local copies, waits for them, and re-layouts  4.22 us

profile of v5, /device:TPU:0, one launch (start us, length us, event | category | flops | bytes accessed | tf_op | source)
XLA Modules:
  0.0 187.0 jit_solution(3026686781737439711)
XLA Ops:
  0.6 84.5 %forward.1 = (bf16[512,512]{1,0:T(8,128)(2,1)}, bf16[512,512]{1,0:T(8,128)(2,1)}, bf16[2,512,512]{2,1,0:T(8,128)(2,1)}, bf16[2,512,512]{2,1,0:T(8,128)(2,1)}, bf...) custom-call(s32[4,8]{1,0:T(4,128)} %lens_ref.3, ...), custom_call_target="tpu_custom_call" | custom-call | tf_op jit(solution)/shard_map/forward/pallas_call | solution.py:1607
  85.2 93.3 %backward.1 = (f32[512,128]{1,0:T(8,128)}, f32[128,512]{1,0:T(8,128)}, f32[128,128]{1,0:T(8,128)}, f32[3,128,128]{2,1,0:T(8,128)}, f32[8,128]{1,0:T(8,128)}, /*i...) custom-call(s32[4,8]{1,0:T(4,128)} %lens_ref.3, ...), custom_call_target="tpu_custom_call" | custom-call | tf_op jit(solution)/shard_map/backward/pallas_call | solution.py:1607
  178.5 0.0 copy-start
  178.5 0.0 copy-start.3
  178.5 0.0 copy-start.4
  178.5 0.0 copy-start.2
  178.5 1.4 fusion
  179.9 0.0 copy-start.5
  179.9 0.0 copy-start.1
  179.9 2.9 %bitcast_convert_fusion = f32[1,4,256,512]{3,2,1,0:T(8,128)} fusion(bf16[4,256,512]{2,1,0:T(8,128)(2,1)} %get-tuple-element.58), kind=kLoop, calls=%fused_computation | loop fusion | flops 524288 | bytes 3145728 | tf_op jit(solution)/shard_map/broadcast_in_dim | solution.py:1757
  182.8 0.0 copy-done
  182.8 1.0 copy.33
  183.8 0.0 copy-done.3
  183.8 0.7 copy.34
  184.5 0.0 copy-done.4
  184.5 0.6 copy.35
  185.1 0.0 copy-done.2
  185.1 0.7 copy.36
  185.8 0.0 copy-done.5
  185.8 0.5 copy.37
  186.3 0.0 copy-done.1
  186.3 0.7 copy.38
Async XLA Ops:
  178.5 4.4 %copy-start = (bf16[4,256,512]{2,1,0:T(8,128)(2,1)S(1)}, bf16[4,256,512]{2,1,0:T(8,128)(2,1)}, u32[]{:S(2)}) copy-start(bf16[4,256,512]{2,1,0:T(8,128)(2,1)} %get-tuple-element.57) | copy-start | bytes 3145732
  178.5 5.3 %copy-start.3 = (f32[3,128,128]{2,1,0:T(8,128)S(1)}, f32[3,128,128]{2,1,0:T(8,128)}, u32[]{:S(2)}) copy-start(f32[3,128,128]{2,1,0:T(8,128)} %get-tuple-element.60) | copy-start | bytes 589828
  178.5 6.0 %copy-start.4 = (f32[128,128]{1,0:T(8,128)S(1)}, f32[128,128]{1,0:T(8,128)}, u32[]{:S(2)}) copy-start(f32[128,128]{1,0:T(8,128)} %get-tuple-element.61) | copy-start | bytes 196612
  178.5 6.6 %copy-start.2 = (f32[128,512]{1,0:T(8,128)S(1)}, f32[128,512]{1,0:T(8,128)}, u32[]{:S(2)}) copy-start(f32[128,512]{1,0:T(8,128)} %get-tuple-element.62) | copy-start | bytes 786436
  179.9 5.9 %copy-start.5 = (f32[1,128]{1,0:T(1,128)S(1)}, f32[1,128]{1,0:T(1,128)}, u32[]{:S(2)}) copy-start(f32[1,128]{1,0:T(1,128)} %get-tuple-element.63) | copy-start | bytes 1540
  179.9 6.4 %copy-start.1 = (f32[512,128]{1,0:T(8,128)S(1)}, f32[512,128]{1,0:T(8,128)}, u32[]{:S(2)}) copy-start(f32[512,128]{1,0:T(8,128)} %get-tuple-element.64) | copy-start | bytes 786436

commit v6 on v5

--- a/solution.py
+++ b/solution.py
@@ -912,10 +912,12 @@
     lax.fori_loop(0, OWN // 128, norm_rows, 0)
 
 
-def greet(partners):
+def greet(partners, meanwhile=None):
     barrier = pltpu.get_barrier_semaphore()
     for partner in partners:
         pl.semaphore_signal(barrier, inc=1, device_id=partner, device_id_type=MESH)
+    if meanwhile is not None:
+        meanwhile()
     pl.semaphore_wait(barrier, len(partners))
 
 
@@ -1040,7 +1042,7 @@
     vec_own[...] = jnp.zeros_like(vec_own)
     for row, vector in enumerate(vectors):
         vec_own[row : row + 1, :] = vector[...]
-    greet(all_partners())
+    greet(all_partners(), partial(fill_masks, lens_ref, bias_ref, False))
 
     steps = (1, 2, 3)
 
@@ -1240,7 +1242,6 @@
         z_start(far, VEC)
     own_copy(VEC).start()
     rows_each(0, "start")
-    fill_masks(lens_ref, bias_ref, False)
     run("masks")
     own_copy(VEC).wait()
     for step in steps:
@@ -1372,7 +1373,7 @@
     dy_copy.start()
     for group in (chunk_set, norm_set, attend_set, project_set):
         start(load(1, *group))
-    greet(all_partners() + [(1 - core, rep, lax.bitwise_xor(part, step)) for step in steps])
+    greet(all_partners() + [(1 - core, rep, lax.bitwise_xor(part, step)) for step in steps], partial(fill_masks, lens_ref, bias_ref, True))
 
     owner = jnp.where((part == 0) | (part == 3), 0, 1)
 
@@ -1484,7 +1485,6 @@
     def kv_copy(layer, pair):
         return remote(kv_out.at[:, pair], kv_got.at[layer, :, pair], kv_send.at[layer, pair], kv_recv.at[layer, pair], sibling())
 
-    fill_masks(lens_ref, bias_ref, True)
     for layer in (1, 0):
         signed = layer == 0
         x_ref, normed_one_t, queries, kv, attended, attended_t, logs, hidden, normed_two_t, act, slope = held
@@ -1528,9 +1528,7 @@
             at(turn, 2, part_start, layer, FEED, 0)
             at(turn, 3, part_start, layer, FEED, 1)
             if layer == 0:
-                at(turn, 3, finish, 1, FEED)
-                at(turn, 3, finish, 1, ATTEND)
-                at(turn, 3, hand_over, 1)
+                at(turn, 2, finish, 1, FEED)
 
         def project_turn(turn):
             pair = turn_part(turn + 1)
@@ -1553,6 +1551,9 @@
         part_start(layer, FEED, 2)
         project_turn(PAIRS - 1)
         part_start(layer, FEED, 3)
+        if layer == 0:
+            finish(1, ATTEND)
+            hand_over(1)
         project_back_norm(x_ref, grad_hidden, vec, dy_ref, grad_low.at[layer], vec_grad.at[layer], total)
         if layer == 1:
             start(load(0, (0, 1), (QKV, VEC)))

time: 187 us -> 187 us (level)
  no operation moved by 1% of the time
where the time goes in v6:
time: 187 us
  Pallas kernels  178 us (95%)
  local copies, waits for them, and re-layouts  5.65 us (3%)
  other arithmetic  2.88 us (2%)
    pallas_call x2, Pallas kernels, kernel_call(): pl.pallas_call(body, out_shape=[jax.ShapeDtypeStruct(shape, kind) for sha...  178 us
    unnamed x18, local copies, waits for them, and re-layouts  4.22 us

profile of v6, /device:TPU:0, one launch (start us, length us, event | category | flops | bytes accessed | tf_op | source)
XLA Modules:
  0.0 187.1 jit_solution(2422541132867277120)
XLA Ops:
  0.6 84.5 %forward.1 = (bf16[512,512]{1,0:T(8,128)(2,1)}, bf16[512,512]{1,0:T(8,128)(2,1)}, bf16[2,512,512]{2,1,0:T(8,128)(2,1)}, bf16[2,512,512]{2,1,0:T(8,128)(2,1)}, bf...) custom-call(s32[4,8]{1,0:T(4,128)} %lens_ref.3, ...), custom_call_target="tpu_custom_call" | custom-call | tf_op jit(solution)/shard_map/forward/pallas_call | solution.py:1608
  85.2 93.3 %backward.1 = (f32[512,128]{1,0:T(8,128)}, f32[128,512]{1,0:T(8,128)}, f32[128,128]{1,0:T(8,128)}, f32[3,128,128]{2,1,0:T(8,128)}, f32[8,128]{1,0:T(8,128)}, /*i...) custom-call(s32[4,8]{1,0:T(4,128)} %lens_ref.3, ...), custom_call_target="tpu_custom_call" | custom-call | tf_op jit(solution)/shard_map/backward/pallas_call | solution.py:1608
  178.5 0.0 copy-start
  178.5 0.0 copy-start.3
  178.6 0.0 copy-start.4
  178.6 0.0 copy-start.2
  178.6 1.4 fusion
  180.0 0.0 copy-start.5
  180.0 0.0 copy-start.1
  180.0 2.9 %bitcast_convert_fusion = f32[1,4,256,512]{3,2,1,0:T(8,128)} fusion(bf16[4,256,512]{2,1,0:T(8,128)(2,1)} %get-tuple-element.58), kind=kLoop, calls=%fused_computation | loop fusion | flops 524288 | bytes 3145728 | tf_op jit(solution)/shard_map/broadcast_in_dim | solution.py:1758
  182.9 0.0 copy-done
  182.9 1.0 copy.33
  183.9 0.0 copy-done.3
  183.9 0.7 copy.34
  184.5 0.0 copy-done.4
  184.5 0.6 copy.35
  185.2 0.0 copy-done.2
  185.2 0.7 copy.36
  185.9 0.0 copy-done.5
  185.9 0.5 copy.37
  186.4 0.0 copy-done.1
  186.4 0.7 copy.38
Async XLA Ops:
  178.5 4.4 %copy-start = (bf16[4,256,512]{2,1,0:T(8,128)(2,1)S(1)}, bf16[4,256,512]{2,1,0:T(8,128)(2,1)}, u32[]{:S(2)}) copy-start(bf16[4,256,512]{2,1,0:T(8,128)(2,1)} %get-tuple-element.57) | copy-start | bytes 3145732
  178.5 5.3 %copy-start.3 = (f32[3,128,128]{2,1,0:T(8,128)S(1)}, f32[3,128,128]{2,1,0:T(8,128)}, u32[]{:S(2)}) copy-start(f32[3,128,128]{2,1,0:T(8,128)} %get-tuple-element.60) | copy-start | bytes 589828
  178.6 6.0 %copy-start.4 = (f32[128,128]{1,0:T(8,128)S(1)}, f32[128,128]{1,0:T(8,128)}, u32[]{:S(2)}) copy-start(f32[128,128]{1,0:T(8,128)} %get-tuple-element.61) | copy-start | bytes 196612
  178.6 6.6 %copy-start.2 = (f32[128,512]{1,0:T(8,128)S(1)}, f32[128,512]{1,0:T(8,128)}, u32[]{:S(2)}) copy-start(f32[128,512]{1,0:T(8,128)} %get-tuple-element.62) | copy-start | bytes 786436
  180.0 5.9 %copy-start.5 = (f32[1,128]{1,0:T(1,128)S(1)}, f32[1,128]{1,0:T(1,128)}, u32[]{:S(2)}) copy-start(f32[1,128]{1,0:T(1,128)} %get-tuple-element.63) | copy-start | bytes 1540
  180.0 6.4 %copy-start.1 = (f32[512,128]{1,0:T(8,128)S(1)}, f32[512,128]{1,0:T(8,128)}, u32[]{:S(2)}) copy-start(f32[512,128]{1,0:T(8,128)} %get-tuple-element.64) | copy-start | bytes 786436
